TPU v7x, 32 devices: a whole 2x2x4 slice. The times are simulated.
32 devices in a mesh: rows: 8 (over y, x, core), kv: 4 (over z).
Axes of the slice: x: 2, y: 2, z: 4, core: 2. Of those that a mesh axis runs over, the one named last changes fastest.
Arguments:
- tokens: bfloat16 [8, 1024, 768], P('rows', 'kv'), may hold values from -6 to 6
- lengths: int32 [8, 4], P('rows'), may hold values from 0 to 1024, as said below
- w_qkv: bfloat16 [2, 768, 2304], P(None, ('rows', 'kv')), may hold values from -0.21875 to 0.21875
- w_out: bfloat16 [2, 768, 768], P(None, ('rows', 'kv')), may hold values from -1.75 to 1.75
- w_up: bfloat16 [2, 768, 3072], P(None, ('rows', 'kv')), may hold values from -0.21875 to 0.21875
- w_down: bfloat16 [2, 3072, 768], P(None, ('rows', 'kv')), may hold values from -0.109375 to 0.109375
- gains: bfloat16 [2, 2, 768], P(None, None, ('rows', 'kv')), may hold values from 0.5 to 1.5
- biases: bfloat16 [2, 2, 768], P(None, None, ('rows', 'kv')), may hold values from -3 to 3
- cotangent: bfloat16 [8, 1024, 768], P('rows', 'kv'), may hold values from -6 to 6
Outputs:
- result: bfloat16 [8, 1024, 768], P('rows', 'kv')
- input_grad: float32 [8, 1024, 768], P('rows', 'kv')
- grad_qkv: float32 [2, 768, 2304], P(None, ('rows', 'kv'))
- grad_out: float32 [2, 768, 768], P(None, ('rows', 'kv'))
- grad_up: float32 [2, 768, 3072], P(None, ('rows', 'kv'))
- grad_down: float32 [2, 3072, 768], P(None, ('rows', 'kv'))
- grad_gains: float32 [2, 2, 768], P(None, None, ('rows', 'kv'))
- grad_biases: float32 [2, 768], P(None, ('rows', 'kv'))
- grad_mid_biases: float32 [2, 768], P(None, ('rows', 'kv'))
Inputs may be any that keep to these rules, and one draw needn't show every extreme that they name: Zero entries are unused; every other length is 64 or more; a row's lengths sum to at most 1024 and the rest of the row is padding. In every row the document of the second length entry starts in the row's first eighth and ends in its last eighth; some row is one document of 1024.
All inputs are finite; a program needn't handle non-finite values.
Results may differ from a plain program's by a relative error of at most 0.019.
Values may be sent and summed in bfloat16 or wider, within the bound.
A program may use at most 256 MiB of HBM per device.

v0:
```python
import math

import jax
import jax.numpy as jnp
from jax import lax
from jax.sharding import PartitionSpec as P

HEADS = 12
HEAD = 64
LAYERS = 2


EPSILON = 1e-05


def norm_rows(stream, gain, bias):
    center = stream - jnp.mean(stream, -1, keepdims=True)
    spread = jnp.mean(center * center, -1, keepdims=True)
    return center * lax.rsqrt(spread + EPSILON) * gain + bias


def normalise(scores, allowed, query_live, signed):
    if signed:
        magnitude = jnp.sqrt(scores * scores + 1.0)
        ceiling = jnp.max(jnp.where(allowed > 0, magnitude, 0.0), -1, keepdims=True)
        shifted = jnp.where(allowed > 0, magnitude - ceiling, -60.0)
    else:
        ceiling = jnp.max(jnp.where(allowed > 0, scores, -10000.0), -1, keepdims=True)
        shifted = jnp.where(allowed > 0, scores - ceiling, -60.0)
    raised = jnp.exp(shifted) * allowed
    normaliser = jnp.sum(raised, -1, keepdims=True) + (1.0 - query_live)[None, :, None]
    unsigned_w = raised / normaliser
    if signed:
        return (jnp.tanh(scores) * unsigned_w, unsigned_w)
    return (unsigned_w, unsigned_w)


def make_mask(query_places, query_docs, query_live, key_places, key_docs, key_live):
    allowed = (
        (query_docs[:, None] == key_docs[None, :]) & (key_places[None, :] <= query_places[:, None])
    ).astype(jnp.float32)
    return allowed * query_live[:, None] * key_live[None, :]


def split_heads(query, keys_vals):
    model_width = query.shape[-1]
    slot_count = keys_vals.shape[0]
    query_heads = query.reshape(-1, HEADS, HEAD)
    key_heads = keys_vals[:, :model_width].reshape(slot_count, HEADS, HEAD)
    value_heads = keys_vals[:, model_width:].reshape(slot_count, HEADS, HEAD)
    return (query_heads, key_heads, value_heads)


def score_grads(scores, unsigned_w, weight_grad, inner_sum, signed):
    if signed:
        tanh_s = jnp.tanh(scores)
        magnitude = jnp.sqrt(scores * scores + 1.0)
        return unsigned_w * (
            (tanh_s * weight_grad - inner_sum) * scores / magnitude
            + weight_grad * (1.0 - tanh_s * tanh_s)
        )
    return unsigned_w * (weight_grad - inner_sum)


def attend_row(query, keys_vals, allowed, query_live, signed, scaling):
    query_heads, key_heads, value_heads = split_heads(query, keys_vals)
    scores = (
        jnp.einsum("qhd,khd->hqk", query_heads, key_heads, preferred_element_type=jnp.float32)
        * scaling
    )
    weights, unsigned_w = normalise(scores, allowed, query_live, signed)
    outcome = jnp.einsum(
        "hqk,khd->qhd",
        weights.astype(jnp.bfloat16),
        value_heads,
        preferred_element_type=jnp.float32,
    )
    return outcome.reshape(query.shape[0], query.shape[1]).astype(jnp.bfloat16)


def attend_back(query, keys_vals, grad_att, allowed, query_live, signed, scaling):
    query_heads, key_heads, value_heads = split_heads(query, keys_vals)
    slot_count = keys_vals.shape[0]
    model_width = query.shape[-1]
    scores = (
        jnp.einsum("qhd,khd->hqk", query_heads, key_heads, preferred_element_type=jnp.float32)
        * scaling
    )
    weights, unsigned_w = normalise(scores, allowed, query_live, signed)
    weights_low = weights.astype(jnp.bfloat16)
    grad_heads = grad_att.reshape(-1, HEADS, HEAD)
    weight_grad = jnp.einsum(
        "qhd,khd->hqk", grad_heads, value_heads, preferred_element_type=jnp.float32
    )
    inner_sum = jnp.sum(weight_grad * weights, -1, keepdims=True)
    score_low = score_grads(scores, unsigned_w, weight_grad, inner_sum, signed).astype(jnp.bfloat16)
    query_grad = (
        jnp.einsum("hqk,khd->qhd", score_low, key_heads, preferred_element_type=jnp.float32)
        * scaling
    )
    key_grad = (
        jnp.einsum("hqk,qhd->khd", score_low, query_heads, preferred_element_type=jnp.float32)
        * scaling
    )
    value_grad = jnp.einsum(
        "hqk,qhd->khd", weights_low, grad_heads, preferred_element_type=jnp.float32
    )
    kv_grad = jnp.concatenate(
        [key_grad.reshape(slot_count, model_width), value_grad.reshape(slot_count, model_width)], -1
    )
    return (query_grad.reshape(query.shape[0], model_width), kv_grad)


def reduce_grads(pairs, g_gain, g_bias):
    n_rows = lax.axis_size("rows")
    n_kv = lax.axis_size("kv")
    lefts = []
    rights = []
    for left_side, right_side in pairs:
        tok_count = left_side.shape[0] * left_side.shape[1]
        in_width = left_side.shape[-1]
        lefts.append(left_side.reshape(tok_count, n_rows, n_kv, in_width // (n_rows * n_kv)))
        rights.append(right_side.reshape(tok_count, right_side.shape[-1]))
    moved = (
        lax.all_to_all(lefts[0], "kv", split_axis=2, concat_axis=0, tiled=True),
        lax.all_to_all(lefts[1], "kv", split_axis=2, concat_axis=0, tiled=True),
        lax.all_to_all(lefts[2], "kv", split_axis=2, concat_axis=0, tiled=True),
        lax.all_to_all(lefts[3], "kv", split_axis=2, concat_axis=0, tiled=True),
    )
    whole = (
        lax.all_gather(rights[0], "kv", axis=0, tiled=True),
        lax.all_gather(rights[1], "kv", axis=0, tiled=True),
        lax.all_gather(rights[2], "kv", axis=0, tiled=True),
        lax.all_gather(rights[3], "kv", axis=0, tiled=True),
    )
    partial_sums = []
    for number in range(4):
        left_block = moved[number].reshape(moved[number].shape[0], -1)
        product = jnp.einsum(
            "ti,to->io", left_block, whole[number], preferred_element_type=jnp.float32
        )
        partial_sums.append(product.reshape(n_rows, -1, product.shape[-1]))
    reduced = (
        lax.psum_scatter(
            partial_sums[0].astype(jnp.bfloat16), "rows", scatter_dimension=0, tiled=True
        ).astype(jnp.float32),
        lax.psum_scatter(
            partial_sums[1].astype(jnp.bfloat16), "rows", scatter_dimension=0, tiled=True
        ).astype(jnp.float32),
        lax.psum_scatter(
            partial_sums[2].astype(jnp.bfloat16), "rows", scatter_dimension=0, tiled=True
        ).astype(jnp.float32),
        lax.psum_scatter(
            partial_sums[3].astype(jnp.bfloat16), "rows", scatter_dimension=0, tiled=True
        ).astype(jnp.float32),
    )
    norm_parts = (
        lax.psum_scatter(g_gain, ("rows", "kv"), scatter_dimension=1, tiled=True),
        lax.psum_scatter(g_bias, ("rows", "kv"), scatter_dimension=1, tiled=True),
    )
    results = tuple((piece.reshape(piece.shape[1], piece.shape[2]) for piece in reduced))
    return results + (norm_parts[0], norm_parts[1])


def local(tokens, lengths, w_qkv, w_out, w_up, w_down, gains, biases, cotangent):
    rows_here, slot_dev, model_width = tokens.shape
    slot_count = slot_dev * lax.axis_size("kv")
    first_slot = lax.axis_index("kv") * slot_dev
    scaling = 1.0 / math.sqrt(HEAD)
    doc_ends = jnp.cumsum(lengths, -1)
    places = jnp.arange(slot_count, dtype=jnp.int32)
    docs_all = jnp.sum((doc_ends[:, None, :] <= places[None, :, None]).astype(jnp.int32), -1)
    live_all = (places[None, :] < doc_ends[:, -1:]).astype(jnp.float32)
    docs_here = lax.dynamic_slice_in_dim(docs_all, first_slot, slot_dev, 1)
    live_here = lax.dynamic_slice_in_dim(live_all, first_slot, slot_dev, 1)
    local_places = first_slot + jnp.arange(slot_dev, dtype=jnp.int32)
    masks = make_mask(local_places, docs_here[0], live_here[0], places, docs_all[0], live_all[0])
    stream = tokens.astype(jnp.float32)
    stored = []
    for number in range(LAYERS):
        signed = number == 0
        pieces = (
            lax.all_gather(w_qkv[number], ("rows", "kv"), axis=0, tiled=True),
            lax.all_gather(w_out[number], ("rows", "kv"), axis=0, tiled=True),
            lax.all_gather(w_up[number], ("rows", "kv"), axis=0, tiled=True),
            lax.all_gather(w_down[number], ("rows", "kv"), axis=0, tiled=True),
            lax.all_gather(gains[number], ("rows", "kv"), axis=1, tiled=True),
            lax.all_gather(biases[number], ("rows", "kv"), axis=1, tiled=True),
        )
        full_qkv, full_out, full_up, full_down, gain_pair, bias_pair = pieces
        gain_pair = gain_pair.astype(jnp.float32)
        bias_pair = bias_pair.astype(jnp.float32)
        normed_in = norm_rows(stream, gain_pair[0], bias_pair[0]).astype(jnp.bfloat16)
        projected = jnp.dot(normed_in, full_qkv, preferred_element_type=jnp.float32).astype(
            jnp.bfloat16
        )
        kv_all = lax.all_gather(projected[:, :, model_width:], "kv", axis=1, tiled=True)
        attended = jnp.stack(
            [
                attend_row(
                    projected[0, :, :model_width], kv_all[0], masks, live_here[0], signed, scaling
                )
            ]
        )
        shared = kv_all
        middle = stream + jnp.dot(attended, full_out, preferred_element_type=jnp.float32)
        normed_mid = norm_rows(middle, gain_pair[1], bias_pair[1]).astype(jnp.bfloat16)
        pre_act = jnp.dot(normed_mid, full_up, preferred_element_type=jnp.float32)
        activated = jax.nn.gelu(pre_act).astype(jnp.bfloat16)
        stored.append(
            (
                stream,
                normed_in,
                projected,
                shared,
                attended,
                middle,
                normed_mid,
                pre_act,
                activated,
                pieces,
            )
        )
        stream = middle + jnp.dot(activated, full_down, preferred_element_type=jnp.float32)
    result = (stream * live_here[..., None]).astype(jnp.bfloat16)
    residual_grad = cotangent.astype(jnp.float32) * live_here[..., None]
    collected = [None] * LAYERS
    for number in reversed(range(LAYERS)):
        signed = number == 0
        (
            stream_in,
            normed_in,
            projected,
            shared,
            attended,
            middle,
            normed_mid,
            pre_act,
            activated,
            kept,
        ) = stored[number]
        pieces = (
            lax.all_gather(w_qkv[number], ("rows", "kv"), axis=0, tiled=True),
            lax.all_gather(w_out[number], ("rows", "kv"), axis=0, tiled=True),
            lax.all_gather(w_up[number], ("rows", "kv"), axis=0, tiled=True),
            lax.all_gather(w_down[number], ("rows", "kv"), axis=0, tiled=True),
            lax.all_gather(gains[number], ("rows", "kv"), axis=1, tiled=True),
            lax.all_gather(biases[number], ("rows", "kv"), axis=1, tiled=True),
        )
        full_qkv, full_out, full_up, full_down, gain_pair, bias_pair = pieces
        gain_pair = gain_pair.astype(jnp.float32)
        bias_pair = bias_pair.astype(jnp.float32)
        down_in = residual_grad.astype(jnp.bfloat16)
        act_grad = jnp.einsum("rtd,fd->rtf", down_in, full_down, preferred_element_type=jnp.float32)
        unused, gelu_pull = jax.vjp(jax.nn.gelu, pre_act)
        pre_grad = gelu_pull(act_grad)[0].astype(jnp.bfloat16)
        mid_normed_grad = jnp.einsum(
            "rtf,df->rtd", pre_grad, full_up, preferred_element_type=jnp.float32
        )
        unused, norm_pull = jax.vjp(norm_rows, middle, gain_pair[1], bias_pair[1])
        middle_part, gain_late, bias_late = norm_pull(mid_normed_grad)
        middle_grad = residual_grad + middle_part
        branch_grad = middle_grad.astype(jnp.bfloat16)
        att_grad = jnp.einsum(
            "rte,de->rtd", branch_grad, full_out, preferred_element_type=jnp.float32
        ).astype(jnp.bfloat16)
        kv_all = shared
        query_grad, kv_grad = attend_back(
            projected[0, :, :model_width],
            kv_all[0],
            att_grad[0],
            masks,
            live_here[0],
            signed,
            scaling,
        )
        query_grads = [query_grad]
        kv_grads = [kv_grad]
        kv_here = lax.psum_scatter(
            jnp.stack(kv_grads).astype(jnp.bfloat16), "kv", scatter_dimension=1, tiled=True
        ).astype(jnp.float32)
        qkv_grad = jnp.concatenate([jnp.stack(query_grads), kv_here], -1).astype(jnp.bfloat16)
        in_normed_grad = jnp.einsum(
            "rte,de->rtd", qkv_grad, full_qkv, preferred_element_type=jnp.float32
        )
        unused, first_pull = jax.vjp(norm_rows, stream_in, gain_pair[0], bias_pair[0])
        stream_part, gain_early, bias_early = first_pull(in_normed_grad)
        residual_grad = middle_grad + stream_part
        g_gain = jnp.stack([gain_early, gain_late])
        g_bias = jnp.stack([bias_early, bias_late])
        pairs = [
            (normed_in, qkv_grad),
            (attended, branch_grad),
            (normed_mid, pre_grad),
            (activated, down_in),
        ]
        collected[number] = reduce_grads(pairs, g_gain, g_bias)
    grad_qkv = jnp.stack([collected[number][0] for number in range(LAYERS)])
    grad_out = jnp.stack([collected[number][1] for number in range(LAYERS)])
    grad_up = jnp.stack([collected[number][2] for number in range(LAYERS)])
    grad_down = jnp.stack([collected[number][3] for number in range(LAYERS)])
    grad_gains = jnp.stack([collected[number][4] for number in range(LAYERS)])
    grad_biases = jnp.stack([collected[number][5][0] for number in range(LAYERS)])
    grad_mid_biases = jnp.stack([collected[number][5][1] for number in range(LAYERS)])
    return (
        result,
        residual_grad,
        grad_qkv,
        grad_out,
        grad_up,
        grad_down,
        grad_gains,
        grad_biases,
        grad_mid_biases,
    )


def solution(mesh):
    in_specs = (
        P("rows", "kv", None),
        P("rows", None),
        P(None, ("rows", "kv"), None),
        P(None, ("rows", "kv"), None),
        P(None, ("rows", "kv"), None),
        P(None, ("rows", "kv"), None),
        P(None, None, ("rows", "kv")),
        P(None, None, ("rows", "kv")),
        P("rows", "kv", None),
    )
    out_specs = (
        P("rows", "kv", None),
        P("rows", "kv", None),
        P(None, ("rows", "kv"), None),
        P(None, ("rows", "kv"), None),
        P(None, ("rows", "kv"), None),
        P(None, ("rows", "kv"), None),
        P(None, None, ("rows", "kv")),
        P(None, ("rows", "kv")),
        P(None, ("rows", "kv")),
    )
    return jax.shard_map(local, mesh=mesh, in_specs=in_specs, out_specs=out_specs, check_vma=False)
```

profile of v0, /device:TPU:0, one launch (start us, length us, event | category | flops | bytes accessed | tf_op | source)
XLA Modules:
  0.0 1875.6 jit_solution(13583126501651541035)
XLA Ops:
  10.6 74.1 %all-gather = bf16[1,2,768]{1,0,2:T(2,128)(2,1)S(1)} all-gather(bf16[1,2,24]{1,0,2:T(2,128)(2,1)S(1)} %copy.196), channel_id=2, replica_groups=mesh['rows'=8,'kv'=4] {'rows','kv'}, dimensions={2}, use_global_device_ids=true | all-gather | bytes 3168 | tf_op jit(solution)/shard_map/all_gather | solution.py:187
  85.1 66.6 %all-gather.1 = bf16[1,2,768]{1,0,2:T(2,128)(2,1)S(1)} all-gather(bf16[1,2,24]{1,0,2:T(2,128)(2,1)S(1)} %copy.197), channel_id=3, replica_groups=mesh['rows'=8,'kv'=4] {'rows','kv'}, dimensions={2}, use_global_device_ids=true | all-gather | bytes 3168 | tf_op jit(solution)/shard_map/all_gather | solution.py:188
  152.5 4.6 slice_reduce_fusion.5
  157.0 4.6 slice_reduce_fusion.4
  174.7 73.8 %all-gather.6 = bf16[1,2,768]{1,0,2:T(2,128)(2,1)S(1)} all-gather(bf16[1,2,24]{1,0,2:T(2,128)(2,1)S(1)} %copy.198), channel_id=8, replica_groups=mesh['rows'=8,'kv'=4] {'rows','kv'}, dimensions={2}, use_global_device_ids=true | all-gather | bytes 3168 | tf_op jit(solution)/shard_map/all_gather | solution.py:187
  248.9 4.6 slice_reduce_fusion.1
  253.5 67.9 %all-gather.7 = bf16[1,2,768]{1,0,2:T(2,128)(2,1)S(1)} all-gather(bf16[1,2,24]{1,0,2:T(2,128)(2,1)S(1)} %copy.199), channel_id=9, replica_groups=mesh['rows'=8,'kv'=4] {'rows','kv'}, dimensions={2}, use_global_device_ids=true | all-gather | bytes 3168 | tf_op jit(solution)/shard_map/all_gather | solution.py:188
  321.8 4.6 slice_reduce_fusion
  333.8 22.4 %fusion.211 = (f32[12,256]{1,0:T(8,128)S(1)}, f32[12,256,1024]{2,1,0:T(8,128)}) fusion(f32[256,1024]{1,0:T(8,128)S(1)} %copy-done.42, pred[256,1024]{1,0:T(8,128)(4,1)} %broadcast_compare_fusion, bf16[256,12,64]{0,2,1:T(8,128)(2,1)S(1)} %bitcast.430, bf16[1024,12,64]{0,2,1:T(8,128)(2,1)} %bitcast.423), kind=kOutput, calls=%fused_computation.267 | convolution fusion | flops 839910400 | bytes 15872000 | tf_op jit(solution)/shard_map/sub | solution.py:26
  356.2 9.5 tanh_multiply_fusion
  365.7 4.6 copy-done.1
  375.6 6.1 multiply_convert_fusion.5
  381.6 39.3 %all-gather.53.cloned.1.call-done = bf16[1,3072,768]{2,1,0:T(8,128)(2,1)} async-done(((bf16[1,96,768]{2,1,0:T(8,128)(2,1)}), bf16[1,3072,768]{2,1,0:T(8,128)(2,1)}) %all-gather.53.cloned.1.call-update) | async-done | bytes 4718608 | tf_op jit(solution)/shard_map/all_gather | solution.py:186
  425.9 56.7 %all-gather.55.cloned.1.call-done = bf16[1,768,2304]{2,1,0:T(8,128)(2,1)} async-done(((bf16[1,24,2304]{2,1,0:T(8,128)(2,1)}), bf16[1,768,2304]{2,1,0:T(8,128)(2,1)}) %all-gather.55.cloned.1.call-update) | async-done | bytes 3538960 | tf_op jit(solution)/shard_map/all_gather | solution.py:183
  490.6 58.5 %all-gather.37.cloned.1.call-done = bf16[1,1024,1536]{2,1,0:T(8,128)(2,1)} async-done(((bf16[1,256,1536]{2,1,0:T(8,128)(2,1)}), bf16[1,1024,1536]{2,1,0:T(8,128)(2,1)}) %all-gather.37.cloned.1.call-update) | async-done | bytes 3145744 | tf_op jit(solution)/shard_map/all_gather | solution.py:197
  556.7 12.5 fusion.214
  569.9 7.4 fusion.137
  577.3 27.3 %all-gather.57.cloned.1.call-done = bf16[1,768,768]{2,1,0:T(8,128)(2,1)} async-done(((bf16[1,24,768]{2,1,0:T(8,128)(2,1)}), bf16[1,768,768]{2,1,0:T(8,128)(2,1)}) %all-gather.57.cloned.1.call-update) | async-done | bytes 1179664 | tf_op jit(solution)/shard_map/all_gather | solution.py:184
  607.2 63.4 %all-gather.59.cloned.1.call-done = bf16[1,768,3072]{2,1,0:T(8,128)(2,1)} async-done(((bf16[1,24,3072]{2,1,0:T(8,128)(2,1)}), bf16[1,768,3072]{2,1,0:T(8,128)(2,1)}) %all-gather.59.cloned.1.call-update) | async-done | bytes 4718608 | tf_op jit(solution)/shard_map/all_gather | solution.py:185
  670.6 6.5 multiply_convert_fusion.4
  677.1 58.5 %all-gather.61.cloned.1.call-done = bf16[1,3072,768]{2,1,0:T(8,128)(2,1)} async-done(((bf16[1,96,768]{2,1,0:T(8,128)(2,1)}), bf16[1,3072,768]{2,1,0:T(8,128)(2,1)}) %all-gather.61.cloned.1.call-update) | async-done | bytes 4718608 | tf_op jit(solution)/shard_map/all_gather | solution.py:186
  735.6 6.1 fusion.78
  743.0 4.5 fusion.167
  751.8 7.4 fusion.96
  759.2 8.5 multiply_reduce_fusion.1
  770.2 9.5 multiply_convert_fusion.1
  783.9 3.8 pad_maximum_fusion
  787.8 5.3 fusion.143
  794.2 52.9 %reduce-scatter.15.cloned.1.call-done = bf16[1,256,1536]{2,1,0:T(8,128)(2,1)} async-done(((bf16[1,1024,1536]{2,1,0:T(8,128)(2,1)}), bf16[1,256,1536]{2,1,0:T(8,128)(2,1)}) %reduce-scatter.15.cloned.1.call-update) | async-done | bytes 786448 | tf_op jit(solution)/shard_map/reduce_scatter | solution.py:279
  847.1 4.3 fusion.168
  852.8 7.8 fusion.71
  860.6 5.0 fusion.169
  870.8 27.4 %multiply_convert_fusion = bf16[12,256,1024]{2,1,0:T(8,128)(2,1)} fusion(f32[12,256,1024]{2,1,0:T(8,128)} %get-tuple-element.60, f32[12,256,1024]{2,1,0:T(8,128)} %copy-done.1, f32[12,256,1024]{2,1,0:T(8,128)} %get-tuple-element.58, f32[12,256]{1,0:T(8,128)S(1)} %copy-done.71, bf16[256,12,64]{0,2,1:T(8,128)(2,1)S(1)} %bitcast.464, ...), kind=kOutput, calls=%fused_computation.3 | convolution fusion | flops 852496384 | bytes 46018560 | tf_op jit(solution)/shard_map/sub | solution.py:59
  898.2 4.0 multiply_convert_fusion.2
  903.8 5.8 fusion.93
  921.4 10.8 all-to-all-done.2
  938.7 19.3 %all-to-all-done.3 = bf16[256,8,4,24]{0,3,1,2:T(8,128)(2,1)S(1)} async-done(((bf16[256,8,4,24]{0,3,1,2:T(8,128)(2,1)}), bf16[256,8,4,24]{0,3,1,2:T(8,128)(2,1)S(1)}, u32[]{:S(2)}, u32[]{:S(2)}) %all-to-all-start.3) | async-done | bytes 393248 | tf_op jit(solution)/shard_map/all_to_all | solution.py:126
  958.0 3.9 all-to-all-start.7
  967.5 57.6 %all-to-all-done.7 = bf16[256,8,4,96]{0,3,1,2:T(8,128)(2,1)S(1)} async-done(((bf16[256,8,4,96]{0,3,1,2:T(8,128)(2,1)}), bf16[256,8,4,96]{0,3,1,2:T(8,128)(2,1)S(1)}, u32[]{:S(2)}, u32[]{:S(2)}) %all-to-all-start.7) | async-done | bytes 1572896 | tf_op jit(solution)/shard_map/all_to_all | solution.py:128
  1040.1 4.3 fusion.110
  1044.5 63.3 %all-to-all-done.6 = bf16[256,8,4,96]{0,3,1,2:T(8,128)(2,1)S(1)} async-done(((bf16[256,8,4,96]{0,3,1,2:T(8,128)(2,1)}), bf16[256,8,4,96]{0,3,1,2:T(8,128)(2,1)S(1)}, u32[]{:S(2)}, u32[]{:S(2)}) %all-to-all-start.6) | async-done | bytes 1572896 | tf_op jit(solution)/shard_map/all_to_all | solution.py:128
  1109.4 4.0 fusion.107
  1115.2 4.8 fusion.144
  1128.0 20.5 %all-to-all-done.5 = bf16[256,8,4,24]{0,3,1,2:T(8,128)(2,1)S(1)} async-done(((bf16[256,8,4,24]{0,3,1,2:T(8,128)(2,1)}), bf16[256,8,4,24]{0,3,1,2:T(8,128)(2,1)S(1)}, u32[]{:S(2)}, u32[]{:S(2)}) %all-to-all-start.5) | async-done | bytes 393248 | tf_op jit(solution)/shard_map/all_to_all | solution.py:127
  1152.4 93.0 %all-gather.45.cloned.1.call-done = bf16[1024,3072]{1,0:T(8,128)(2,1)} async-done(((bf16[256,3072]{1,0:T(8,128)(2,1)}), bf16[1024,3072]{1,0:T(8,128)(2,1)}) %all-gather.45.cloned.1.call-update) | async-done | bytes 6291472 | tf_op jit(solution)/shard_map/all_gather | solution.py:133
  1245.5 5.2 fusion.54
  1256.1 23.8 %all-to-all-done.4 = bf16[256,8,4,24]{0,3,1,2:T(8,128)(2,1)S(1)} async-done(((bf16[256,8,4,24]{0,3,1,2:T(8,128)(2,1)}), bf16[256,8,4,24]{0,3,1,2:T(8,128)(2,1)S(1)}, u32[]{:S(2)}, u32[]{:S(2)}) %all-to-all-start.4) | async-done | bytes 393248 | tf_op jit(solution)/shard_map/all_to_all | solution.py:127
  1284.5 19.8 %all-to-all-done.1 = bf16[256,8,4,24]{0,3,1,2:T(8,128)(2,1)S(1)} async-done(((bf16[256,8,4,24]{0,3,1,2:T(8,128)(2,1)}), bf16[256,8,4,24]{0,3,1,2:T(8,128)(2,1)S(1)}, u32[]{:S(2)}, u32[]{:S(2)}) %all-to-all-start.1) | async-done | bytes 393248 | tf_op jit(solution)/shard_map/all_to_all | solution.py:125
  1306.1 71.5 %all-gather.43.cloned.1.call-done = bf16[1024,3072]{1,0:T(8,128)(2,1)} async-done(((bf16[256,3072]{1,0:T(8,128)(2,1)}), bf16[1024,3072]{1,0:T(8,128)(2,1)}) %all-gather.43.cloned.1.call-update) | async-done | bytes 6291472 | tf_op jit(solution)/shard_map/all_gather | solution.py:133
  1377.5 5.2 fusion.51
  1382.9 5.1 fusion.140
  1390.2 23.0 %reduce-scatter.25.cloned.1.call-done = bf16[1,24,768]{2,1,0:T(8,128)(2,1)} async-done(((bf16[8,24,768]{2,1,0:T(8,128)(2,1)}), bf16[1,24,768]{2,1,0:T(8,128)(2,1)}) %reduce-scatter.25.cloned.1.call-update) | async-done | bytes 36880 | tf_op jit(solution)/shard_map/reduce_scatter | solution.py:147
  1413.2 35.8 %reduce-scatter.23.cloned.1.call-done = bf16[1,24,768]{2,1,0:T(8,128)(2,1)} async-done(((bf16[8,24,768]{2,1,0:T(8,128)(2,1)}), bf16[1,24,768]{2,1,0:T(8,128)(2,1)}) %reduce-scatter.23.cloned.1.call-update) | async-done | bytes 36880 | tf_op jit(solution)/shard_map/reduce_scatter | solution.py:147
  1450.5 38.6 %reduce-scatter.33.cloned.1.call-done = bf16[1,96,768]{2,1,0:T(8,128)(2,1)} async-done(((bf16[8,96,768]{2,1,0:T(8,128)(2,1)}), bf16[1,96,768]{2,1,0:T(8,128)(2,1)}) %reduce-scatter.33.cloned.1.call-update) | async-done | bytes 147472 | tf_op jit(solution)/shard_map/reduce_scatter | solution.py:153
  1489.1 40.4 %reduce-scatter.31.cloned.1.call-done = bf16[1,96,768]{2,1,0:T(8,128)(2,1)} async-done(((bf16[8,96,768]{2,1,0:T(8,128)(2,1)}), bf16[1,96,768]{2,1,0:T(8,128)(2,1)}) %reduce-scatter.31.cloned.1.call-update) | async-done | bytes 147472 | tf_op jit(solution)/shard_map/reduce_scatter | solution.py:153
  1535.0 85.5 %all-gather.41.cloned.1.call-done = bf16[1024,2304]{1,0:T(8,128)(2,1)} async-done(((bf16[256,2304]{1,0:T(8,128)(2,1)}), bf16[1024,2304]{1,0:T(8,128)(2,1)}) %all-gather.41.cloned.1.call-update) | async-done | bytes 4718608 | tf_op jit(solution)/shard_map/all_gather | solution.py:131
  1620.5 4.4 fusion.48
  1625.5 44.5 %all-reduce.4 = (f32[2,768]{1,0:T(2,128)S(1)}, f32[2,768]{1,0:T(2,128)S(1)}, f32[2,768]{1,0:T(2,128)S(1)}, f32[2,768]{1,0:T(2,128)S(1)}) all-reduce(f32[2,768]{1,0:T(2,128)S(1)} %pad_maximum_fusion.5, f32[2,768]{1,0:T(2,128)S(1)} %pad_maximum_fusion.4, ...), channel_id=29, replica_groups=mesh['rows'=8,'kv'=4] {'rows','kv'}, use_global_device_ids=true, to_apply=%region_39.40.clone | all-reduce | flops 6144 | bytes 49152
  1670.0 40.7 %all-gather.39.cloned.1.call-done = bf16[1024,2304]{1,0:T(8,128)(2,1)} async-done(((bf16[256,2304]{1,0:T(8,128)(2,1)}), bf16[1024,2304]{1,0:T(8,128)(2,1)}) %all-gather.39.cloned.1.call-update) | async-done | bytes 4718608 | tf_op jit(solution)/shard_map/all_gather | solution.py:131
  1710.8 4.5 fusion.45
  1718.3 31.0 %reduce-scatter.29.cloned.1.call-done = bf16[1,24,3072]{2,1,0:T(8,128)(2,1)} async-done(((bf16[8,24,3072]{2,1,0:T(8,128)(2,1)}), bf16[1,24,3072]{2,1,0:T(8,128)(2,1)}) %reduce-scatter.29.cloned.1.call-update) | async-done | bytes 147472 | tf_op jit(solution)/shard_map/reduce_scatter | solution.py:150
  1749.3 40.2 %reduce-scatter.27.cloned.1.call-done = bf16[1,24,3072]{2,1,0:T(8,128)(2,1)} async-done(((bf16[8,24,3072]{2,1,0:T(8,128)(2,1)}), bf16[1,24,3072]{2,1,0:T(8,128)(2,1)}) %reduce-scatter.27.cloned.1.call-update) | async-done | bytes 147472 | tf_op jit(solution)/shard_map/reduce_scatter | solution.py:150
  1791.4 36.4 %reduce-scatter.21.cloned.1.call-done = bf16[1,24,2304]{2,1,0:T(8,128)(2,1)} async-done(((bf16[8,24,2304]{2,1,0:T(8,128)(2,1)}), bf16[1,24,2304]{2,1,0:T(8,128)(2,1)}) %reduce-scatter.21.cloned.1.call-update) | async-done | bytes 110608 | tf_op jit(solution)/shard_map/reduce_scatter | solution.py:144
  1827.8 38.7 %reduce-scatter.19.cloned.1.call-done = bf16[1,24,2304]{2,1,0:T(8,128)(2,1)} async-done(((bf16[8,24,2304]{2,1,0:T(8,128)(2,1)}), bf16[1,24,2304]{2,1,0:T(8,128)(2,1)}) %reduce-scatter.19.cloned.1.call-update) | async-done | bytes 110608 | tf_op jit(solution)/shard_map/reduce_scatter | solution.py:144
  (410 shorter events, 157.8 us)
Async XLA Ops:
  7.2 144.9 %copy-start.2 = (bf16[1,256,768]{2,1,0:T(8,128)(2,1)S(1)}, bf16[1,256,768]{2,1,0:T(8,128)(2,1)}, u32[]{:S(2)}) copy-start(bf16[1,256,768]{2,1,0:T(8,128)(2,1)} %param.9) | copy-start | bytes 1179652
  7.2 155.3 %all-gather.47.cloned.1.call-start = ((), (), s32[]{:S(2)}) async-start(), calls=%async_computation.34 | async-start | bytes 3649536 | tf_op jit(solution)/shard_map/all_gather | solution.py:183
  8.9 317.6 %all-gather.35.cloned.1.call-start = ((), (), s32[]{:S(2)}) async-start(), calls=%async_computation.18 | async-start | bytes 3932160 | tf_op jit(solution)/shard_map/all_gather | solution.py:197
  157.0 218.3 %copy-start.53 = (f32[768]{0:T(1024)}, f32[768]{0:T(1024)S(1)}, u32[]{:S(2)}) copy-start(f32[768]{0:T(1024)S(1)} %get-tuple-element.21) | copy-start | bytes 9220
  166.8 206.3 %all-gather.49.cloned.1.call-start = ((), (), s32[]{:S(2)}) async-start(), calls=%async_computation.35 | async-start | bytes 1216512 | tf_op jit(solution)/shard_map/all_gather | solution.py:184
  167.5 208.0 %all-gather.51.cloned.1.call-start = ((), (), s32[]{:S(2)}) async-start(), calls=%async_computation.36 | async-start | bytes 4866048 | tf_op jit(solution)/shard_map/all_gather | solution.py:185
  168.3 252.7 %all-gather.53.cloned.1.call-start = ((), (), s32[]{:S(2)}) async-start(), calls=%async_computation.37 | async-start | bytes 4866048 | tf_op jit(solution)/shard_map/all_gather | solution.py:186
  169.2 313.4 %all-gather.55.cloned.1.call-start = ((), (), s32[]{:S(2)}) async-start(), calls=%async_computation.38 | async-start | bytes 3649536 | tf_op jit(solution)/shard_map/all_gather | solution.py:183
  169.7 379.4 %all-gather.37.cloned.1.call-start = ((), (), s32[]{:S(2)}) async-start(), calls=%async_computation.19 | async-start | bytes 3932160 | tf_op jit(solution)/shard_map/all_gather | solution.py:197
  171.9 316.9 %copy-start.50 = (f32[1,256]{1,0:T(1,128)}, f32[1,256]{1,0:T(1,128)S(1)}, u32[]{:S(2)}) copy-start(f32[1,256]{1,0:T(1,128)S(1)} %compare_convert_fusion) | copy-start | bytes 3076
  171.9 184.2 %copy-start.88 = (f32[256]{0:T(256)}, f32[256]{0:T(256)S(1)}, u32[]{:S(2)}) copy-start(f32[256]{0:T(256)S(1)} %broadcast_subtract_fusion) | copy-start | bytes 3076
  253.5 171.6 %copy-start.55 = (f32[768]{0:T(1024)}, f32[768]{0:T(1024)S(1)}, u32[]{:S(2)}) copy-start(f32[768]{0:T(1024)S(1)} %get-tuple-element.18) | copy-start | bytes 9220
  333.7 32.0 %copy-start.12 = (bf16[1024,768]{0,1:T(8,128)(2,1)}, bf16[1024,768]{0,1:T(8,128)(2,1)S(1)}, u32[]{:S(2)}) copy-start(bf16[1024,768]{0,1:T(8,128)(2,1)S(1)} %copy.150) | copy-start | bytes 4718596
  381.6 43.1 %copy-start.29 = (bf16[256,3072]{1,0:T(8,128)(2,1)}, bf16[256,3072]{1,0:T(8,128)(2,1)S(1)}, u32[]{:S(2)}) copy-start(bf16[256,3072]{1,0:T(8,128)(2,1)S(1)} %get-tuple-element.63) | copy-start | bytes 4718596
  424.8 179.9 %copy-start.4 = (f32[1,256,768]{2,1,0:T(8,128)}, f32[1,256,768]{2,1,0:T(8,128)S(1)}, u32[]{:S(2)}) copy-start(f32[1,256,768]{2,1,0:T(8,128)S(1)} %get-tuple-element.66) | copy-start | bytes 2359300
  425.9 60.8 %copy-start.37 = (bf16[1,256,768]{2,1,0:T(8,128)(2,1)}, bf16[1,256,768]{2,1,0:T(8,128)(2,1)S(1)}, u32[]{:S(2)}) copy-start(bf16[1,256,768]{2,1,0:T(8,128)(2,1)S(1)} %add_convert_fusion.1) | copy-start | bytes 1179652
  425.9 62.9 %copy-start.16 = (bf16[1,256,768]{2,1,0:T(8,128)(2,1)S(1)}, bf16[1,256,768]{2,1,0:T(8,128)(2,1)}, u32[]{:S(2)}) copy-start(bf16[1,256,768]{2,1,0:T(8,128)(2,1)} %param.17) | copy-start | bytes 1179652
  486.7 118.0 %all-gather.57.cloned.1.call-start = ((), (), s32[]{:S(2)}) async-start(), calls=%async_computation.39 | async-start | bytes 1216512 | tf_op jit(solution)/shard_map/all_gather | solution.py:184
  487.4 183.2 %all-gather.59.cloned.1.call-start = ((), (), s32[]{:S(2)}) async-start(), calls=%async_computation.40 | async-start | bytes 4866048 | tf_op jit(solution)/shard_map/all_gather | solution.py:185
  488.1 247.5 %all-gather.61.cloned.1.call-start = ((), (), s32[]{:S(2)}) async-start(), calls=%async_computation.41 | async-start | bytes 4866048 | tf_op jit(solution)/shard_map/all_gather | solution.py:186
  488.7 358.3 %reduce-scatter.15.cloned.1.call-start = ((), (), s32[]{:S(2)}) async-start(), calls=%async_computation.20 | async-start | bytes 3932160 | tf_op jit(solution)/shard_map/reduce_scatter | solution.py:279
  577.3 29.6 %copy-start.57 = (f32[768]{0:T(1024)S(1)}, f32[768]{0:T(1024)}, u32[]{:S(2)}) copy-start(f32[768]{0:T(1024)} %get-tuple-element.17) | copy-start | bytes 9220
  577.3 29.6 %copy-start.63 = (f32[768]{0:T(1024)S(1)}, f32[768]{0:T(1024)}, u32[]{:S(2)}) copy-start(f32[768]{0:T(1024)} %get-tuple-element.19) | copy-start | bytes 9220
  606.7 70.4 %copy-start.68 = (f32[256]{0:T(256)}, f32[256]{0:T(256)S(1)}, u32[]{:S(2)}) copy-start(f32[256]{0:T(256)S(1)} %broadcast_multiply_fusion) | copy-start | bytes 3076
  606.9 70.2 %copy-start.86 = (f32[256]{0:T(256)}, f32[256]{0:T(256)S(1)}, u32[]{:S(2)}) copy-start(f32[256]{0:T(256)S(1)} %multiply_reduce_fusion.2) | copy-start | bytes 3076
  606.9 70.2 %copy-start.78 = (f32[256]{0:T(256)}, f32[256]{0:T(256)S(1)}, u32[]{:S(2)}) copy-start(f32[256]{0:T(256)S(1)} %fusion.190) | copy-start | bytes 3076
  607.2 69.9 %copy-start.39 = (bf16[1,256,768]{2,1,0:T(8,128)(2,1)}, bf16[1,256,768]{2,1,0:T(8,128)(2,1)S(1)}, u32[]{:S(2)}) copy-start(bf16[1,256,768]{2,1,0:T(8,128)(2,1)S(1)} %add_convert_fusion) | copy-start | bytes 1179652
  787.7 59.3 %copy-start.5 = (f32[1,256,768]{2,1,0:T(8,128)S(1)}, f32[1,256,768]{2,1,0:T(8,128)}, u32[]{:S(2)}) copy-start(f32[1,256,768]{2,1,0:T(8,128)} %copy-done.4) | copy-start | bytes 2359300
  787.8 59.3 %copy-start.56 = (f32[768]{0:T(1024)S(1)}, f32[768]{0:T(1024)}, u32[]{:S(2)}) copy-start(f32[768]{0:T(1024)} %copy-done.55) | copy-start | bytes 9220
  787.8 59.3 %copy-start.67 = (f32[256]{0:T(256)S(1)}, f32[256]{0:T(256)}, u32[]{:S(2)}) copy-start(f32[256]{0:T(256)} %copy-done.66) | copy-start | bytes 3076
  787.8 59.3 %copy-start.77 = (f32[256]{0:T(256)S(1)}, f32[256]{0:T(256)}, u32[]{:S(2)}) copy-start(f32[256]{0:T(256)} %copy-done.76) | copy-start | bytes 3076
  787.8 242.2 %all-gather.65.cloned.1.call-start = ((), (), s32[]{:S(2)}) async-start(), calls=%async_computation.43 | async-start | bytes 1966080 | tf_op jit(solution)/shard_map/all_gather | solution.py:132
  793.2 240.1 %all-gather.63.cloned.1.call-start = ((), (), s32[]{:S(2)}) async-start(), calls=%async_computation.42 | async-start | bytes 1966080 | tf_op jit(solution)/shard_map/all_gather | solution.py:132
  866.4 31.8 %copy-start.89 = (f32[256]{0:T(256)}, f32[256]{0:T(256)S(1)}, u32[]{:S(2)}) copy-start(f32[256]{0:T(256)S(1)} %negate_multiply_fusion.1) | copy-start | bytes 3076
  867.5 172.6 %all-gather.69.cloned.1.call-start = ((), (), s32[]{:S(2)}) async-start(), calls=%async_computation.45 | async-start | bytes 1966080 | tf_op jit(solution)/shard_map/all_gather | solution.py:134
  868.1 241.3 %all-gather.67.cloned.1.call-start = ((), (), s32[]{:S(2)}) async-start(), calls=%async_computation.44 | async-start | bytes 1966080 | tf_op jit(solution)/shard_map/all_gather | solution.py:134
  868.7 251.6 %reduce-scatter.17.cloned.1.call-start = ((), (), s32[]{:S(2)}) async-start(), calls=%async_computation.21 | async-start | bytes 3932160 | tf_op jit(solution)/shard_map/reduce_scatter | solution.py:279
  870.8 27.4 %copy-start.20 = (bf16[1,256,768]{1,2,0:T(8,128)(2,1)S(1)}, bf16[1,256,768]{1,2,0:T(8,128)(2,1)}, u32[]{:S(2)}) copy-start(bf16[1,256,768]{1,2,0:T(8,128)(2,1)} %copy-done.19) | copy-start | bytes 1179652
  915.1 330.4 %all-gather.45.cloned.1.call-start = ((), (), s32[]{:S(2)}) async-start(), calls=%async_computation.30 | async-start | bytes 7864320 | tf_op jit(solution)/shard_map/all_gather | solution.py:133
  915.7 461.9 %all-gather.43.cloned.1.call-start = ((), (), s32[]{:S(2)}) async-start(), calls=%async_computation.28 | async-start | bytes 7864320 | tf_op jit(solution)/shard_map/all_gather | solution.py:133
  917.0 15.2 all-to-all-start.2
  932.3 25.8 %all-to-all-start.3 = ((bf16[256,8,4,24]{0,3,1,2:T(8,128)(2,1)}), bf16[256,8,4,24]{0,3,1,2:T(8,128)(2,1)S(1)}, u32[]{:S(2)}, u32[]{:S(2)}) async-start(bf16[256,8,4,24]{0,3,1,2:T(8,128)(2,1)} %copy.174), calls=%async_computation.8 | async-start | bytes 786432 | tf_op jit(solution)/shard_map/all_to_all | solution.py:126
  958.0 67.2 %all-to-all-start.7 = ((bf16[256,8,4,96]{0,3,1,2:T(8,128)(2,1)}), bf16[256,8,4,96]{0,3,1,2:T(8,128)(2,1)S(1)}, u32[]{:S(2)}, u32[]{:S(2)}) async-start(bf16[256,8,4,96]{0,3,1,2:T(8,128)(2,1)} %copy.186), calls=%async_computation.16 | async-start | bytes 3145728 | tf_op jit(solution)/shard_map/all_to_all | solution.py:128
  1026.3 81.4 %all-to-all-start.6 = ((bf16[256,8,4,96]{0,3,1,2:T(8,128)(2,1)}), bf16[256,8,4,96]{0,3,1,2:T(8,128)(2,1)S(1)}, u32[]{:S(2)}, u32[]{:S(2)}) async-start(bf16[256,8,4,96]{0,3,1,2:T(8,128)(2,1)} %copy.183), calls=%async_computation.14 | async-start | bytes 3145728 | tf_op jit(solution)/shard_map/all_to_all | solution.py:128
  1029.9 383.3 %reduce-scatter.25.cloned.1.call-start = ((), (), s32[]{:S(2)}) async-start(), calls=%async_computation.27 | async-start | bytes 331776 | tf_op jit(solution)/shard_map/reduce_scatter | solution.py:147
  1032.6 416.4 %reduce-scatter.23.cloned.1.call-start = ((), (), s32[]{:S(2)}) async-start(), calls=%async_computation.26 | async-start | bytes 331776 | tf_op jit(solution)/shard_map/reduce_scatter | solution.py:147
  1035.9 453.2 %reduce-scatter.33.cloned.1.call-start = ((), (), s32[]{:S(2)}) async-start(), calls=%async_computation.33 | async-start | bytes 1327104 | tf_op jit(solution)/shard_map/reduce_scatter | solution.py:153
  1044.4 485.0 %reduce-scatter.31.cloned.1.call-start = ((), (), s32[]{:S(2)}) async-start(), calls=%async_computation.32 | async-start | bytes 1327104 | tf_op jit(solution)/shard_map/reduce_scatter | solution.py:153
  1113.4 507.1 %all-gather.41.cloned.1.call-start = ((), (), s32[]{:S(2)}) async-start(), calls=%async_computation.24 | async-start | bytes 5898240 | tf_op jit(solution)/shard_map/all_gather | solution.py:131
  1114.7 596.1 %all-gather.39.cloned.1.call-start = ((), (), s32[]{:S(2)}) async-start(), calls=%async_computation.22 | async-start | bytes 5898240 | tf_op jit(solution)/shard_map/all_gather | solution.py:131
  1123.6 25.0 %all-to-all-start.5 = ((bf16[256,8,4,24]{0,3,1,2:T(8,128)(2,1)}), bf16[256,8,4,24]{0,3,1,2:T(8,128)(2,1)S(1)}, u32[]{:S(2)}, u32[]{:S(2)}) async-start(bf16[256,8,4,24]{0,3,1,2:T(8,128)(2,1)} %copy.180), calls=%async_computation.12 | async-start | bytes 786432 | tf_op jit(solution)/shard_map/all_to_all | solution.py:127
  1148.5 103.1 %all-to-all-start = ((bf16[256,8,4,24]{0,3,1,2:T(8,128)(2,1)}), bf16[256,8,4,24]{0,3,1,2:T(8,128)(2,1)S(1)}, u32[]{:S(2)}, u32[]{:S(2)}) async-start(bf16[256,8,4,24]{0,3,1,2:T(8,128)(2,1)} %copy.167), calls=%async_computation.2 | async-start | bytes 786432 | tf_op jit(solution)/shard_map/all_to_all | solution.py:125
  1152.0 597.3 %reduce-scatter.29.cloned.1.call-start = ((), (), s32[]{:S(2)}) async-start(), calls=%async_computation.31 | async-start | bytes 1327104 | tf_op jit(solution)/shard_map/reduce_scatter | solution.py:150
  1251.7 28.3 %all-to-all-start.4 = ((bf16[256,8,4,24]{0,3,1,2:T(8,128)(2,1)}), bf16[256,8,4,24]{0,3,1,2:T(8,128)(2,1)S(1)}, u32[]{:S(2)}, u32[]{:S(2)}) async-start(bf16[256,8,4,24]{0,3,1,2:T(8,128)(2,1)} %copy.177), calls=%async_computation.10 | async-start | bytes 786432 | tf_op jit(solution)/shard_map/all_to_all | solution.py:127
  1255.4 50.1 %copy-start.91 = (f32[768]{0:T(1024)S(1)}, f32[768]{0:T(1024)}, u32[]{:S(2)}) copy-start(f32[768]{0:T(1024)} %get-tuple-element.13) | copy-start | bytes 9220
  1255.4 50.0 %copy-start.23 = (f32[256,768]{1,0:T(8,128)S(1)}, f32[256,768]{1,0:T(8,128)}, u32[]{:S(2)}) copy-start(f32[256,768]{1,0:T(8,128)} %copy-done.22) | copy-start | bytes 2359300
  1279.9 24.3 %all-to-all-start.1 = ((bf16[256,8,4,24]{0,3,1,2:T(8,128)(2,1)}), bf16[256,8,4,24]{0,3,1,2:T(8,128)(2,1)S(1)}, u32[]{:S(2)}, u32[]{:S(2)}) async-start(bf16[256,8,4,24]{0,3,1,2:T(8,128)(2,1)} %copy.170), calls=%async_computation.4 | async-start | bytes 786432 | tf_op jit(solution)/shard_map/all_to_all | solution.py:125
  1283.4 506.2 %reduce-scatter.27.cloned.1.call-start = ((), (), s32[]{:S(2)}) async-start(), calls=%async_computation.29 | async-start | bytes 1327104 | tf_op jit(solution)/shard_map/reduce_scatter | solution.py:150
  1382.8 148.5 %copy-start.3 = (bf16[1,256,768]{2,1,0:T(8,128)(2,1)S(1)}, bf16[1,256,768]{2,1,0:T(8,128)(2,1)}, u32[]{:S(2)}) copy-start(bf16[1,256,768]{2,1,0:T(8,128)(2,1)} %param.9) | copy-start | bytes 1179652
  1382.8 148.5 %copy-start.49 = (f32[768]{0:T(1024)S(1)}, f32[768]{0:T(1024)}, u32[]{:S(2)}) copy-start(f32[768]{0:T(1024)} %copy-done.48) | copy-start | bytes 9220
  1382.8 148.5 %copy-start.62 = (f32[256]{0:T(256)S(1)}, f32[256]{0:T(256)}, u32[]{:S(2)}) copy-start(f32[256]{0:T(256)} %copy-done.61) | copy-start | bytes 3076
  1382.9 445.0 %reduce-scatter.21.cloned.1.call-start = ((), (), s32[]{:S(2)}) async-start(), calls=%async_computation.25 | async-start | bytes 995328 | tf_op jit(solution)/shard_map/reduce_scatter | solution.py:144
  1531.3 89.1 %copy-start.44 = (bf16[24,8,4,256]{3,1,2,0:T(8,128)(2,1)S(1)}, bf16[24,8,4,256]{3,1,2,0:T(8,128)(2,1)}, u32[]{:S(2)}) copy-start(bf16[24,8,4,256]{3,1,2,0:T(8,128)(2,1)} %copy.201) | copy-start | bytes 1179652
  1624.9 241.7 %reduce-scatter.19.cloned.1.call-start = ((), (), s32[]{:S(2)}) async-start(), calls=%async_computation.23 | async-start | bytes 995328 | tf_op jit(solution)/shard_map/reduce_scatter | solution.py:144
  (65 other events, 318.1 us)
Sparse Core Ops, SparseCore 0:
  11.4 63.5 all-gather.46
  166.9 67.3 all-gather.34
  237.1 52.8 all-gather.48
  293.2 62.6 all-gather.50
  358.6 62.3 all-gather.52
  423.6 58.9 all-gather.54
  486.8 62.2 all-gather.36
  551.9 52.7 all-gather.56
  608.1 62.4 all-gather.58
  673.2 62.3 all-gather.60
  787.9 59.1 reduce-scatter.14
  848.5 37.0 all-gather.64
  887.1 35.9 all-gather.62
  924.5 56.7 all-gather.68
  982.7 45.2 all-gather.66
  1030.2 82.7 reduce-scatter.16
  1114.4 131.0 all-gather.44
  1246.9 130.6 all-gather.42
  1381.2 32.0 reduce-scatter.24
  1416.2 32.8 reduce-scatter.22
  1452.3 36.7 reduce-scatter.32
  1492.7 36.7 reduce-scatter.30
  1531.1 89.3 all-gather.40
  1621.9 88.8 all-gather.38
  1714.0 35.3 reduce-scatter.28
  1752.8 36.7 reduce-scatter.26
  1792.7 35.1 reduce-scatter.20
  1831.4 35.0 reduce-scatter.18
where the time goes:
time: 1890 us; the launch traced here: 1880 us
  waiting for transfers between devices  1150 us (61%)
  blocking collectives  327 us (17%)
  matrix products  218 us (12%)
  local copies, waits for them, and re-layouts  88.5 us (5%)
  other arithmetic  44.2 us (2%)
  starting transfers between devices  30 us (2%)
    all_gather x2, waiting for transfers between devices, reduce_grads(): lax.all_gather(rights[2], 'kv', axis=0, tiled=True)  164 us
    all_gather x2, blocking collectives, local(): lax.all_gather(gains[number], ('rows', 'kv'), axis=1, tiled=True)  148 us
    all_gather x2, blocking collectives, local(): lax.all_gather(biases[number], ('rows', 'kv'), axis=1, tiled=True)  134 us
    all_gather x2, waiting for transfers between devices, reduce_grads(): lax.all_gather(rights[0], 'kv', axis=0, tiled=True)  126 us
    all_to_all x2, waiting for transfers between devices, reduce_grads(): lax.all_to_all(lefts[3], 'kv', split_axis=2, concat_axis=0, tiled=True)  121 us
    all_gather x2, waiting for transfers between devices, local(): lax.all_gather(w_down[number], ('rows', 'kv'), axis=0, tiled=True)  97.9 us
    reduce_scatter x2, waiting for transfers between devices, reduce_grads(): lax.psum_scatter(partial_sums[3].astype(jnp.bfloat16), 'rows', scatter_di...  79 us
    reduce_scatter x2, waiting for transfers between devices, reduce_grads(): lax.psum_scatter(partial_sums[0].astype(jnp.bfloat16), 'rows', scatter_di...  75.1 us
  transfers between devices with their start and end apart: 36, of which 26 were waited for; matrix products, arithmetic and copies ran while one was open for 15% of the time, Pallas kernels for 0%

commit v1 on v0

--- a/solution.py
+++ b/solution.py
@@ -3,6 +3,8 @@
 import jax
 import jax.numpy as jnp
 from jax import lax
+from jax.experimental import pallas as pl
+from jax.experimental.pallas import tpu as pltpu
 from jax.sharding import PartitionSpec as P
 
 HEADS = 12
@@ -162,7 +164,7 @@
     return results + (norm_parts[0], norm_parts[1])
 
 
-def local(tokens, lengths, w_qkv, w_out, w_up, w_down, gains, biases, cotangent):
+def local_generic(tokens, lengths, w_qkv, w_out, w_up, w_down, gains, biases, cotangent):
     rows_here, slot_dev, model_width = tokens.shape
     slot_count = slot_dev * lax.axis_size("kv")
     first_slot = lax.axis_index("kv") * slot_dev
@@ -315,6 +317,558 @@
     )
 
 
+F32 = jnp.float32
+BF16 = jnp.bfloat16
+MESH = pl.DeviceIdType.MESH
+ZN = 4
+
+
+def flip(value, unit):
+    bit = lax.rem(lax.div(value, unit), 2)
+    return value + unit - 2 * unit * bit
+
+
+def places_of():
+    r = lax.axis_index("rows")
+    z = lax.axis_index("kv")
+    return r, z, flip(r, 2), flip(r, 4), flip(flip(r, 2), 4), flip(r, 1)
+
+
+def turn(z, k):
+    return lax.rem(z + k, ZN)
+
+
+def rcopy(src, dst, ssem, rsem, device):
+    return pltpu.make_async_remote_copy(
+        src_ref=src, dst_ref=dst, send_sem=ssem, recv_sem=rsem, device_id=device, device_id_type=MESH
+    )
+
+
+def band(start, size):
+    return pl.ds(pl.multiple_of(start, 16), size)
+
+
+def greet(peers):
+    barrier = pltpu.get_barrier_semaphore()
+    for peer in peers:
+        pl.semaphore_signal(barrier, inc=1, device_id=peer, device_id_type=MESH)
+    pl.semaphore_wait(barrier, len(peers))
+
+
+def comm_peers():
+    r, z, rx, ry, rd, rc = places_of()
+    return [(r, turn(z, 1)), (r, turn(z, 2)), (r, turn(z, 3)), (rx, z), (ry, z), (rc, z)]
+
+
+def col_step(width):
+    return 256 if width % 256 == 0 else 128
+
+
+class Gather:
+    SEMS = 14
+
+    def __init__(self, own, whole, zm, zt, ssem, rsem, base):
+        self.own, self.whole, self.zm, self.zt = own, whole, zm, zt
+        self.ssem, self.rsem, self.base = ssem, rsem, base
+        self.split = zm is not None
+        self.rows = whole.shape[0] // 8
+        self.width = whole.shape[1]
+        self.sent = []
+
+    def _copy(self, src, dst, at, device):
+        return rcopy(src, dst, self.ssem.at[self.base + at], self.rsem.at[self.base + at], device)
+
+    def _block(self, r, half=None):
+        if half is None:
+            return self.whole.at[band(r * self.rows, self.rows), :]
+        part = self.rows // 2
+        return self.whole.at[band(r * self.rows + half * part, part), :]
+
+    def _send(self, src, dst, at, device):
+        copy = self._copy(src, dst, at, device)
+        copy.start()
+        self.sent.append(copy)
+
+    def prepare(self):
+        r, z = places_of()[:2]
+        if self.split:
+            half = self.width // 2
+            own = self.own[...].astype(F32)
+            self.zm[pl.ds(z, 1)] = own[:16].astype(BF16)[None]
+            self.zt[pl.ds(z, 1)] = jnp.concatenate([own[16:, :half], own[16:, half:]], 0).astype(BF16)[None]
+        else:
+            part = self.rows // ZN
+            self.whole[band(r * self.rows + z * part, part), :] = self.own[...]
+
+    def _zrefs(self, z):
+        if self.split:
+            return [self.zm.at[z], self.zt.at[z]]
+        part = self.rows // ZN
+        return [self.whole.at[band(places_of()[0] * self.rows + z * part, part), :]]
+
+    def send_z(self):
+        r, z = places_of()[:2]
+        for k in (1, 2, 3):
+            for i, ref in enumerate(self._zrefs(z)):
+                self._send(ref, ref, 2 * (k - 1) + i, (r, turn(z, k)))
+
+    def wait_z(self):
+        r, z = places_of()[:2]
+        for k in (1, 2, 3):
+            for i, ref in enumerate(self._zrefs(turn(z, ZN - k))):
+                self._copy(ref, ref, 2 * (k - 1) + i, (r, turn(z, ZN - k))).wait_recv()
+        if self.split:
+            half = self.width // 2
+            step = col_step(half)
+            for side in (0, 1):
+                def assemble(i, carry, side=side):
+                    at = pl.multiple_of(i * step, step)
+                    here = pl.ds(pl.multiple_of(side * half + i * step, 128), step)
+                    parts = []
+                    for piece in range(ZN):
+                        parts.append(self.zm[piece, :, here].astype(F32))
+                        parts.append(self.zt[piece, :, pl.ds(at, step)].astype(F32)[8 * side : 8 * side + 8])
+                    self.whole[band(r * self.rows, self.rows), here] = jnp.concatenate(parts, 0).astype(BF16)
+                    return carry
+                lax.fori_loop(0, half // step, assemble, 0)
+
+    def send_plane(self):
+        r, z, rx, ry, rd, rc = places_of()
+        own = self._block(r)
+        self._send(own, own, 6, (rx, z))
+        self._send(own, own, 7, (ry, z))
+        self._send(own, own, 10, (rc, z))
+
+    def forward(self):
+        r, z, rx, ry, rd, rc = places_of()
+        first, second = self._block(rx), self._block(ry)
+        self._copy(first, first, 6, (rx, z)).wait_recv()
+        part = self._block(rx, 0)
+        self._send(part, part, 8, (ry, z))
+        self._send(first, first, 11, (rc, z))
+        self._copy(second, second, 7, (ry, z)).wait_recv()
+        part = self._block(ry, 1)
+        self._send(part, part, 9, (rx, z))
+        self._send(second, second, 12, (rc, z))
+
+    def forward_last(self):
+        r, z, rx, ry, rd, rc = places_of()
+        part = self._block(rd, 0)
+        self._copy(part, part, 8, (ry, z)).wait_recv()
+        part = self._block(rd, 1)
+        self._copy(part, part, 9, (rx, z)).wait_recv()
+        diagonal = self._block(rd)
+        self._send(diagonal, diagonal, 13, (rc, z))
+
+    def finish(self):
+        r, z, rx, ry, rd, rc = places_of()
+        for at, block in ((10, r), (11, rx), (12, ry), (13, rd)):
+            ref = self._block(flip(block, 1))
+            self._copy(ref, ref, at, (rc, z)).wait_recv()
+
+    def drain(self):
+        for copy in self.sent:
+            copy.wait_send()
+
+
+def add_rows(dst, src, rows):
+    def step(i, carry):
+        here = band(i * 16, 16)
+        dst[here, :] = (dst[here, :].astype(F32) + src[here, :].astype(F32)).astype(BF16)
+        return carry
+    lax.fori_loop(0, rows // 16, step, 0)
+
+
+class Scatter:
+    SEMS = 14
+
+    def __init__(self, mine, got, half, near, zs, zr, out, ssem, rsem, base):
+        self.mine, self.got, self.half, self.near = mine, got, half, near
+        self.zs, self.zr, self.out = zs, zr, out
+        self.ssem, self.rsem, self.base = ssem, rsem, base
+        self.rows, self.width = mine.shape[1], mine.shape[2]
+        self.split = len(zs) == 2
+        self.sent = []
+
+    def _copy(self, src, dst, at, device):
+        return rcopy(src, dst, self.ssem.at[self.base + at], self.rsem.at[self.base + at], device)
+
+    def _send(self, src, dst, at, device):
+        copy = self._copy(src, dst, at, device)
+        copy.start()
+        self.sent.append(copy)
+
+    def send_core(self, b, src):
+        r, z, rx, ry, rd, rc = places_of()
+        self._send(src, self.got.at[b], b, (rc, z))
+
+    def add_core(self, b):
+        r, z, rx, ry, rd, rc = places_of()
+        self._copy(self.got.at[b], self.got.at[b], b, (rc, z)).wait_recv()
+        add_rows(self.mine.at[b], self.got.at[b], self.rows)
+
+    def add_core_block(self, block):
+        r, z, rx, ry, rd, rc = places_of()
+        return block
+
+    def send_diagonal(self):
+        r, z, rx, ry, rd, rc = places_of()
+        part = self.rows // 2
+        diagonal = lax.div(rd, 2)
+        self._send(self.mine.at[diagonal, pl.ds(0, part)], self.half.at[0], 4, (ry, z))
+        self._send(self.mine.at[diagonal, pl.ds(part, part)], self.half.at[1], 5, (rx, z))
+
+    def send_near(self):
+        r, z, rx, ry, rd, rc = places_of()
+        part = self.rows // 2
+        for at, side, other in ((4, ry, rx), (5, rx, ry)):
+            i = at - 4
+            self._copy(self.half.at[i], self.half.at[i], at, (side, z)).wait_recv()
+            block = self.mine.at[lax.div(other, 2)]
+            add_rows(block.at[pl.ds(i * part, part)], self.half.at[i], part)
+            self._send(block, self.near.at[i], 6 + i, (other, z))
+
+    def send_z(self):
+        r, z, rx, ry, rd, rc = places_of()
+        for i, side in ((0, rx), (1, ry)):
+            self._copy(self.near.at[i], self.near.at[i], 6 + i, (side, z)).wait_recv()
+        own = self.mine.at[lax.div(r, 2)]
+        if self.split:
+            half = self.width // 2
+            step = col_step(half)
+            def cut(i, carry):
+                sums = []
+                for side in (0, 1):
+                    here = pl.ds(pl.multiple_of(side * half + i * step, 128), step)
+                    sums.append(
+                        own[:, here].astype(F32) + self.near[0, :, here].astype(F32) + self.near[1, :, here].astype(F32)
+                    )
+                at = pl.ds(pl.multiple_of(i * step, 128), step)
+                for piece in range(ZN):
+                    for side in (0, 1):
+                        here = pl.ds(pl.multiple_of(side * half + i * step, 128), step)
+                        self.zs[0][piece, :, here] = sums[side][24 * piece : 24 * piece + 16].astype(BF16)
+                    self.zs[1][piece, :, at] = jnp.concatenate(
+                        [sums[side][24 * piece + 16 : 24 * piece + 24] for side in (0, 1)], 0
+                    ).astype(BF16)
+                return carry
+            lax.fori_loop(0, half // step, cut, 0)
+        else:
+            part = self.rows // ZN
+            for piece in range(ZN):
+                def cut_rows(i, carry, piece=piece):
+                    here = band(piece * part + i * 16, 16)
+                    self.zs[0][piece, band(i * 16, 16), :] = (
+                        own[here, :].astype(F32) + self.near[0, here, :].astype(F32) + self.near[1, here, :].astype(F32)
+                    ).astype(BF16)
+                    return carry
+                lax.fori_loop(0, part // 16, cut_rows, 0)
+        for k in (1, 2, 3):
+            for i in range(len(self.zs)):
+                self._send(self.zs[i].at[turn(z, k)], self.zr[i].at[k - 1], 8 + 2 * (k - 1) + i, (r, turn(z, k)))
+
+    def finish(self):
+        r, z = places_of()[:2]
+        for k in (1, 2, 3):
+            for i in range(len(self.zs)):
+                ref = self.zr[i].at[k - 1]
+                self._copy(ref, ref, 8 + 2 * (k - 1) + i, (r, turn(z, ZN - k))).wait_recv()
+        if self.split:
+            half = self.width // 2
+            main = self.zs[0][z].astype(F32)
+            tail = self.zs[1][z].astype(F32)
+            for k in range(3):
+                main = main + self.zr[0][k].astype(F32)
+                tail = tail + self.zr[1][k].astype(F32)
+            self.out[pl.ds(0, 16), :] = main
+            self.out[pl.ds(16, 8), pl.ds(0, half)] = tail[:8]
+            self.out[pl.ds(16, 8), pl.ds(half, half)] = tail[8:]
+        else:
+            def total(i, carry):
+                here = band(i * 16, 16)
+                value = self.zs[0][z, here, :].astype(F32)
+                for k in range(3):
+                    value = value + self.zr[0][k, here, :].astype(F32)
+                self.out[here, :] = value
+                return carry
+            lax.fori_loop(0, self.out.shape[0] // 16, total, 0)
+
+    def drain(self):
+        for copy in self.sent:
+            copy.wait_send()
+
+
+def gather_kernel(*refs):
+    owns, outs, rest = refs[:8], refs[8:16], list(refs[16:])
+    wholes = [rest.pop(0) for _ in range(8)]
+    zbuf = [(None, None) if n % 4 == 3 else (rest.pop(0), rest.pop(0)) for n in range(8)]
+    ssem, rsem, osem = rest
+    greet(comm_peers())
+    jobs = [
+        Gather(owns[n], wholes[n], zbuf[n][0], zbuf[n][1], ssem, rsem, n * Gather.SEMS) for n in range(8)
+    ]
+    for job in jobs:
+        job.prepare()
+        job.send_z()
+    stores = []
+    for n in range(8 + 3):
+        if n < 8:
+            jobs[n].wait_z()
+            jobs[n].send_plane()
+        if 0 <= n - 1 < 8:
+            jobs[n - 1].forward()
+        if 0 <= n - 2 < 8:
+            jobs[n - 2].forward_last()
+        if 0 <= n - 3 < 8:
+            jobs[n - 3].finish()
+            store = pltpu.make_async_copy(wholes[n - 3], outs[n - 3], osem.at[n - 3])
+            store.start()
+            stores.append(store)
+    for job in jobs:
+        job.drain()
+    for store in stores:
+        store.wait()
+
+
+def gather_weights(owns):
+    shapes = [((own.shape[0] * 32), own.shape[1]) for own in owns]
+    zshapes = []
+    for n, own in enumerate(owns):
+        if n % 4 != 3:
+            zshapes += [
+                pltpu.VMEM((ZN, 16, own.shape[1]), BF16),
+                pltpu.VMEM((ZN, 16, own.shape[1] // 2), BF16),
+            ]
+    return pl.pallas_call(
+        gather_kernel,
+        out_shape=[jax.ShapeDtypeStruct(shape, BF16) for shape in shapes],
+        in_specs=[pl.BlockSpec(memory_space=pltpu.VMEM)] * 8,
+        out_specs=[pl.BlockSpec(memory_space=pl.ANY)] * 8,
+        scratch_shapes=[pltpu.VMEM(shape, BF16) for shape in shapes]
+        + zshapes
+        + [
+            pltpu.SemaphoreType.DMA((8 * Gather.SEMS,)),
+            pltpu.SemaphoreType.DMA((8 * Gather.SEMS,)),
+            pltpu.SemaphoreType.DMA((8,)),
+        ],
+        compiler_params=pltpu.CompilerParams(collective_id=0, has_side_effects=True, vmem_limit_bytes=58 * 2**20),
+    )(*owns)
+
+
+def scatter_kernel(*refs):
+    terms, outs, rest = refs[:4], refs[4:8], list(refs[8:])
+    jobs = []
+    sems = rest[-3:]
+    ssem, rsem, lsem = sems
+    greet(comm_peers())
+    r, z, rx, ry, rd, rc = places_of()
+    for n in range(4):
+        mine, got, half, near = [rest.pop(0) for _ in range(4)]
+        count = 1 if n == 3 else 2
+        zs = [rest.pop(0) for _ in range(count)]
+        zr = [rest.pop(0) for _ in range(count)]
+        jobs.append(Scatter(mine, got, half, near, zs, zr, outs[n], ssem, rsem, n * Scatter.SEMS))
+    loads = []
+    for n, job in enumerate(jobs):
+        rows = job.rows
+        for b in range(4):
+            theirs = terms[n].at[band((2 * b + lax.rem(rc, 2)) * rows, rows), :]
+            job.send_core(b, theirs)
+            ours = terms[n].at[band((2 * b + lax.rem(r, 2)) * rows, rows), :]
+            load = pltpu.make_async_copy(ours, job.mine.at[b], lsem.at[4 * n + b])
+            load.start()
+            loads.append(load)
+    for n in range(4 + 3):
+        if n < 4:
+            for b in range(4):
+                loads[4 * n + b].wait()
+                jobs[n].add_core(b)
+            jobs[n].send_diagonal()
+        if 0 <= n - 1 < 4:
+            jobs[n - 1].send_near()
+        if 0 <= n - 2 < 4:
+            jobs[n - 2].send_z()
+        if 0 <= n - 3 < 4:
+            jobs[n - 3].finish()
+    for job in jobs:
+        job.drain()
+
+
+def scatter_grads(terms):
+    scratch = []
+    outs = []
+    for n, term in enumerate(terms):
+        rows, width = term.shape[0] // 8, term.shape[1]
+        scratch += [
+            pltpu.VMEM((4, rows, width), BF16),
+            pltpu.VMEM((4, rows, width), BF16),
+            pltpu.VMEM((2, rows // 2, width), BF16),
+            pltpu.VMEM((2, rows, width), BF16),
+        ]
+        if n == 3:
+            cuts = [(rows // 4, width)]
+        else:
+            cuts = [(16, width), (16, width // 2)]
+        scratch += [pltpu.VMEM((4,) + cut, BF16) for cut in cuts]
+        scratch += [pltpu.VMEM((3,) + cut, BF16) for cut in cuts]
+        outs.append(jax.ShapeDtypeStruct((rows // 4, width), F32))
+    return pl.pallas_call(
+        scatter_kernel,
+        out_shape=outs,
+        in_specs=[pl.BlockSpec(memory_space=pl.ANY)] * 4,
+        out_specs=[pl.BlockSpec(memory_space=pltpu.VMEM)] * 4,
+        scratch_shapes=scratch
+        + [
+            pltpu.SemaphoreType.DMA((4 * Scatter.SEMS,)),
+            pltpu.SemaphoreType.DMA((4 * Scatter.SEMS,)),
+            pltpu.SemaphoreType.DMA((16,)),
+        ],
+        compiler_params=pltpu.CompilerParams(collective_id=1, has_side_effects=True, vmem_limit_bytes=58 * 2**20),
+    )(*terms)
+
+
+def local_fast(tokens, lengths, w_qkv, w_out, w_up, w_down, gains, biases, cotangent):
+    rows_here, slot_dev, model_width = tokens.shape
+    slot_count = slot_dev * lax.axis_size("kv")
+    first_slot = lax.axis_index("kv") * slot_dev
+    scaling = 1.0 / math.sqrt(HEAD)
+    doc_ends = jnp.cumsum(lengths, -1)
+    places = jnp.arange(slot_count, dtype=jnp.int32)
+    docs_all = jnp.sum((doc_ends[:, None, :] <= places[None, :, None]).astype(jnp.int32), -1)
+    live_all = (places[None, :] < doc_ends[:, -1:]).astype(jnp.float32)
+    docs_here = lax.dynamic_slice_in_dim(docs_all, first_slot, slot_dev, 1)
+    live_here = lax.dynamic_slice_in_dim(live_all, first_slot, slot_dev, 1)
+    local_places = first_slot + jnp.arange(slot_dev, dtype=jnp.int32)
+    masks = make_mask(local_places, docs_here[0], live_here[0], places, docs_all[0], live_all[0])
+    stream = tokens.astype(jnp.float32)
+    norms = lax.all_gather(
+        jnp.concatenate([gains.reshape(4, -1), biases.reshape(4, -1)], 0), ("rows", "kv"), axis=1, tiled=True
+    )
+    weights = gather_weights([w[number] for number in range(LAYERS) for w in (w_qkv, w_out, w_up, w_down)])
+    gathered = [
+        tuple(weights[4 * number : 4 * number + 4]) + (norms[2 * number : 2 * number + 2], norms[4 + 2 * number : 6 + 2 * number])
+        for number in range(LAYERS)
+    ]
+    stored = []
+    for number in range(LAYERS):
+        signed = number == 0
+        pieces = gathered[number]
+        full_qkv, full_out, full_up, full_down, gain_pair, bias_pair = pieces
+        gain_pair = gain_pair.astype(jnp.float32)
+        bias_pair = bias_pair.astype(jnp.float32)
+        normed_in = norm_rows(stream, gain_pair[0], bias_pair[0]).astype(jnp.bfloat16)
+        projected = jnp.dot(normed_in, full_qkv, preferred_element_type=jnp.float32).astype(
+            jnp.bfloat16
+        )
+        kv_all = lax.all_gather(projected[:, :, model_width:], "kv", axis=1, tiled=True)
+        attended = jnp.stack(
+            [
+                attend_row(
+                    projected[0, :, :model_width], kv_all[0], masks, live_here[0], signed, scaling
+                )
+            ]
+        )
+        shared = kv_all
+        middle = stream + jnp.dot(attended, full_out, preferred_element_type=jnp.float32)
+        normed_mid = norm_rows(middle, gain_pair[1], bias_pair[1]).astype(jnp.bfloat16)
+        pre_act = jnp.dot(normed_mid, full_up, preferred_element_type=jnp.float32)
+        activated = jax.nn.gelu(pre_act).astype(jnp.bfloat16)
+        stored.append(
+            (
+                stream,
+                normed_in,
+                projected,
+                shared,
+                attended,
+                middle,
+                normed_mid,
+                pre_act,
+                activated,
+                pieces,
+            )
+        )
+        stream = middle + jnp.dot(activated, full_down, preferred_element_type=jnp.float32)
+    result = (stream * live_here[..., None]).astype(jnp.bfloat16)
+    residual_grad = cotangent.astype(jnp.float32) * live_here[..., None]
+    collected = [None] * LAYERS
+    norm_grads = [None] * LAYERS
+    for number in reversed(range(LAYERS)):
+        signed = number == 0
+        (
+            stream_in,
+            normed_in,
+            projected,
+            shared,
+            attended,
+            middle,
+            normed_mid,
+            pre_act,
+            activated,
+            kept,
+        ) = stored[number]
+        pieces = gathered[number]
+        full_qkv, full_out, full_up, full_down, gain_pair, bias_pair = pieces
+        gain_pair = gain_pair.astype(jnp.float32)
+        bias_pair = bias_pair.astype(jnp.float32)
+        down_in = residual_grad.astype(jnp.bfloat16)
+        act_grad = jnp.einsum("rtd,fd->rtf", down_in, full_down, preferred_element_type=jnp.float32)
+        unused, gelu_pull = jax.vjp(jax.nn.gelu, pre_act)
+        pre_grad = gelu_pull(act_grad)[0].astype(jnp.bfloat16)
+        mid_normed_grad = jnp.einsum(
+            "rtf,df->rtd", pre_grad, full_up, preferred_element_type=jnp.float32
+        )
+        unused, norm_pull = jax.vjp(norm_rows, middle, gain_pair[1], bias_pair[1])
+        middle_part, gain_late, bias_late = norm_pull(mid_normed_grad)
+        middle_grad = residual_grad + middle_part
+        branch_grad = middle_grad.astype(jnp.bfloat16)
+        att_grad = jnp.einsum(
+            "rte,de->rtd", branch_grad, full_out, preferred_element_type=jnp.float32
+        ).astype(jnp.bfloat16)
+        kv_all = shared
+        query_grad, kv_grad = attend_back(
+            projected[0, :, :model_width],
+            kv_all[0],
+            att_grad[0],
+            masks,
+            live_here[0],
+            signed,
+            scaling,
+        )
+        query_grads = [query_grad]
+        kv_grads = [kv_grad]
+        kv_here = lax.psum_scatter(
+            jnp.stack(kv_grads).astype(jnp.bfloat16), "kv", scatter_dimension=1, tiled=True
+        ).astype(jnp.float32)
+        qkv_grad = jnp.concatenate([jnp.stack(query_grads), kv_here], -1).astype(jnp.bfloat16)
+        in_normed_grad = jnp.einsum(
+            "rte,de->rtd", qkv_grad, full_qkv, preferred_element_type=jnp.float32
+        )
+        unused, first_pull = jax.vjp(norm_rows, stream_in, gain_pair[0], bias_pair[0])
+        stream_part, gain_early, bias_early = first_pull(in_normed_grad)
+        residual_grad = middle_grad + stream_part
+        pairs = [
+            (normed_in, qkv_grad),
+            (attended, branch_grad),
+            (normed_mid, pre_grad),
+            (activated, down_in),
+        ]
+        terms = [
+            jnp.einsum("ti,to->io", left[0], right[0], preferred_element_type=F32).astype(BF16)
+            for left, right in pairs
+        ]
+        collected[number] = scatter_grads(terms)
+        norm_grads[number] = [gain_early, gain_late, bias_early, bias_late]
+    norm_sums = lax.psum_scatter(
+        jnp.stack([norm_grads[n][i] for n in range(LAYERS) for i in range(4)]), ("rows", "kv"), scatter_dimension=1, tiled=True
+    ).reshape(LAYERS, 4, -1)
+    return (
+        result,
+        residual_grad,
+    ) + tuple(jnp.stack([collected[number][i] for number in range(LAYERS)]) for i in range(4)) + (
+        norm_sums[:, :2], norm_sums[:, 2], norm_sums[:, 3]
+    )
+
+
 def solution(mesh):
     in_specs = (
         P("rows", "kv", None),
@@ -338,4 +892,5 @@
         P(None, ("rows", "kv")),
         P(None, ("rows", "kv")),
     )
-    return jax.shard_map(local, mesh=mesh, in_specs=in_specs, out_specs=out_specs, check_vma=False)
+    fast = dict(mesh.shape) == {"rows": 8, "kv": 4}
+    return jax.shard_map(local_fast if fast else local_generic, mesh=mesh, in_specs=in_specs, out_specs=out_specs, check_vma=False)

time: 1890 us -> 866 us (0.46)
  waiting for transfers between devices: 1150 us -> 181 us
  Pallas kernels: 0 us -> 299 us
  blocking collectives: 327 us -> 111 us
  local copies, waits for them, and re-layouts: 88.5 us -> 46.2 us
  matrix products: 218 us -> 177 us
  starting transfers between devices: 30 us -> 0.16 us
    all_gather x18 -> x2, waiting for transfers between devices: 595 us -> 128 us  [local_fast(): lax.all_gather(projected[:, :, model_width:], 'kv', axis=1, tiled=True)]
    pallas_call x0 -> x3, Pallas kernels: none -> 299 us  [the longest x2 161 us: scatter_grads(): pl.pallas_call(scatter_kernel, out_shape=outs, in_specs=[pl.BlockSpec(mem...]
    reduce_scatter x10 -> x2, waiting for transfers between devices: 337 us -> 53 us  [local_fast(): lax.psum_scatter(jnp.stack(kv_grads).astype(jnp.bfloat16), 'kv', scatter_...]
    all_to_all x8 -> x0, waiting for transfers between devices: 215 us -> none  [the longest x2 121 us: reduce_grads(): lax.all_to_all(lefts[3], 'kv', split_axis=2, concat_axis=0, tiled=True)]
    all_gather x4 -> x1, blocking collectives: 282 us -> 70.1 us  [local_fast(): lax.all_gather(jnp.concatenate([gains.reshape(4, -1), biases.reshape(4, -...]
    dot_general x24, matrix products: 98.8 us -> 63.2 us  [the longest x8 29.8 us: local_fast(): jnp.einsum('ti,to->io', left[0], right[0], preferred_element_type=F32)]
    all_to_all x8 -> x0, starting transfers between devices: 28.4 us -> none  [the longest x2 7.42 us: reduce_grads(): lax.all_to_all(lefts[3], 'kv', split_axis=2, concat_axis=0, tiled=True)]
    slice x19 -> x11, local copies, waits for them, and re-layouts: 27 us -> 5.06 us  [the longest x2 1.87 us: local_fast(): projected[:, :, model_width:]]
  transfers between devices with their start and end apart: 36 -> 4, of which waited for: 26 -> 3; matrix products, arithmetic and copies ran while one was open for 15% -> 5% of each run, Pallas kernels for 0% -> 9%
where the time goes in v1:
time: 866 us; the launch traced here: 860 us
  Pallas kernels  299 us (35%)
  waiting for transfers between devices  181 us (21%)
  matrix products  177 us (20%)
  blocking collectives  111 us (13%)
  local copies, waits for them, and re-layouts  46.2 us (5%)
  other arithmetic  30.5 us (4%)
  between operations  15.2 us (2%)
    pallas_call x2, Pallas kernels, scatter_grads(): pl.pallas_call(scatter_kernel, out_shape=outs, in_specs=[pl.BlockSpec(mem...  161 us
    pallas_call x1, Pallas kernels, gather_weights(): pl.pallas_call(gather_kernel, out_shape=[jax.ShapeDtypeStruct(shape, BF16...  138 us
    all_gather x2, waiting for transfers between devices, local_fast(): lax.all_gather(projected[:, :, model_width:], 'kv', axis=1, tiled=True)  128 us
    all_gather x1, blocking collectives, local_fast(): lax.all_gather(jnp.concatenate([gains.reshape(4, -1), biases.reshape(4, -...  70.1 us
    reduce_scatter x2, waiting for transfers between devices, local_fast(): lax.psum_scatter(jnp.stack(kv_grads).astype(jnp.bfloat16), 'kv', scatter_...  53 us
    unnamed x1, blocking collectives  41 us
    dot_general x8, matrix products, local_fast(): jnp.einsum('ti,to->io', left[0], right[0], preferred_element_type=F32)  29.8 us
    sub x1, matrix products, score_grads(): tanh_s * weight_grad - inner_sum  25.8 us
  transfers between devices with their start and end apart: 4, of which 3 were waited for; matrix products, arithmetic and copies ran while one was open for 5% of the time, Pallas kernels for 9%

profile of v1, /device:TPU:0, one launch (start us, length us, event | category | flops | bytes accessed | tf_op | source)
XLA Modules:
  0.0 860.0 jit_solution(16357039857227522780)
XLA Ops:
  7.2 1.7 slice_bitcast_fusion.4
  8.9 1.4 slice_bitcast_fusion.6
  10.3 1.7 slice_bitcast_fusion.1
  12.1 1.7 slice_bitcast_fusion
  14.5 70.1 %all-gather = bf16[32,24,8]{1,2,0:T(8,128)(2,1)S(1)} all-gather(bf16[1,24,8]{1,2,0:T(8,128)(2,1)S(1)} %maximum_bitcast_fusion), channel_id=1, replica_groups=mesh['rows'=8,'kv'=4] {'rows','kv'}, dimensions={0}, use_global_device_ids=true | all-gather | bytes 12672 | tf_op jit(solution)/shard_map/all_gather | solution.py:744
  85.9 1.2 fusion.81
  87.3 137.7 %shard_map.160 = (bf16[768,2304]{1,0:T(8,128)(2,1)}, bf16[768,768]{1,0:T(8,128)(2,1)}, bf16[768,3072]{1,0:T(8,128)(2,1)}, bf16[3072,768]{1,0:T(8,128)(2,1)}, bf1...) custom-call(bf16[24,2304]{1,0:T(8,128)(2,1)} %get-tuple-element.72.ref, ...), custom_call_target="tpu_custom_call" | custom-call | tf_op jit(solution)/shard_map/pallas_call | solution.py:642
  225.0 3.2 fusion.21
  233.2 67.1 %all-gather.4.cloned.1.call-done = bf16[1,1024,1536]{2,1,0:T(8,128)(2,1)} async-done(((bf16[1,256,1536]{2,1,0:T(8,128)(2,1)}), bf16[1,1024,1536]{2,1,0:T(8,128)(2,1)}) %all-gather.4.cloned.1.call-update) | async-done | bytes 3145744 | tf_op jit(solution)/shard_map/all_gather | solution.py:763
  300.2 3.8 fusion.144
  304.0 1.9 copy.53
  305.9 3.2 copy.55
  309.0 22.2 %fusion.146 = (f32[12,256]{1,0:T(8,128)S(1)}, f32[12,256,1024]{2,1,0:T(8,128)}) fusion(f32[256,1024]{1,0:T(8,128)S(1)} %select_multiply_fusion, pred[256,1024]{1,0:T(8,128)(4,1)} %broadcast_compare_fusion, bf16[256,12,64]{0,2,1:T(8,128)(2,1)S(1)} %bitcast.250, bf16[1024,12,64]{0,2,1:T(8,128)(2,1)} %bitcast.243), kind=kOutput, calls=%fused_computation.233 | convolution fusion | flops 839910400 | bytes 15872000 | tf_op jit(solution)/shard_map/sub | solution.py:28
  331.2 9.5 %tanh_multiply_fusion = (f32[12,256,1024]{2,1,0:T(8,128)S(1)}, f32[12,256,1024]{2,1,0:T(8,128)}) fusion(f32[12,256,1024]{2,1,0:T(8,128)} %get-tuple-element.82, f32[12,256]{1,0:T(8,128)S(1)} %broadcast_add_fusion.1, bf16[256,12,64]{0,2,1:T(8,128)(2,1)} %bitcast.251, bf16[1024,12,64]{0,2,1:T(8,128)(2,1)} %bitcast.244), kind=kOutput, calls=%fused_computation.6 | convolution fusion | flops 412090368 | bytes 39727104 | tf_op jit(solution)/shard_map/qhd,khd->hqk/dot_general | solution.py:70
  340.8 2.0 fusion.62
  342.8 4.2 copy-done.1
  347.9 1.5 fusion.138
  349.6 2.0 fusion.148
  357.0 61.0 %all-gather.6.cloned.1.call-done = bf16[1,1024,1536]{2,1,0:T(8,128)(2,1)} async-done(((bf16[1,256,1536]{2,1,0:T(8,128)(2,1)}), bf16[1,1024,1536]{2,1,0:T(8,128)(2,1)}) %all-gather.6.cloned.1.call-update) | async-done | bytes 3145744 | tf_op jit(solution)/shard_map/all_gather | solution.py:763
  418.0 3.7 fusion.143
  421.8 2.9 copy.56
  424.7 2.6 copy.58
  427.3 10.8 %fusion.149 = (f32[12,256]{1,0:T(8,128)S(1)}, f32[12,256,1024]{2,1,0:T(8,128)}) fusion(f32[256,1024]{1,0:T(8,128)} %copy-done.30, pred[256,1024]{1,0:T(8,128)(4,1)S(1)} %copy-done.35, bf16[256,12,64]{0,2,1:T(8,128)(2,1)S(1)} %bitcast.253, bf16[1024,12,64]{0,2,1:T(8,128)(2,1)} %bitcast.246), kind=kOutput, calls=%fused_computation.236 | convolution fusion | flops 827327488 | bytes 15872000 | tf_op jit(solution)/shard_map/sub | solution.py:31
  438.1 7.3 fusion.65
  446.4 1.5 fusion.133
  448.2 4.1 fusion.36
  452.3 1.6 fusion.83
  455.8 1.3 convolution_convert_fusion.11
  457.0 1.9 copy.59
  459.0 6.4 fusion.50
  465.4 9.2 %multiply_reduce_fusion.1 = (f32[12,256]{1,0:T(8,128)S(1)}, f32[12,256,1024]{2,1,0:T(8,128)}) fusion(f32[12,256,1024]{2,1,0:T(8,128)} %get-tuple-element.90, f32[12,256]{1,0:T(8,128)S(1)} %broadcast_add_fusion, bf16[256,12,64]{0,2,1:T(8,128)(2,1)S(1)} %bitcast.273, bf16[1024,12,64]{0,2,1:T(8,128)(2,1)S(1)} %bitcast.262), kind=kOutput, calls=%fused_computation.8 | convolution fusion | flops 412087296 | bytes 27156480 | tf_op jit(solution)/shard_map/qhd,khd->hqk/dot_general | solution.py:94
  474.6 5.9 multiply_convert_fusion.1
  481.8 1.4 copy-done
  483.2 2.0 pad_maximum_fusion
  485.3 6.0 fusion.69
  491.4 53.0 %reduce-scatter.4.cloned.1.call-done = bf16[1,256,1536]{1,2,0:T(8,128)(2,1)} async-done(((bf16[1,1024,1536]{1,2,0:T(8,128)(2,1)}), bf16[1,256,1536]{1,2,0:T(8,128)(2,1)}) %reduce-scatter.4.cloned.1.call-update) | async-done | bytes 786448 | tf_op jit(solution)/shard_map/reduce_scatter | solution.py:839
  544.3 3.8 fusion.84
  549.3 1.4 copy-done.55
  550.7 3.1 fusion.29
  553.9 1.6 fusion.85
  557.0 1.3 convolution_convert_fusion.10
  558.3 1.9 copy.60
  560.2 7.1 fusion.47
  567.3 25.8 %multiply_convert_fusion = bf16[12,256,1024]{2,1,0:T(8,128)(2,1)} fusion(f32[12,256,1024]{2,1,0:T(8,128)} %get-tuple-element.84, f32[12,256,1024]{2,1,0:T(8,128)} %copy-done.1, f32[12,256,1024]{2,1,0:T(8,128)} %get-tuple-element.82, f32[12,256]{1,0:T(8,128)S(1)} %broadcast_add_fusion.1, bf16[256,12,64]{0,2,1:T(8,128)(2,1)} %bitcast.267, ...), kind=kOutput, calls=%fused_computation.3 | convolution fusion | flops 852496384 | bytes 46018560 | tf_op jit(solution)/shard_map/sub | solution.py:61
  593.2 4.2 multiply_convert_fusion.2
  597.4 1.9 pad_maximum_fusion.1
  600.6 2.7 convolution_convert_fusion.8.refs_1_
  603.3 5.4 convolution_convert_fusion.1.refs_2_
  608.7 4.4 convolution_convert_fusion.refs_3_
  613.1 2.7 fusion.68
  618.3 4.3 convolution_convert_fusion.2.refs_0_
  622.6 81.2 %shard_map.162 = (f32[24,2304]{1,0:T(8,128)}, f32[24,768]{1,0:T(8,128)}, f32[24,3072]{1,0:T(8,128)}, f32[96,768]{1,0:T(8,128)}) custom-call(bf16[768,2304]{1,0:T(8,128)(2,1)} %convolution_convert_fusion.2.refs_0_, bf16[768,768]{1,0:T(8,128)(2,1)} %convolution_convert_fusion.8.refs_1_, bf16[768,3072]{1,0:T(8,128)(2,1)} %convolution_convert_fusion.1.refs_2_, ...), custom_call_target="tpu_custom_call" | custom-call | tf_op jit(solution)/shard_map/pallas_call | solution.py:715
  703.8 1.5 convolution_convert_fusion.9.refs_1_
  705.3 4.0 convolution_convert_fusion.4.refs_2_
  709.3 4.5 convolution_convert_fusion.3.refs_3_
  713.8 2.0 fusion.70
  715.9 3.5 fusion.82
  719.5 3.1 convolution_convert_fusion.5.refs_0_
  723.2 41.0 %all-reduce = f32[8,768]{1,0:T(8,128)S(1)} all-reduce(f32[8,768]{1,0:T(8,128)S(1)} %stack.87), channel_id=4, replica_groups=mesh['rows'=8,'kv'=4] {'rows','kv'}, use_global_device_ids=true, to_apply=%region_34.35.clone | all-reduce | flops 6144 | bytes 49152
  766.6 79.7 %shard_map.161 = (f32[24,2304]{1,0:T(8,128)}, f32[24,768]{1,0:T(8,128)}, f32[24,3072]{1,0:T(8,128)}, f32[96,768]{1,0:T(8,128)}) custom-call(bf16[768,2304]{1,0:T(8,128)(2,1)} %convolution_convert_fusion.5.refs_0_, bf16[768,768]{1,0:T(8,128)(2,1)} %convolution_convert_fusion.9.refs_1_, bf16[768,3072]{1,0:T(8,128)(2,1)} %convolution_convert_fusion.4.refs_2_, ...), custom_call_target="tpu_custom_call" | custom-call | tf_op jit(solution)/shard_map/pallas_call | solution.py:715
  846.4 1.7 pad_maximum_fusion.10
  848.1 1.6 pad_maximum_fusion.11
  849.7 1.8 pad_maximum_fusion.8
  851.5 1.8 pad_maximum_fusion.9
  (243 shorter events, 27.0 us)
Async XLA Ops:
  7.2 217.8 %copy-start.2 = (bf16[1,256,768]{2,1,0:T(8,128)(2,1)S(1)}, bf16[1,256,768]{2,1,0:T(8,128)(2,1)}, u32[]{:S(2)}) copy-start(bf16[1,256,768]{2,1,0:T(8,128)(2,1)} %param.9) | copy-start | bytes 1179652
  7.2 293.0 %all-gather.4.cloned.1.call-start = ((), (), s32[]{:S(2)}) async-start(), calls=%async_computation.2 | async-start | bytes 3932160 | tf_op jit(solution)/shard_map/all_gather | solution.py:763
  85.9 142.3 %copy-start.48 = (f32[256]{0:T(256)}, f32[256]{0:T(256)S(1)}, u32[]{:S(2)}) copy-start(f32[256]{0:T(256)S(1)} %broadcast_multiply_fusion.3) | copy-start | bytes 3076
  87.2 141.0 %copy-start.50 = (f32[256]{0:T(256)}, f32[256]{0:T(256)S(1)}, u32[]{:S(2)}) copy-start(f32[256]{0:T(256)S(1)} %fusion.81) | copy-start | bytes 3076
  87.2 141.0 %copy-start.46 = (f32[256]{0:T(256)}, f32[256]{0:T(256)S(1)}, u32[]{:S(2)}) copy-start(f32[256]{0:T(256)S(1)} %fusion.116) | copy-start | bytes 3076
  87.2 141.0 %copy-start.37 = (f32[768]{0:T(1024)}, f32[768]{0:T(1024)S(1)}, u32[]{:S(2)}) copy-start(f32[768]{0:T(1024)S(1)} %get-tuple-element.102) | copy-start | bytes 9220
  87.3 141.0 %copy-start.39 = (f32[768]{0:T(1024)}, f32[768]{0:T(1024)S(1)}, u32[]{:S(2)}) copy-start(f32[768]{0:T(1024)S(1)} %get-tuple-element.56) | copy-start | bytes 9220
  87.3 260.6 %copy-start.41 = (f32[768]{0:T(1024)}, f32[768]{0:T(1024)S(1)}, u32[]{:S(2)}) copy-start(f32[768]{0:T(1024)S(1)} %get-tuple-element.55) | copy-start | bytes 9220
  229.2 188.9 %all-gather.6.cloned.1.call-start = ((), (), s32[]{:S(2)}) async-start(), calls=%async_computation.3 | async-start | bytes 3932160 | tf_op jit(solution)/shard_map/all_gather | solution.py:763
  230.2 78.8 %copy-start.13 = (bf16[1,256,768]{1,2,0:T(8,128)(2,1)}, bf16[1,256,768]{1,2,0:T(8,128)(2,1)S(1)}, u32[]{:S(2)}) copy-start(bf16[1,256,768]{1,2,0:T(8,128)(2,1)S(1)} %copy.54) | copy-start | bytes 1179652
  231.8 120.1 %copy-start.43 = (f32[768]{0:T(1024)}, f32[768]{0:T(1024)S(1)}, u32[]{:S(2)}) copy-start(f32[768]{0:T(1024)S(1)} %get-tuple-element.52) | copy-start | bytes 9220
  233.2 75.9 %copy-start.30 = (f32[256,1024]{1,0:T(8,128)}, f32[256,1024]{1,0:T(8,128)S(1)}, u32[]{:S(2)}) copy-start(f32[256,1024]{1,0:T(8,128)S(1)} %select_multiply_fusion) | copy-start | bytes 3145732
  305.9 34.9 %copy-start.4 = (bf16[1024,768]{0,1:T(8,128)(2,1)}, bf16[1024,768]{0,1:T(8,128)(2,1)S(1)}, u32[]{:S(2)}) copy-start(bf16[1024,768]{0,1:T(8,128)(2,1)S(1)} %copy.53) | copy-start | bytes 4718596
  340.7 6.3 copy-start.1
  340.7 7.2 slice-start.9
  340.8 6.3 copy-start.7
  340.8 7.1 slice-start.10
  347.1 2.4 slice-start.13
  349.6 3.0 copy-start.52
  355.7 188.6 %reduce-scatter.4.cloned.1.call-start = ((), (), s32[]{:S(2)}) async-start(), calls=%async_computation.4 | async-start | bytes 3932160 | tf_op jit(solution)/shard_map/reduce_scatter | solution.py:839
  357.0 70.3 %copy-start.14 = (bf16[1,256,768]{1,2,0:T(8,128)(2,1)}, bf16[1,256,768]{1,2,0:T(8,128)(2,1)S(1)}, u32[]{:S(2)}) copy-start(bf16[1,256,768]{1,2,0:T(8,128)(2,1)S(1)} %copy.57) | copy-start | bytes 1179652
  421.8 5.6 copy-start.35
  438.1 8.2 slice-start.17
  438.1 7.3 copy-start.9
  438.1 8.2 slice-start.18
  445.5 2.4 copy-start.28
  445.5 2.4 slice-start.5
  447.8 4.5 copy-start.57
  459.0 6.4 copy-start.21
  459.0 6.4 copy-start.32
  459.0 15.6 %slice-start.2 = ((s8[12582912]{0:T(1024)(128)(4,1)}), s8[4194304]{0:T(1024)(128)(4,1)S(1)}, s32[]{:S(2)}) async-start(s8[12582912]{0:T(1024)(128)(4,1)} %bitcast.238), calls=%async_computation.8 | async-start | bytes 8388608
  459.0 15.6 %slice-start.3 = ((s8[12582912]{0:T(1024)(128)(4,1)}), s8[4194304]{0:T(1024)(128)(4,1)S(1)}, s32[]{:S(2)}) async-start(s8[12582912]{0:T(1024)(128)(4,1)} %bitcast.238), calls=%async_computation.9 | async-start | bytes 8388608
  465.4 9.3 %slice-start.4 = ((s8[12582912]{0:T(1024)(128)(4,1)}), s8[4194304]{0:T(1024)(128)(4,1)S(1)}, s32[]{:S(2)}) async-start(s8[12582912]{0:T(1024)(128)(4,1)} %bitcast.238), calls=%async_computation.10 | async-start | bytes 8388608
  474.6 5.9 copy-start.15
  480.6 2.7 copy-start
  485.3 230.6 %reduce-scatter.6.cloned.1.call-start = ((), (), s32[]{:S(2)}) async-start(), calls=%async_computation.5 | async-start | bytes 3932160 | tf_op jit(solution)/shard_map/reduce_scatter | solution.py:839
  544.3 5.0 slice-start.15
  544.3 4.7 copy-start.23
  544.3 5.0 slice-start.16
  544.3 9.5 %slice-start.11 = ((s8[4718592]{0:T(1024)(128)(4,1)}), s8[4194304]{0:T(1024)(128)(4,1)S(1)}, s32[]{:S(2)}) async-start(s8[4718592]{0:T(1024)(128)(4,1)} %bitcast.304), calls=%async_computation.17 | async-start | bytes 8388608
  548.2 2.5 copy-start.55
  550.7 5.2 copy-start.17
  550.7 3.2 slice-start.12
  593.1 4.2 copy-start.5
  603.3 5.4 copy-start.24
  603.3 5.4 copy-start.58
  603.3 9.8 %slice-start.7 = ((s8[4718592]{0:T(1024)(128)(4,1)}), s8[4194304]{0:T(1024)(128)(4,1)S(1)}, s32[]{:S(2)}) async-start(s8[4718592]{0:T(1024)(128)(4,1)} %bitcast.300), calls=%async_computation.13 | async-start | bytes 8388608
  608.7 4.4 slice-start.8
  613.1 5.2 copy-start.44
  622.6 81.2 %copy-start.11 = (bf16[12,64,256]{2,1,0:T(8,128)(2,1)S(1)}, bf16[12,64,256]{2,1,0:T(8,128)(2,1)}, u32[]{:S(2)}) copy-start(bf16[12,64,256]{2,1,0:T(8,128)(2,1)} %copy-done.10) | copy-start | bytes 1179652
  622.6 82.7 %copy-start.42 = (f32[768]{0:T(1024)S(1)}, f32[768]{0:T(1024)}, u32[]{:S(2)}) copy-start(f32[768]{0:T(1024)} %copy-done.41) | copy-start | bytes 9220
  705.3 4.0 copy-start.18
  705.3 4.0 copy-start.56
  705.3 8.4 slice-start
  709.3 4.5 slice-start.1
  709.3 4.5 copy-start.6
  715.9 3.6 copy-start.31
  715.9 3.6 copy-start.40
  715.9 3.6 copy-start.47
  719.5 3.1 copy-start.51
  766.6 79.8 %copy-start.36 = (f32[24,2304]{1,0:T(8,128)S(1)}, f32[24,2304]{1,0:T(8,128)}, u32[]{:S(2)}) copy-start(f32[24,2304]{1,0:T(8,128)} %get-tuple-element.34) | copy-start | bytes 663556
  766.6 81.5 %copy-start.45 = (f32[24,768]{1,0:T(8,128)S(1)}, f32[24,768]{1,0:T(8,128)}, u32[]{:S(2)}) copy-start(f32[24,768]{1,0:T(8,128)} %get-tuple-element.36) | copy-start | bytes 221188
  766.6 83.1 %copy-start.34 = (f32[24,3072]{1,0:T(8,128)S(1)}, f32[24,3072]{1,0:T(8,128)}, u32[]{:S(2)}) copy-start(f32[24,3072]{1,0:T(8,128)} %get-tuple-element.38) | copy-start | bytes 884740
  766.6 84.9 %copy-start.33 = (f32[96,768]{1,0:T(8,128)S(1)}, f32[96,768]{1,0:T(8,128)}, u32[]{:S(2)}) copy-start(f32[96,768]{1,0:T(8,128)} %get-tuple-element.40) | copy-start | bytes 884740
  (18 other events, 27.8 us)
Sparse Core Ops, SparseCore 0:
  229.3 70.8 all-gather.3
  355.9 62.1 all-gather.5
  485.4 58.8 reduce-scatter.3
  599.5 68.2 reduce-scatter.5

commit v2 on v0

--- a/solution.py
+++ b/solution.py
@@ -3,6 +3,8 @@
 import jax
 import jax.numpy as jnp
 from jax import lax
+from jax.experimental import pallas as pl
+from jax.experimental.pallas import tpu as pltpu
 from jax.sharding import PartitionSpec as P
 
 HEADS = 12
@@ -162,7 +164,7 @@
     return results + (norm_parts[0], norm_parts[1])
 
 
-def local(tokens, lengths, w_qkv, w_out, w_up, w_down, gains, biases, cotangent):
+def local_generic(tokens, lengths, w_qkv, w_out, w_up, w_down, gains, biases, cotangent):
     rows_here, slot_dev, model_width = tokens.shape
     slot_count = slot_dev * lax.axis_size("kv")
     first_slot = lax.axis_index("kv") * slot_dev
@@ -315,6 +317,1271 @@
     )
 
 
+F32 = jnp.float32
+BF16 = jnp.bfloat16
+MESH = pl.DeviceIdType.MESH
+ZN = 4
+
+
+def flip(value, unit):
+    bit = lax.rem(lax.div(value, unit), 2)
+    return value + unit - 2 * unit * bit
+
+
+def places_of():
+    r = lax.axis_index("rows")
+    z = lax.axis_index("kv")
+    return r, z, flip(r, 2), flip(r, 4), flip(flip(r, 2), 4), flip(r, 1)
+
+
+def turn(z, k):
+    return lax.rem(z + k, ZN)
+
+
+def rcopy(src, dst, ssem, rsem, device):
+    return pltpu.make_async_remote_copy(
+        src_ref=src, dst_ref=dst, send_sem=ssem, recv_sem=rsem, device_id=device, device_id_type=MESH
+    )
+
+
+def band(start, size):
+    return pl.ds(pl.multiple_of(start, 16), size)
+
+
+def greet(peers):
+    barrier = pltpu.get_barrier_semaphore()
+    for peer in peers:
+        pl.semaphore_signal(barrier, inc=1, device_id=peer, device_id_type=MESH)
+    pl.semaphore_wait(barrier, len(peers))
+
+
+def comm_peers():
+    r, z, rx, ry, rd, rc = places_of()
+    return [(r, turn(z, 1)), (r, turn(z, 2)), (r, turn(z, 3)), (rx, z), (ry, z), (rc, z)]
+
+
+def col_step(width):
+    return 256 if width % 256 == 0 else 128
+
+
+class Gather:
+    SEMS = 14
+
+    def __init__(self, own, whole, zm, zt, ssem, rsem, base):
+        self.own, self.whole, self.zm, self.zt = own, whole, zm, zt
+        self.ssem, self.rsem, self.base = ssem, rsem, base
+        self.split = zm is not None
+        self.rows = whole.shape[0] // 8
+        self.width = whole.shape[1]
+        self.sent = []
+
+    def _copy(self, src, dst, at, device):
+        return rcopy(src, dst, self.ssem.at[self.base + at], self.rsem.at[self.base + at], device)
+
+    def _block(self, r, half=None):
+        if half is None:
+            return self.whole.at[band(r * self.rows, self.rows), :]
+        part = self.rows // 2
+        return self.whole.at[band(r * self.rows + half * part, part), :]
+
+    def _send(self, src, dst, at, device):
+        copy = self._copy(src, dst, at, device)
+        copy.start()
+        self.sent.append(copy)
+
+    def prepare(self):
+        r, z = places_of()[:2]
+        if self.split:
+            half = self.width // 2
+            own = self.own[...].astype(F32)
+            self.zm[pl.ds(z, 1)] = own[:16].astype(BF16)[None]
+            self.zt[pl.ds(z, 1)] = jnp.concatenate([own[16:, :half], own[16:, half:]], 0).astype(BF16)[None]
+        else:
+            part = self.rows // ZN
+            self.whole[band(r * self.rows + z * part, part), :] = self.own[...]
+
+    def _zrefs(self, z):
+        if self.split:
+            return [self.zm.at[z], self.zt.at[z]]
+        part = self.rows // ZN
+        return [self.whole.at[band(places_of()[0] * self.rows + z * part, part), :]]
+
+    def send_z(self):
+        r, z = places_of()[:2]
+        for k in (1, 2, 3):
+            for i, ref in enumerate(self._zrefs(z)):
+                self._send(ref, ref, 2 * (k - 1) + i, (r, turn(z, k)))
+
+    def wait_z(self):
+        r, z = places_of()[:2]
+        for k in (1, 2, 3):
+            for i, ref in enumerate(self._zrefs(turn(z, ZN - k))):
+                self._copy(ref, ref, 2 * (k - 1) + i, (r, turn(z, ZN - k))).wait_recv()
+        if self.split:
+            half = self.width // 2
+            step = col_step(half)
+            for side in (0, 1):
+                def assemble(i, carry, side=side):
+                    at = pl.multiple_of(i * step, step)
+                    here = pl.ds(pl.multiple_of(side * half + i * step, 128), step)
+                    parts = []
+                    for piece in range(ZN):
+                        parts.append(self.zm[piece, :, here].astype(F32))
+                        parts.append(self.zt[piece, :, pl.ds(at, step)].astype(F32)[8 * side : 8 * side + 8])
+                    self.whole[band(r * self.rows, self.rows), here] = jnp.concatenate(parts, 0).astype(BF16)
+                    return carry
+                lax.fori_loop(0, half // step, assemble, 0)
+
+    def send_plane(self):
+        r, z, rx, ry, rd, rc = places_of()
+        own = self._block(r)
+        self._send(own, own, 6, (rx, z))
+        self._send(own, own, 7, (ry, z))
+        self._send(own, own, 10, (rc, z))
+
+    def forward(self):
+        r, z, rx, ry, rd, rc = places_of()
+        first, second = self._block(rx), self._block(ry)
+        self._copy(first, first, 6, (rx, z)).wait_recv()
+        part = self._block(rx, 0)
+        self._send(part, part, 8, (ry, z))
+        self._send(first, first, 11, (rc, z))
+        self._copy(second, second, 7, (ry, z)).wait_recv()
+        part = self._block(ry, 1)
+        self._send(part, part, 9, (rx, z))
+        self._send(second, second, 12, (rc, z))
+
+    def forward_last(self):
+        r, z, rx, ry, rd, rc = places_of()
+        part = self._block(rd, 0)
+        self._copy(part, part, 8, (ry, z)).wait_recv()
+        part = self._block(rd, 1)
+        self._copy(part, part, 9, (rx, z)).wait_recv()
+        diagonal = self._block(rd)
+        self._send(diagonal, diagonal, 13, (rc, z))
+
+    def finish(self):
+        r, z, rx, ry, rd, rc = places_of()
+        for at, block in ((10, r), (11, rx), (12, ry), (13, rd)):
+            ref = self._block(flip(block, 1))
+            self._copy(ref, ref, at, (rc, z)).wait_recv()
+
+    def drain(self):
+        for copy in self.sent:
+            copy.wait_send()
+
+
+def add_rows(dst, src, rows):
+    def step(i, carry):
+        here = band(i * 16, 16)
+        dst[here, :] = (dst[here, :].astype(F32) + src[here, :].astype(F32)).astype(BF16)
+        return carry
+    lax.fori_loop(0, rows // 16, step, 0)
+
+
+GROUP = 640
+TOK = 256
+WIDE = 256
+
+
+def dot(a, b):
+    return jnp.dot(a, b, preferred_element_type=F32)
+
+
+def dot_nt(a, b):
+    return lax.dot_general(a, b, (((1,), (1,)), ((), ())), preferred_element_type=F32)
+
+
+def dot_tn(a, b):
+    return lax.dot_general(a, b, (((0,), (0,)), ((), ())), preferred_element_type=F32)
+
+
+def loop(count, body):
+    def step(i, carry):
+        body(i)
+        return carry
+    lax.fori_loop(0, count, step, 0)
+
+
+def cols(i, size):
+    return pl.ds(pl.multiple_of(i * size, 128), size)
+
+
+class Spot:
+    def __init__(self):
+        self.r, self.z, self.rx, self.ry, self.rd, self.rc = places_of()
+        self.c = lax.rem(self.r, 2)
+        self.member = 2 * self.c + lax.rem(self.z, 2)
+        self.swaps = (self.c + lax.div(self.z, 2)) == 1
+        self.partner = (self.rc, flip(self.z, 2))
+
+    def mate(self, k):
+        r = self.rc if k >= 2 else self.r
+        z = flip(self.z, 1) if k % 2 else self.z
+        return (r, z), 2 * lax.rem(r, 2) + lax.rem(z, 2)
+
+    def device(self, member):
+        return (self.r - self.c + lax.div(member, 2), self.z - lax.rem(self.z, 2) + lax.rem(member, 2))
+
+    def peers(self):
+        return comm_peers() + [(self.rc, flip(self.z, 1)), self.partner]
+
+
+def swap(spot, src, dst, ssem, rsem):
+    @pl.when(spot.swaps)
+    def _():
+        rcopy(src, dst, ssem, rsem, spot.partner).start()
+
+    @pl.when(jnp.logical_not(spot.swaps))
+    def _():
+        pltpu.make_async_copy(src, dst, rsem).start()
+
+
+def swap_wait(spot, src, dst, ssem, rsem):
+    @pl.when(spot.swaps)
+    def _():
+        rcopy(src, dst, ssem, rsem, spot.partner).wait()
+
+    @pl.when(jnp.logical_not(spot.swaps))
+    def _():
+        pltpu.make_async_copy(src, dst, rsem).wait()
+
+
+def starts_of(lens, i):
+    places = lax.broadcasted_iota(jnp.int32, (1, TOK), 1) + i * TOK
+    end = jnp.zeros((1, 1), jnp.int32)
+    start = jnp.zeros((1, TOK), jnp.int32)
+    for n in range(4):
+        end = end + lens[0:1, n : n + 1]
+        start = jnp.maximum(start, jnp.where(end <= places, end, 0))
+    live = places < end
+    return places, jnp.where(live, start, 1 << 20), live
+
+
+def live_column(lens, spot, rows, first):
+    places = lax.broadcasted_iota(jnp.int32, (rows, 1), 0) + spot.member * TOK + first
+    end = lens[0:1, 0:1] + lens[0:1, 1:2] + lens[0:1, 2:3] + lens[0:1, 3:4]
+    return (places < end).astype(F32)
+
+
+def centred(value):
+    center = value - jnp.mean(value, -1, keepdims=True)
+    spread = jnp.mean(center * center, -1, keepdims=True)
+    return center * lax.rsqrt(spread + EPSILON)
+
+
+CHUNK = 64
+
+
+def allowed_rows(first, rows, places, start):
+    keys = lax.broadcasted_iota(jnp.int32, (rows, TOK), 0) + first
+    return (keys >= start) & (keys <= places)
+
+
+def fold_rows(value, op):
+    rows = value.shape[0]
+    parts = [value[8 * n : 8 * n + 8] for n in range(rows // 8)]
+    while len(parts) > 1:
+        parts = [op(parts[n], parts[n + 1]) if n + 1 < len(parts) else parts[n] for n in range(0, len(parts), 2)]
+    return parts[0]
+
+
+def head_lanes(shape, h, offset):
+    lanes = lax.broadcasted_iota(jnp.int32, shape, 1)
+    return lax.div(lanes, HEAD) == h + offset
+
+
+def ceiling_of(s_ref, count, places, start, signed):
+    def step(n, top):
+        here = pl.ds(pl.multiple_of(n * CHUNK, CHUNK), CHUNK)
+        s = s_ref[here, :]
+        value = s * s if signed else s
+        value = jnp.where(allowed_rows(n * CHUNK, CHUNK, places, start), value, 0.0 if signed else -10000.0)
+        return jnp.maximum(top, fold_rows(value, jnp.maximum))
+    first = -1.0 if signed else -10000.0
+    top = lax.fori_loop(0, count, step, jnp.full((8, TOK), first, F32))
+    return jnp.max(top, 0, keepdims=True)
+
+
+def attend_quarter(i, lens, qkv, vt, s_ref, p_ref, o_ref, signed):
+    places, start, live = starts_of(lens, i)
+    queries = qkv[i, :, 0:WIDE].astype(F32)
+    keys_len = TOK * (i + 1)
+
+    def head(h):
+        mine = jnp.where(head_lanes((TOK, WIDE), h, 0), queries * 0.125, 0.0).astype(BF16)
+
+        def score(j):
+            s_ref[pl.ds(pl.multiple_of(j * TOK, TOK), TOK), :] = dot_nt(qkv[j, :, 384:640], mine)
+        loop(i + 1, score)
+        top = ceiling_of(s_ref, keys_len // CHUNK, places, start, signed)
+        if signed:
+            top = jnp.where(top < 0.0, 0.0, jnp.sqrt(jnp.maximum(top, 0.0) + 1.0))
+
+        def weigh(n, total):
+            here = pl.ds(pl.multiple_of(n * CHUNK, CHUNK), CHUNK)
+            s = s_ref[here, :]
+            okay = allowed_rows(n * CHUNK, CHUNK, places, start)
+            if signed:
+                shifted = jnp.sqrt(s * s + 1.0) - top
+            else:
+                shifted = s - top
+            raised = jnp.where(okay, jnp.exp(jnp.where(okay, shifted, -60.0)), 0.0)
+            weights = jnp.tanh(s) * raised if signed else raised
+            p_ref[here, :] = weights.astype(BF16)
+            return total + fold_rows(raised, jnp.add)
+        total = lax.fori_loop(0, keys_len // CHUNK, weigh, jnp.zeros((8, TOK), F32))
+        normaliser = jnp.sum(total, 0, keepdims=True) + (1.0 - live.astype(F32))
+        outcome = dot(vt[pl.ds(pl.multiple_of(HEAD + HEAD * h, HEAD), HEAD), 0:keys_len], p_ref[0:keys_len, :])
+        o_ref[i, pl.ds(pl.multiple_of(HEAD * h, HEAD), HEAD), :] = (outcome / normaliser).astype(BF16)
+    loop(HEADS // 4, head)
+
+
+class Keep:
+    def __init__(self, src, dst, sem):
+        self.copy = pltpu.make_async_copy(src, dst, sem)
+        self.copy.start()
+        self.open = True
+
+    def wait(self):
+        if self.open:
+            self.copy.wait()
+        self.open = False
+
+
+class Pump:
+    def __init__(self, jobs):
+        self.steps = []
+        self.done = set()
+        count = len(jobs)
+        ahead = 2
+
+        def zstep(n):
+            def run():
+                jobs[n].wait_z()
+                jobs[n].send_plane()
+                if n + ahead < count:
+                    jobs[n + ahead].send_z()
+            return run
+        for n in range(count + 2):
+            if n < count:
+                self.steps.append((("z", n), zstep(n)))
+            if 0 <= n - 1 < count:
+                self.steps.append((("f", n - 1), jobs[n - 1].forward))
+            if 0 <= n - 2 < count:
+                self.steps.append((("l", n - 2), jobs[n - 2].forward_last))
+        self.jobs = jobs
+
+    def __call__(self, n=1):
+        for _ in range(n):
+            if self.steps:
+                name, run = self.steps.pop(0)
+                run()
+                self.done.add(name)
+
+    def need(self, n):
+        while ("l", n) not in self.done:
+            self()
+        self.jobs[n].finish()
+
+
+STASH = ("stream", "qkv", "middle", "nin_t", "att_t", "nmid_t", "pre", "act_t")
+
+
+def stash_shapes(d, ff):
+    return [
+        ((TOK, d), F32),
+        ((4, TOK, GROUP), BF16),
+        ((TOK, d), F32),
+        ((d, TOK), BF16),
+        ((d, TOK), BF16),
+        ((d, TOK), BF16),
+        ((TOK, ff), F32),
+        ((ff, TOK), BF16),
+    ]
+
+
+def forward_kernel(*refs):
+    refs = list(refs)
+    take = lambda n: [refs.pop(0) for _ in range(n)]
+    tok, cot, lens_in = take(3)
+    owns = take(8)
+    result_o, cot_o, lens_o, norms_o = take(4)
+    whole_o = take(8)
+    stash_o = [take(8), take(8)]
+    wholes = take(8)
+    zbuf = [(None, None) if n % 4 == 3 else tuple(take(2)) for n in range(8)]
+    tok_v, lens_v, stream, normed, qkv_s, qkv0, qkv1, vt, s_ref, p_ref, o_ref, att0, att1, pre, act, act_t, nt_in, nt_mid, middle, res = take(20)
+    ssem, rsem, osem, stsem, qs, qr, os_, or_, ms, mr = take(10)
+    spot = Spot()
+    greet(spot.peers())
+    jobs = [Gather(owns[n], wholes[n], zbuf[n][0], zbuf[n][1], ssem, rsem, n * Gather.SEMS) for n in range(8)]
+    jobs[0].prepare()
+    jobs[0].send_z()
+    swap(spot, tok, tok_v, ms.at[0], mr.at[0])
+    swap(spot, lens_in, lens_v, ms.at[1], mr.at[1])
+    for job in jobs[1:]:
+        job.prepare()
+    jobs[1].send_z()
+    swap(spot, cot, cot_o, ms.at[2], mr.at[2])
+    pump = Pump(jobs)
+    stores = []
+
+    def keep(src, dst, sem):
+        stores.append(Keep(src, dst, sem))
+        return stores[-1]
+
+    swap_wait(spot, tok, tok_v, ms.at[0], mr.at[0])
+    swap_wait(spot, lens_in, lens_v, ms.at[1], mr.at[1])
+    lens_o[...] = lens_v[...]
+    pump(2)
+
+    def widen(n):
+        here = band(n * CHUNK, CHUNK)
+        stream[here, :] = tok_v[here, :].astype(F32)
+    loop(TOK // CHUNK, widen)
+
+    stream_store = keep(stream, stash_o[0][0], stsem.at[0])
+    previous = None
+    for layer in range(LAYERS):
+        w_qkv, w_out, w_up, w_down = wholes[4 * layer : 4 * layer + 4]
+        qkv = (qkv0, qkv1)[layer]
+        att = (att0, att1)[layer]
+        out = stash_o[layer]
+        base = 8 * layer
+        signed = layer == 0
+        pump.need(4 * layer)
+        keep(w_qkv, whole_o[4 * layer], osem.at[4 * layer])
+        edge = w_qkv[:, 512:640].astype(F32).T
+        norms_o[layer] = edge[HEAD : HEAD + 8]
+        if previous:
+            previous[3].wait()
+
+        def first_norm(n):
+            here = band(n * CHUNK, CHUNK)
+            value = centred(stream[here, :]) * norms_o[layer, 0:1, :] + norms_o[layer, 1:2, :]
+            normed[here, :] = value.astype(BF16)
+        loop(TOK // CHUNK, first_norm)
+        for k in (1, 3, 2, 0):
+            mate, member = spot.mate(k)
+            group = dot(normed[...], w_qkv[:, pl.ds(pl.multiple_of(member * GROUP, 128), GROUP)]).astype(BF16)
+            if k:
+                qkv_s[layer, k - 1] = group
+                rcopy(qkv_s.at[layer, k - 1], qkv.at[spot.member], qs.at[4 * layer + k], qr.at[4 * layer + k], mate).start()
+            else:
+                qkv[pl.ds(spot.member, 1)] = group[None]
+        nt_in[...] = normed[...].astype(F32).T.astype(BF16)
+        kept = [None] * 8
+        kept[3] = keep(nt_in, out[3], stsem.at[base + 3])
+        pump(2)
+        for k in (1, 3, 2):
+            mate, member = spot.mate(k)
+            rcopy(qkv_s.at[layer, k - 1], qkv.at[member], qs.at[4 * layer + k], qr.at[4 * layer + k], mate).wait_recv()
+        kept[1] = keep(qkv, out[1], stsem.at[base + 1])
+
+        def turn_values(j):
+            vt[:, cols(j, TOK)] = qkv[j, :, 128:384].astype(F32).T.astype(BF16)
+        loop(4, turn_values)
+        for i in range(4):
+            attend_quarter(i, lens_v, qkv, vt, s_ref, p_ref, o_ref.at[layer], signed)
+
+            @pl.when(spot.member != i)
+            def _():
+                rcopy(
+                    o_ref.at[layer, i],
+                    att.at[band(spot.member * 192, 192), :],
+                    os_.at[4 * layer + i],
+                    or_.at[4 * layer + spot.member],
+                    spot.device(i),
+                ).start()
+
+            @pl.when(spot.member == i)
+            def _():
+                att[i * 192 : (i + 1) * 192, :] = o_ref[layer, i]
+            pump(1)
+        pump.need(4 * layer + 1)
+        keep(w_out, whole_o[4 * layer + 1], osem.at[4 * layer + 1])
+        for i in range(4):
+            @pl.when(spot.member != i)
+            def _():
+                ref = att.at[i * 192 : (i + 1) * 192, :]
+                rcopy(ref, ref, os_.at[4 * layer + i], or_.at[4 * layer + i], spot.device(i)).wait_recv()
+        kept[4] = keep(att, out[4], stsem.at[base + 4])
+        if previous:
+            previous[2].wait()
+        middle[...] = stream[...] + dot_tn(att[...], w_out[...])
+        kept[2] = keep(middle, out[2], stsem.at[base + 2])
+        if previous:
+            previous[5].wait()
+
+        def second_norm(n):
+            here = band(n * CHUNK, CHUNK)
+            value = centred(middle[here, :]) * norms_o[layer, 2:3, :] + norms_o[layer, 3:4, :]
+            normed[here, :] = value.astype(BF16)
+        loop(TOK // CHUNK, second_norm)
+        nt_mid[...] = normed[...].astype(F32).T.astype(BF16)
+        kept[5] = keep(nt_mid, out[5], stsem.at[base + 5])
+        pump.need(4 * layer + 2)
+        keep(w_up, whole_o[4 * layer + 2], osem.at[4 * layer + 2])
+        if previous:
+            previous[6].wait()
+            previous[7].wait()
+        tile = 512
+
+        def up(n):
+            value = dot(normed[...], w_up[:, cols(n, tile)])
+            pre[:, cols(n, tile)] = value
+            active = jax.nn.gelu(value)
+            act[:, cols(n, tile)] = active.astype(BF16)
+            act_t[pl.ds(pl.multiple_of(n * tile, tile), tile), :] = active.T.astype(BF16)
+        loop(w_up.shape[1] // tile, up)
+        kept[6] = keep(pre, out[6], stsem.at[base + 6])
+        kept[7] = keep(act_t, out[7], stsem.at[base + 7])
+        pump(1)
+        pump.need(4 * layer + 3)
+        keep(w_down, whole_o[4 * layer + 3], osem.at[4 * layer + 3])
+        if previous:
+            previous[0].wait()
+        else:
+            stream_store.wait()
+
+        def down(n):
+            here = cols(n, 256)
+            stream[:, here] = middle[:, here] + dot(act[...], w_down[:, here])
+        loop(3, down)
+        if layer == 0:
+            kept[0] = keep(stream, stash_o[1][0], stsem.at[8])
+        previous = kept
+
+    def last(n):
+        here = band(n * CHUNK, CHUNK)
+        res[here, :] = (stream[here, :] * live_column(lens_v, spot, CHUNK, n * CHUNK)).astype(BF16)
+    loop(TOK // CHUNK, last)
+    swap(spot, res, result_o, ms.at[3], mr.at[3])
+    for job in jobs:
+        job.drain()
+    for layer in range(LAYERS):
+        qkv = (qkv0, qkv1)[layer]
+        att = (att0, att1)[layer]
+        for k in (1, 3, 2):
+            mate, member = spot.mate(k)
+            rcopy(qkv_s.at[layer, k - 1], qkv.at[spot.member], qs.at[4 * layer + k], qr.at[4 * layer + k], mate).wait_send()
+        for i in range(4):
+            @pl.when(spot.member != i)
+            def _():
+                rcopy(
+                    o_ref.at[layer, i],
+                    att.at[band(spot.member * 192, 192), :],
+                    os_.at[4 * layer + i],
+                    or_.at[4 * layer + spot.member],
+                    spot.device(i),
+                ).wait_send()
+    for store in stores:
+        store.wait()
+    swap_wait(spot, cot, cot_o, ms.at[2], mr.at[2])
+    swap_wait(spot, res, result_o, ms.at[3], mr.at[3])
+
+
+def forward_call(tok, cot, lens, owns):
+    d, ff = tok.shape[1], owns[2].shape[1]
+    shapes = [(own.shape[0] * 32, own.shape[1]) for own in owns]
+    zshapes = []
+    for n, own in enumerate(owns):
+        if n % 4 != 3:
+            zshapes += [pltpu.VMEM((ZN, 16, own.shape[1]), BF16), pltpu.VMEM((ZN, 16, own.shape[1] // 2), BF16)]
+    any_space = pl.BlockSpec(memory_space=pl.ANY)
+    vmem = pl.BlockSpec(memory_space=pltpu.VMEM)
+    stash = [jax.ShapeDtypeStruct(shape, kind) for shape, kind in stash_shapes(d, ff)]
+    dma = lambda n: pltpu.SemaphoreType.DMA((n,))
+    outs = pl.pallas_call(
+        forward_kernel,
+        out_shape=[
+            jax.ShapeDtypeStruct((TOK, d), BF16),
+            jax.ShapeDtypeStruct((TOK, d), BF16),
+            jax.ShapeDtypeStruct((8, 128), jnp.int32),
+            jax.ShapeDtypeStruct((LAYERS, 8, d), F32),
+        ]
+        + [jax.ShapeDtypeStruct(shape, BF16) for shape in shapes]
+        + stash
+        + stash,
+        in_specs=[any_space, any_space] + [vmem] * 9,
+        out_specs=[any_space, any_space, vmem, vmem] + [any_space] * 24,
+        scratch_shapes=[pltpu.VMEM(shape, BF16) for shape in shapes]
+        + zshapes
+        + [
+            pltpu.VMEM((TOK, d), BF16),
+            pltpu.VMEM((8, 128), jnp.int32),
+            pltpu.VMEM((TOK, d), F32),
+            pltpu.VMEM((TOK, d), BF16),
+            pltpu.VMEM((LAYERS, 3, TOK, GROUP), BF16),
+            pltpu.VMEM((4, TOK, GROUP), BF16),
+            pltpu.VMEM((4, TOK, GROUP), BF16),
+            pltpu.VMEM((WIDE, 4 * TOK), BF16),
+            pltpu.VMEM((4 * TOK, TOK), F32),
+            pltpu.VMEM((4 * TOK, TOK), BF16),
+            pltpu.VMEM((LAYERS, 4, 192, TOK), BF16),
+            pltpu.VMEM((d, TOK), BF16),
+            pltpu.VMEM((d, TOK), BF16),
+            pltpu.VMEM((TOK, ff), F32),
+            pltpu.VMEM((TOK, ff), BF16),
+            pltpu.VMEM((ff, TOK), BF16),
+            pltpu.VMEM((d, TOK), BF16),
+            pltpu.VMEM((d, TOK), BF16),
+            pltpu.VMEM((TOK, d), F32),
+            pltpu.VMEM((TOK, d), BF16),
+        ]
+        + [dma(8 * Gather.SEMS), dma(8 * Gather.SEMS), dma(8), dma(16), dma(8), dma(8), dma(8), dma(8), dma(4), dma(4)],
+        compiler_params=pltpu.CompilerParams(collective_id=0, has_side_effects=True, vmem_limit_bytes=62 * 2**20),
+    )(tok, cot, lens, *owns)
+    return outs[:4], outs[4:12], (outs[12:20], outs[20:28])
+
+
+class Reduce:
+    SEMS = 14
+
+    def __init__(self, send, got, half, near, zs, zr, out, ssem, rsem, base):
+        self.send, self.got, self.half, self.near = send, got, half, near
+        self.zs, self.zr, self.out = zs, zr, out
+        self.ssem, self.rsem, self.base = ssem, rsem, base
+        self.rows, self.width = got.shape[1], got.shape[2]
+        self.split = len(zs) == 2
+        self.sent = []
+        self.core_sent = []
+
+    def _copy(self, src, dst, at, device):
+        return rcopy(src, dst, self.ssem.at[self.base + at], self.rsem.at[self.base + at], device)
+
+    def _send(self, src, dst, at, device):
+        copy = self._copy(src, dst, at, device)
+        copy.start()
+        self.sent.append(copy)
+
+    def send_core(self):
+        r, z, rx, ry, rd, rc = places_of()
+        for b in range(4):
+            copy = self._copy(self.send.at[b, :, pl.ds(0, self.width)], self.got.at[b], b, (rc, z))
+            copy.start()
+            self.core_sent.append(copy)
+
+    def free_send(self):
+        for copy in self.core_sent:
+            copy.wait_send()
+        self.core_sent = []
+
+    def wait_core(self):
+        r, z, rx, ry, rd, rc = places_of()
+        for b in range(4):
+            self._copy(self.got.at[b], self.got.at[b], b, (rc, z)).wait_recv()
+
+    def send_diagonal(self):
+        r, z, rx, ry, rd, rc = places_of()
+        part = self.rows // 2
+        diagonal = lax.div(rd, 2)
+        self._send(self.got.at[diagonal, pl.ds(0, part)], self.half.at[0], 4, (ry, z))
+        self._send(self.got.at[diagonal, pl.ds(part, part)], self.half.at[1], 5, (rx, z))
+
+    def send_near(self):
+        r, z, rx, ry, rd, rc = places_of()
+        part = self.rows // 2
+        for at, side, other in ((4, ry, rx), (5, rx, ry)):
+            i = at - 4
+            self._copy(self.half.at[i], self.half.at[i], at, (side, z)).wait_recv()
+            block = self.got.at[lax.div(other, 2)]
+            add_rows(block.at[pl.ds(i * part, part)], self.half.at[i], part)
+            self._send(block, self.near.at[i], 6 + i, (other, z))
+
+    def send_z(self):
+        r, z, rx, ry, rd, rc = places_of()
+        for i, side in ((0, rx), (1, ry)):
+            self._copy(self.near.at[i], self.near.at[i], 6 + i, (side, z)).wait_recv()
+        own = self.got.at[lax.div(r, 2)]
+        near = self.near
+
+        def total(rows, here):
+            return own[rows, here].astype(F32) + near[0, rows, here].astype(F32) + near[1, rows, here].astype(F32)
+
+        if self.split:
+            half = self.width // 2
+            step = col_step(half)
+
+            def cut(i):
+                at = pl.ds(pl.multiple_of(i * step, 128), step)
+                sums = [
+                    total(slice(None), pl.ds(pl.multiple_of(side * half + i * step, 128), step)) for side in (0, 1)
+                ]
+                for piece in range(ZN):
+                    for side in (0, 1):
+                        here = pl.ds(pl.multiple_of(side * half + i * step, 128), step)
+                        self.zs[0][piece, :, here] = sums[side][24 * piece : 24 * piece + 16].astype(BF16)
+                    self.zs[1][piece, :, at] = jnp.concatenate(
+                        [sums[side][24 * piece + 16 : 24 * piece + 24] for side in (0, 1)], 0
+                    ).astype(BF16)
+            loop(half // step, cut)
+        else:
+            part = self.rows // ZN
+            for piece in range(ZN):
+                def cut_rows(i, piece=piece):
+                    self.zs[0][piece, band(i * 16, 16), :] = total(band(piece * part + i * 16, 16), slice(None)).astype(BF16)
+                loop(part // 16, cut_rows)
+        for k in (1, 2, 3):
+            for i in range(len(self.zs)):
+                self._send(self.zs[i].at[turn(z, k)], self.zr[i].at[k - 1], 8 + 2 * (k - 1) + i, (r, turn(z, k)))
+
+    def finish(self):
+        r, z = places_of()[:2]
+        for k in (1, 2, 3):
+            for i in range(len(self.zs)):
+                ref = self.zr[i].at[k - 1]
+                self._copy(ref, ref, 8 + 2 * (k - 1) + i, (r, turn(z, ZN - k))).wait_recv()
+        if self.split:
+            half = self.width // 2
+            main = self.zs[0][z].astype(F32)
+            tail = self.zs[1][z].astype(F32)
+            for k in range(3):
+                main = main + self.zr[0][k].astype(F32)
+                tail = tail + self.zr[1][k].astype(F32)
+            self.out[pl.ds(0, 16), :] = main
+            self.out[pl.ds(16, 8), pl.ds(0, half)] = tail[:8]
+            self.out[pl.ds(16, 8), pl.ds(half, half)] = tail[8:]
+        else:
+            def total(i):
+                here = band(i * 16, 16)
+                value = self.zs[0][z, here, :].astype(F32)
+                for k in range(3):
+                    value = value + self.zr[0][k, here, :].astype(F32)
+                self.out[here, :] = value
+            loop(self.out.shape[0] // 16, total)
+
+    def drain(self):
+        self.free_send()
+        for copy in self.sent:
+            copy.wait_send()
+        self.sent = []
+
+
+class Line:
+    def __init__(self):
+        self.queue = []
+
+    def add(self, steps):
+        self.queue.append(list(steps))
+
+    def __call__(self, n=1):
+        for _ in range(n):
+            if self.queue:
+                steps = self.queue.pop(0)
+                steps.pop(0)()
+                if steps:
+                    self.queue.append(steps)
+
+    def flush(self):
+        while self.queue:
+            self()
+
+
+def left_rows(left, c):
+    return jnp.concatenate([left[band((2 * b + c) * 96, 96), :] for b in range(4)], 0)
+
+
+def norm_back(source, upstream, gain, add, out, low, sums):
+    sums[...] = jnp.zeros_like(sums)
+
+    def step(n):
+        here = band(n * CHUNK, CHUNK)
+        value = source[here, :]
+        center = value - jnp.mean(value, -1, keepdims=True)
+        scale = lax.rsqrt(jnp.mean(center * center, -1, keepdims=True) + EPSILON)
+        normal = center * scale
+        up = upstream[here, :]
+        sums[0:8, :] += fold_rows(up * normal, jnp.add)
+        sums[8:16, :] += fold_rows(up, jnp.add)
+        up = up * gain
+        inner = up - jnp.mean(up, -1, keepdims=True) - normal * jnp.mean(up * normal, -1, keepdims=True)
+        total = add[here, :] + inner * scale
+        out[here, :] = total
+        low[here, :] = total.astype(BF16)
+    loop(TOK // CHUNK, step)
+    gain_grad = jnp.sum(sums[0:8, :], 0, keepdims=True)
+    bias_grad = jnp.sum(sums[8:16, :], 0, keepdims=True)
+    return gain_grad, bias_grad
+
+
+def gelu_slope(x):
+    root = 0.7978845608028654
+    square = x * x
+    bend = jnp.tanh(root * (x + 0.044715 * x * square))
+    return 0.5 * (1.0 + bend) + 0.5 * x * (1.0 - bend * bend) * root * (1.0 + 3 * 0.044715 * square)
+
+
+def attend_quarter_back(i, lens, qkv, kt, datt, scratch, signed):
+    s_ref, dp_ref, e_ref, t_ref, p_ref, ds_ref, dk, dv, dq = scratch
+    places, start, live = starts_of(lens, i)
+    queries = qkv[i, :, 0:WIDE].astype(F32)
+    keys_len = TOK * (i + 1)
+    grads_t = jnp.concatenate([jnp.zeros((HEAD, TOK), F32), datt[i].astype(F32)], 0)
+    grads = grads_t.T
+    rows = lax.div(lax.broadcasted_iota(jnp.int32, (WIDE, TOK), 0), HEAD)
+
+    def head(h):
+        mine = jnp.where(head_lanes((TOK, WIDE), h, 0), queries * 0.125, 0.0).astype(BF16)
+        out_t = jnp.where(rows == h + 1, grads_t, 0.0).astype(BF16)
+        out = jnp.where(head_lanes((TOK, WIDE), h, 1), grads, 0.0).astype(BF16)
+
+        def score(j):
+            here = pl.ds(pl.multiple_of(j * TOK, TOK), TOK)
+            s_ref[here, :] = dot_nt(qkv[j, :, 384:640], mine)
+            dp_ref[here, :] = dot(qkv[j, :, 128:384], out_t)
+        loop(i + 1, score)
+        top = ceiling_of(s_ref, keys_len // CHUNK, places, start, signed)
+        if signed:
+            top = jnp.where(top < 0.0, 0.0, jnp.sqrt(jnp.maximum(top, 0.0) + 1.0))
+
+        def weigh(n, sums):
+            here = pl.ds(pl.multiple_of(n * CHUNK, CHUNK), CHUNK)
+            s = s_ref[here, :]
+            dp = dp_ref[here, :]
+            okay = allowed_rows(n * CHUNK, CHUNK, places, start)
+            if signed:
+                square = s * s + 1.0
+                back = lax.rsqrt(square)
+                shifted = square * back - top
+            else:
+                shifted = s - top
+            raised = jnp.where(okay, jnp.exp(jnp.where(okay, shifted, -60.0)), 0.0)
+            e_ref[here, :] = raised
+            weights = raised
+            if signed:
+                bend = jnp.tanh(s)
+                t_ref[here, :] = bend
+                s_ref[here, :] = s * back
+                weights = bend * raised
+            return sums[0] + fold_rows(raised, jnp.add), sums[1] + fold_rows(dp * weights, jnp.add)
+        zero = jnp.zeros((8, TOK), F32)
+        sums = lax.fori_loop(0, keys_len // CHUNK, weigh, (zero, zero))
+        inverse = 1.0 / (jnp.sum(sums[0], 0, keepdims=True) + (1.0 - live.astype(F32)))
+        inner = jnp.sum(sums[1], 0, keepdims=True) * inverse
+
+        def slope(n):
+            here = pl.ds(pl.multiple_of(n * CHUNK, CHUNK), CHUNK)
+            dp = dp_ref[here, :]
+            unsigned = e_ref[here, :] * inverse
+            if signed:
+                bend = t_ref[here, :]
+                p_ref[here, :] = (unsigned * bend).astype(BF16)
+                grad = unsigned * ((bend * dp - inner) * s_ref[here, :] + dp * (1.0 - bend * bend))
+            else:
+                p_ref[here, :] = unsigned.astype(BF16)
+                grad = unsigned * (dp - inner)
+            ds_ref[here, :] = grad.astype(BF16)
+        loop(keys_len // CHUNK, slope)
+
+        def spread(j):
+            here = pl.ds(pl.multiple_of(j * TOK, TOK), TOK)
+            dv[here, :] += dot(p_ref[here, :], out)
+            dk[here, :] += dot(ds_ref[here, :], mine)
+        loop(i + 1, spread)
+        dq[pl.ds(pl.multiple_of(HEAD * h, HEAD), HEAD), :] = 0.125 * dot(
+            kt[pl.ds(pl.multiple_of(HEAD * h, HEAD), HEAD), 0:keys_len], ds_ref[0:keys_len, :]
+        )
+    loop(HEADS // 4, head)
+    query_grad = jnp.concatenate([dq[...], jnp.zeros((HEAD, TOK), F32)], 0).T
+    value_grad = dv[i * TOK : (i + 1) * TOK, :]
+    key_grad = dk[i * TOK : (i + 1) * TOK, :]
+    lanes = lax.broadcasted_iota(jnp.int32, (TOK, 128), 1)
+    return jnp.concatenate(
+        [
+            query_grad[:, :128],
+            jnp.where(lanes < HEAD, query_grad[:, 128:], value_grad[:, :128]),
+            value_grad[:, 128:],
+            key_grad,
+        ],
+        1,
+    ).astype(BF16)
+
+
+def backward_kernel(*refs):
+    refs = list(refs)
+    take = lambda n: [refs.pop(0) for _ in range(n)]
+    cot, lens, norms = take(3)
+    wholes = take(8)
+    stash = [take(8), take(8)]
+    (input_o,) = take(1)
+    grads_o = take(8)
+    w_qkv, w_out, w_up, w_down = take(4)
+    stream, qkv, middle, nin_t, att_t, nmid_t, pre, act_t = take(8)
+    cot_v, grad, low, branch, dpre, dmid, sums, edge, datt_s, datt_r, kt = take(11)
+    scratch = take(9)
+    dk, dv = scratch[6], scratch[7]
+    dq_s, dq_r, big, small, tall, final_r = take(6)
+    buffers = []
+    for n in range(4):
+        got, half, near = take(3)
+        count = 1 if n == 3 else 2
+        buffers.append((got, half, near, take(count), take(count)))
+    ssem, rsem, lsem, csem, as_, ar, ds_, dr, ms, mr = take(10)
+    spot = Spot()
+    r, z, rx, ry, rd, rc = spot.r, spot.z, spot.rx, spot.ry, spot.rd, spot.rc
+    sources = dict(zip(STASH, range(8)))
+    homes = dict(zip(STASH, (stream, qkv, middle, nin_t, att_t, nmid_t, pre, act_t)))
+    loads = {}
+
+    def load(layer, *names):
+        for name in names:
+            if name in homes:
+                src, dst, at = stash[layer][sources[name]], homes[name], sources[name]
+            else:
+                at = ("w_qkv", "w_out", "w_up", "w_down").index(name)
+                src, dst = wholes[4 * layer + at], (w_qkv, w_out, w_up, w_down)[at]
+                at = 8 + at
+            loads[(layer, name)] = Keep(src, dst, lsem.at[12 * layer + at])
+
+    def ready(layer, *names):
+        for name in names:
+            loads[(layer, name)].wait()
+
+    start = Keep(cot, cot_v, lsem.at[24])
+    load(1, "act_t", "w_down", "pre", "nmid_t", "w_up", "middle", "w_out", "att_t", "qkv", "nin_t", "w_qkv", "stream")
+    greet(spot.peers())
+    jobs = []
+    for layer in range(LAYERS):
+        row = []
+        for n in range(4):
+            got, half, near, zs, zr = buffers[n]
+            send = (big, small, big, tall)[n]
+            row.append(Reduce(send, got, half, near, zs, zr, grads_o[4 * layer + n], ssem, rsem, (4 * layer + n) * Reduce.SEMS))
+        jobs.append(row)
+    line = Line()
+    closed = set()
+    peers = comm_peers()
+
+    def steps_of(layer, n):
+        job = jobs[layer][n]
+
+        def close():
+            job.finish()
+            closed.add((layer, n))
+            if layer == 1:
+                job.drain()
+                for peer in peers:
+                    pl.semaphore_signal(csem.at[n], inc=1, device_id=peer, device_id_type=MESH)
+        return [job.send_near, job.send_z, close]
+
+    def credit(layer, n):
+        if layer == 0:
+            assert (1, n) in closed
+            pl.semaphore_wait(csem.at[n], len(peers))
+
+    def begin(n):
+        here = band(n * CHUNK, CHUNK)
+        value = cot_v[here, :].astype(F32) * live_column(lens, spot, CHUNK, n * CHUNK)
+        grad[here, :] = value
+        low[here, :] = value.astype(BF16)
+    start.wait()
+    loop(TOK // CHUNK, begin)
+
+    def terms(job, left, width, tile, right, other, extra=None):
+        c = lax.rem(rc, 2) if other else spot.c
+        rows = left_rows(left, c)
+
+        def step(n):
+            here = cols(n, tile)
+            value = dot(rows, right(n))
+            for b in range(4):
+                part = value[96 * b : 96 * b + 96]
+                if other:
+                    job.send[b, :, here] = part.astype(BF16)
+                else:
+                    job.got[b, :, here] = (job.got[b, :, here].astype(F32) + part).astype(BF16)
+        loop(width // tile, step)
+        if extra is not None:
+            target = job.send if other else job.got
+            for b in range(4):
+                target[b, :, 512:640] = (
+                    target[b, :, 512:640].astype(F32) + extra[pl.ds(pl.multiple_of((2 * b + c) * 96, 8), 96), :]
+                ).astype(BF16)
+
+    def down_terms(job, other):
+        c = lax.rem(rc, 2) if other else spot.c
+
+        def step(b):
+            value = dot(act_t[band((2 * b + c) * 384, 384), :], low[...])
+            if other:
+                job.send[b] = value.astype(BF16)
+            else:
+                job.got[b] = (job.got[b].astype(F32) + value).astype(BF16)
+        loop(4, step)
+
+    def att_sent(layer, g):
+        @pl.when(spot.member != g)
+        def _():
+            rcopy(
+                datt_s.at[g], datt_r.at[spot.member], as_.at[4 * layer + g], ar.at[4 * layer + spot.member], spot.device(g)
+            ).wait_send()
+
+    for layer in (1, 0):
+        signed = layer == 0
+        j_qkv, j_out, j_up, j_down = jobs[layer]
+        prior = jobs[1] if layer == 0 else None
+        gains = norms[layer]
+        ready(layer, "act_t")
+        credit(layer, 3)
+        down_terms(j_down, True)
+        j_down.send_core()
+        ready(layer, "w_down", "pre")
+        line(1)
+
+        def slope(n):
+            here = cols(n, 512)
+            value = dot_nt(low[...], w_down[pl.ds(pl.multiple_of(n * 512, 512), 512), :])
+            dpre[:, here] = (gelu_slope(pre[:, here]) * value).astype(BF16)
+        loop(6, slope)
+        if layer:
+            load(0, "w_down", "pre")
+        ready(layer, "nmid_t")
+        credit(layer, 2)
+        if prior:
+            prior[0].free_send()
+        terms(j_up, nmid_t, 3072, 512, lambda n: dpre[:, cols(n, 512)], True)
+        j_up.send_core()
+        j_down.wait_core()
+        down_terms(j_down, False)
+        if layer:
+            load(0, "act_t")
+        line(1)
+        j_down.send_diagonal()
+        ready(layer, "w_up")
+        dmid[...] = jnp.zeros_like(dmid)
+
+        def through_up(n):
+            here = cols(n, 512)
+            dmid[...] += dot_nt(dpre[:, here], w_up[:, here])
+        loop(6, through_up)
+        if layer:
+            load(0, "w_up")
+        ready(layer, "middle")
+        gain_late, bias_late = norm_back(middle, dmid, gains[2:3, :], grad, grad, branch, sums)
+        if layer:
+            load(0, "middle")
+        ready(layer, "w_out")
+        for g in range(4):
+            value = dot_nt(w_out[192 * g : 192 * g + 192, :], branch[...]).astype(BF16)
+            if layer == 0:
+                att_sent(1, g)
+            datt_s[g] = value
+
+            @pl.when(spot.member != g)
+            def _():
+                rcopy(
+                    datt_s.at[g], datt_r.at[spot.member], as_.at[4 * layer + g], ar.at[4 * layer + spot.member], spot.device(g)
+                ).start()
+
+            @pl.when(spot.member == g)
+            def _():
+                datt_r[g] = datt_s[g]
+        if layer:
+            load(0, "w_out")
+        line.add(steps_of(layer, 3))
+        line(1)
+        ready(layer, "att_t")
+        credit(layer, 1)
+        terms(j_out, att_t, 768, 256, lambda n: branch[:, cols(n, 256)], True)
+        j_out.send_core()
+        j_up.wait_core()
+        terms(j_up, nmid_t, 3072, 512, lambda n: dpre[:, cols(n, 512)], False)
+        j_up.send_diagonal()
+        if layer:
+            load(0, "nmid_t")
+        j_out.wait_core()
+        terms(j_out, att_t, 768, 256, lambda n: branch[:, cols(n, 256)], False)
+        if layer:
+            load(0, "att_t")
+        line(1)
+        j_out.send_diagonal()
+        ready(layer, "qkv")
+
+        def turn_keys(j):
+            kt[:, cols(j, TOK)] = qkv[j, :, 384:640].astype(F32).T.astype(BF16)
+        loop(4, turn_keys)
+        dk[...] = jnp.zeros_like(dk)
+        dv[...] = jnp.zeros_like(dv)
+        line.add(steps_of(layer, 2))
+        line.add(steps_of(layer, 1))
+        for g in range(4):
+            @pl.when(spot.member != g)
+            def _():
+                rcopy(
+                    datt_r.at[g], datt_r.at[g], as_.at[4 * layer + g], ar.at[4 * layer + g], spot.device(g)
+                ).wait_recv()
+        if layer == 0:
+            for g in range(4):
+                @pl.when(spot.member != g)
+                def _():
+                    rcopy(dq_s.at[g], dq_r.at[spot.member], ds_.at[4 + g], dr.at[4 + spot.member], spot.device(g)).wait_send()
+        for i in (3, 2, 1, 0):
+            block = attend_quarter_back(i, lens, qkv, kt, datt_r, scratch, signed)
+            dq_s[i] = block
+
+            @pl.when(spot.member != i)
+            def _():
+                rcopy(
+                    dq_s.at[i], dq_r.at[spot.member], ds_.at[4 * layer + i], dr.at[4 * layer + spot.member], spot.device(i)
+                ).start()
+
+            @pl.when(spot.member == i)
+            def _():
+                dq_r[i] = dq_s[i]
+            line(2)
+        if layer:
+            load(0, "qkv")
+        ready(layer, "w_qkv", "stream", "nin_t")
+        for g in range(4):
+            @pl.when(spot.member != g)
+            def _():
+                rcopy(dq_r.at[g], dq_r.at[g], ds_.at[4 * layer + g], dr.at[4 * layer + g], spot.device(g)).wait_recv()
+        dmid[...] = jnp.zeros_like(dmid)
+
+        def through_qkv(g):
+            dmid[...] += dot_nt(dq_r[g], w_qkv[:, cols(g, GROUP)])
+        loop(4, through_qkv)
+        if layer:
+            load(0, "w_qkv")
+        gain_early, bias_early = norm_back(stream, dmid, gains[0:1, :], grad, grad, low, sums)
+        if layer:
+            load(0, "stream")
+        rows = [jnp.zeros((HEAD, 768), F32), gain_early, bias_early, gain_late, bias_late, jnp.zeros((HEAD - 4, 768), F32)]
+        edge[...] = jnp.concatenate(rows, 0).T
+        if layer == 0:
+            swap(spot, low, final_r, ms.at[0], mr.at[0])
+        credit(layer, 0)
+        j_up.free_send()
+        terms(j_qkv, nin_t, 4 * GROUP, GROUP, lambda g: dq_r[g], True, edge)
+        j_qkv.send_core()
+        line(1)
+        j_qkv.wait_core()
+        terms(j_qkv, nin_t, 4 * GROUP, GROUP, lambda g: dq_r[g], False, edge)
+        if layer:
+            load(0, "nin_t")
+        j_qkv.send_diagonal()
+        line.add(steps_of(layer, 0))
+    line.flush()
+    for job in jobs[0]:
+        job.drain()
+    for g in range(4):
+        att_sent(0, g)
+    for g in range(4):
+        @pl.when(spot.member != g)
+        def _():
+            rcopy(dq_s.at[g], dq_r.at[spot.member], ds_.at[g], dr.at[spot.member], spot.device(g)).wait_send()
+    swap_wait(spot, low, final_r, ms.at[0], mr.at[0])
+
+    def widen(n):
+        here = band(n * CHUNK, CHUNK)
+        input_o[here, :] = final_r[here, :].astype(F32)
+    loop(TOK // CHUNK, widen)
+
+
+def backward_call(cot, lens, norms, wholes, stash):
+    d = cot.shape[1]
+    ff = wholes[2].shape[1]
+    any_space = pl.BlockSpec(memory_space=pl.ANY)
+    vmem = pl.BlockSpec(memory_space=pltpu.VMEM)
+    dma = lambda n: pltpu.SemaphoreType.DMA((n,))
+    shapes = [(whole.shape[0] // 32, whole.shape[1]) for whole in wholes]
+    buffers = []
+    for n in range(4):
+        rows, width = wholes[n].shape[0] // 8, wholes[n].shape[1]
+        cuts = [(rows // 4, width)] if n == 3 else [(16, width), (16, width // 2)]
+        buffers += [
+            pltpu.VMEM((4, rows, width), BF16),
+            pltpu.VMEM((2, rows // 2, width), BF16),
+            pltpu.VMEM((2, rows, width), BF16),
+        ]
+        buffers += [pltpu.VMEM((4,) + cut, BF16) for cut in cuts]
+        buffers += [pltpu.VMEM((3,) + cut, BF16) for cut in cuts]
+    outs = pl.pallas_call(
+        backward_kernel,
+        out_shape=[jax.ShapeDtypeStruct((TOK, d), F32)] + [jax.ShapeDtypeStruct(shape, F32) for shape in shapes],
+        in_specs=[any_space, vmem, vmem] + [any_space] * 24,
+        out_specs=[vmem] * 9,
+        scratch_shapes=[pltpu.VMEM(whole.shape, BF16) for whole in wholes[:4]]
+        + [pltpu.VMEM(shape, kind) for shape, kind in stash_shapes(d, ff)]
+        + [
+            pltpu.VMEM((TOK, d), BF16),
+            pltpu.VMEM((TOK, d), F32),
+            pltpu.VMEM((TOK, d), BF16),
+            pltpu.VMEM((TOK, d), BF16),
+            pltpu.VMEM((TOK, ff), BF16),
+            pltpu.VMEM((TOK, d), F32),
+            pltpu.VMEM((16, d), F32),
+            pltpu.VMEM((d, 128), F32),
+            pltpu.VMEM((4, 192, TOK), BF16),
+            pltpu.VMEM((4, 192, TOK), BF16),
+            pltpu.VMEM((WIDE, 4 * TOK), BF16),
+        ]
+        + [pltpu.VMEM((4 * TOK, TOK), F32)] * 4
+        + [pltpu.VMEM((4 * TOK, TOK), BF16)] * 2
+        + [pltpu.VMEM((4 * TOK, WIDE), F32)] * 2
+        + [
+            pltpu.VMEM((192, TOK), F32),
+            pltpu.VMEM((4, TOK, GROUP), BF16),
+            pltpu.VMEM((4, TOK, GROUP), BF16),
+            pltpu.VMEM((4, 96, ff), BF16),
+            pltpu.VMEM((4, 96, d), BF16),
+            pltpu.VMEM((4, ff // 8, d), BF16),
+            pltpu.VMEM((TOK, d), BF16),
+        ]
+        + buffers
+        + [
+            dma(8 * Reduce.SEMS),
+            dma(8 * Reduce.SEMS),
+            dma(25),
+            pltpu.SemaphoreType.REGULAR((4,)),
+            dma(8),
+            dma(8),
+            dma(8),
+            dma(8),
+            dma(1),
+            dma(1),
+        ],
+        compiler_params=pltpu.CompilerParams(collective_id=1, has_side_effects=True, vmem_limit_bytes=63 * 2**20),
+    )(cot, lens, norms, *wholes, *stash[0], *stash[1])
+    return outs[0], outs[1:]
+
+
+def backward_part(result, cot, lens, norms, wholes, stash):
+    input_grad, grads = backward_call(cot, lens, norms, wholes, stash)
+    both = [jnp.stack([grads[n], grads[4 + n]]) for n in range(4)]
+    own = both[0].shape[1]
+    groups = both[0].reshape(LAYERS, own, 4, GROUP)
+    parts = [groups[..., at : at + 192].reshape(LAYERS, own, -1) for at in (0, 384, 192)]
+    edge = groups[:, :, 0, 3 * 192 : 3 * 192 + 4]
+    return (
+        result[None],
+        input_grad[None],
+        jnp.concatenate(parts, -1),
+        both[1],
+        both[2],
+        both[3],
+        jnp.stack([edge[..., 0], edge[..., 2]], 1),
+        edge[..., 1],
+        edge[..., 3],
+    )
+
+
+def local_fast(tokens, lengths, w_qkv, w_out, w_up, w_down, gains, biases, cotangent):
+    own = w_qkv.shape[1]
+    parts = [w_qkv[:, :, n * 768 : (n + 1) * 768].reshape(LAYERS, own, 4, 192) for n in range(3)]
+    edge = jnp.stack([gains[:, 0], biases[:, 0], gains[:, 1], biases[:, 1]], -1)
+    edge = jnp.pad(edge[:, :, None, :], ((0, 0), (0, 0), (0, 3), (0, HEAD - 4)))
+    grouped = jnp.concatenate([parts[0], parts[2], parts[1], edge], -1).reshape(LAYERS, own, 4 * GROUP)
+    lens = jnp.pad(lengths, ((0, 7), (0, 124)))
+    owns = []
+    for number in range(LAYERS):
+        owns += [grouped[number], w_out[number], w_up[number], w_down[number]]
+    (result, cot, lens, norms), wholes, stash = forward_call(tokens[0], cotangent[0], lens, owns)
+    return backward_part(result, cot, lens, norms, wholes, stash)
+
+
 def solution(mesh):
     in_specs = (
         P("rows", "kv", None),
@@ -338,4 +1605,5 @@
         P(None, ("rows", "kv")),
         P(None, ("rows", "kv")),
     )
-    return jax.shard_map(local, mesh=mesh, in_specs=in_specs, out_specs=out_specs, check_vma=False)
+    fast = dict(mesh.shape) == {"rows": 8, "kv": 4}
+    return jax.shard_map(local_fast if fast else local_generic, mesh=mesh, in_specs=in_specs, out_specs=out_specs, check_vma=False)

time: 1890 us -> 428 us (0.23)
  waiting for transfers between devices: 1150 us -> 0 us
  Pallas kernels: 0 us -> 406 us
  blocking collectives: 327 us -> 0 us
  matrix products: 218 us -> 0 us
  local copies, waits for them, and re-layouts: 88.5 us -> 15.5 us
  other arithmetic: 44.2 us -> 4.35 us
  starting transfers between devices: 30 us -> 0 us
    all_gather x18 -> x0, waiting for transfers between devices: 595 us -> none  [the longest x2 164 us: reduce_grads(): lax.all_gather(rights[2], 'kv', axis=0, tiled=True)]
    pallas_call x0 -> x2, Pallas kernels: none -> 406 us  [the longest x1 232 us: backward_call(): pl.pallas_call(backward_kernel, out_shape=[jax.ShapeDtypeStruct((TOK, d),...]
    reduce_scatter x10 -> x0, waiting for transfers between devices: 337 us -> none  [the longest x2 79 us: reduce_grads(): lax.psum_scatter(partial_sums[3].astype(jnp.bfloat16), 'rows', scatter_di...]
    all_gather x4 -> x0, blocking collectives: 282 us -> none  [the longest x2 148 us: local(): lax.all_gather(gains[number], ('rows', 'kv'), axis=1, tiled=True)]
    all_to_all x8 -> x0, waiting for transfers between devices: 215 us -> none  [the longest x2 121 us: reduce_grads(): lax.all_to_all(lefts[3], 'kv', split_axis=2, concat_axis=0, tiled=True)]
    dot_general x34 -> x0, matrix products: 156 us -> none  [the longest x8 32.8 us: reduce_grads(): jnp.einsum('ti,to->io', left_block, whole[number], preferred_element_type...]
    sub x3 -> x0, matrix products: 62.3 us -> none  [the longest x1 27.4 us: score_grads(): tanh_s * weight_grad - inner_sum]
    unnamed x1 -> x0, blocking collectives: 44.5 us -> none
  transfers between devices with their start and end apart: 36 -> 0, of which waited for: 26 -> 0; matrix products, arithmetic and copies ran while one was open for 15% -> 0% of each run, Pallas kernels for 0% -> 0%
where the time goes in v2:
time: 428 us; the launch traced here: 427 us
  Pallas kernels  406 us (95%)
  local copies, waits for them, and re-layouts  15.5 us (4%)
  other arithmetic  4.35 us (1%)
    pallas_call x1, Pallas kernels, backward_call(): pl.pallas_call(backward_kernel, out_shape=[jax.ShapeDtypeStruct((TOK, d),...  232 us
    pallas_call x1, Pallas kernels, forward_call(): pl.pallas_call(forward_kernel, out_shape=[jax.ShapeDtypeStruct((TOK, d),...  174 us

profile of v2, /device:TPU:0, one launch (start us, length us, event | category | flops | bytes accessed | tf_op | source)
XLA Modules:
  0.0 426.7 jit_solution(16774424629751471601)
XLA Ops:
  0.6 0.0 copy-start.2
  0.7 0.8 fusion.5
  1.4 0.8 fusion.6
  2.2 1.2 pad.8.refs_2_
  3.5 0.1 copy.47
  3.6 1.4 slice_bitcast_fusion.4
  5.0 1.0 fusion.4
  5.9 0.1 reshape.46
  6.1 0.1 reshape.48
  6.2 0.1 reshape.47
  6.4 0.2 fusion.1
  6.6 0.1 fusion.3
  6.7 0.7 copy.49
  7.4 0.7 copy.48
  8.0 1.7 slice_bitcast_fusion.1
  9.8 0.0 copy-done.2
  9.8 0.7 slice_bitcast_fusion
  10.5 174.4 %shard_map.160 = (bf16[256,768]{1,0:T(8,128)(2,1)}, bf16[256,768]{1,0:T(8,128)(2,1)}, s32[8,128]{1,0:T(8,128)}, f32[2,8,768]{2,1,0:T(8,128)}, bf16[768,2560]{1,0...) custom-call(bf16[256,768]{1,0:T(8,128)(2,1)} %bitcast.48, ...), custom_call_target="tpu_custom_call" | custom-call | tf_op jit(solution)/shard_map/pallas_call | solution.py:896
  184.9 231.6 %shard_map.161 = (f32[256,768]{1,0:T(8,128)}, f32[24,2560]{1,0:T(8,128)}, f32[24,768]{1,0:T(8,128)}, f32[24,3072]{1,0:T(8,128)}, f32[96,768]{1,0:T(8,128)}, /*in...) custom-call(bf16[256,768]{1,0:T(8,128)(2,1)} %get-tuple-element.47.refs_0_, ...), custom_call_target="tpu_custom_call" | custom-call | tf_op jit(solution)/shard_map/pallas_call | solution.py:1501
  416.5 1.6 pad_maximum_fusion.3
  418.1 0.0 copy-start.5
  418.1 0.0 copy-start.6
  418.1 1.1 stack.43
  419.2 1.0 stack.44
  420.3 0.0 copy-start.3
  420.3 0.0 copy-start.4
  420.3 0.1 slice_bitcast_fusion.6
  420.4 0.7 slice_reduce_fusion
  421.1 0.6 copy.42
  421.7 0.0 copy-start.1
  421.7 0.1 fusion.2
  421.8 0.0 copy-start
  421.9 0.1 copy.39
  421.9 0.1 reshape.49
  422.1 0.1 copy.41
  422.2 0.1 reshape.51
  422.3 0.1 copy.40
  422.4 0.1 reshape.50
  422.5 0.8 pad_maximum_fusion.2
  423.3 0.0 copy-done.5
  423.3 0.0 copy-done.6
  423.3 0.9 pad_maximum_fusion
  424.2 0.0 copy-done.3
  424.2 0.0 copy-done.4
  424.2 0.9 pad_maximum_fusion.1
  425.1 0.0 copy-done.1
  425.1 0.7 copy.59
  425.8 0.0 copy-done
  425.8 0.9 copy.60
  (6 shorter events, 0.1 us)
Async XLA Ops:
  0.6 9.1 %copy-start.2 = (bf16[2,96,768]{2,1,0:T(8,128)(2,1)S(1)}, bf16[2,96,768]{2,1,0:T(8,128)(2,1)}, u32[]{:S(2)}) copy-start(bf16[2,96,768]{2,1,0:T(8,128)(2,1)} %param.14) | copy-start | bytes 884740
  418.1 5.2 %copy-start.5 = (f32[24,3072]{1,0:T(8,128)S(1)}, f32[24,3072]{1,0:T(8,128)}, u32[]{:S(2)}) copy-start(f32[24,3072]{1,0:T(8,128)} %get-tuple-element.79) | copy-start | bytes 884740
  418.1 5.2 %copy-start.6 = (f32[24,3072]{1,0:T(8,128)S(1)}, f32[24,3072]{1,0:T(8,128)}, u32[]{:S(2)}) copy-start(f32[24,3072]{1,0:T(8,128)} %get-tuple-element.80) | copy-start | bytes 884740
  420.3 3.9 copy-start.3
  420.3 3.9 copy-start.4
  421.7 3.3 copy-start.1
  421.8 4.0 copy-start

commit v3 on v0

--- a/solution.py
+++ b/solution.py
@@ -3,6 +3,8 @@
 import jax
 import jax.numpy as jnp
 from jax import lax
+from jax.experimental import pallas as pl
+from jax.experimental.pallas import tpu as pltpu
 from jax.sharding import PartitionSpec as P
 
 HEADS = 12
@@ -162,7 +164,7 @@
     return results + (norm_parts[0], norm_parts[1])
 
 
-def local(tokens, lengths, w_qkv, w_out, w_up, w_down, gains, biases, cotangent):
+def local_generic(tokens, lengths, w_qkv, w_out, w_up, w_down, gains, biases, cotangent):
     rows_here, slot_dev, model_width = tokens.shape
     slot_count = slot_dev * lax.axis_size("kv")
     first_slot = lax.axis_index("kv") * slot_dev
@@ -315,6 +317,1483 @@
     )
 
 
+F32 = jnp.float32
+BF16 = jnp.bfloat16
+MESH = pl.DeviceIdType.MESH
+ZN = 4
+
+
+def flip(value, unit):
+    bit = lax.rem(lax.div(value, unit), 2)
+    return value + unit - 2 * unit * bit
+
+
+def places_of():
+    r = lax.axis_index("rows")
+    z = lax.axis_index("kv")
+    return r, z, flip(r, 2), flip(r, 4), flip(flip(r, 2), 4), flip(r, 1)
+
+
+def turn(z, k):
+    return lax.rem(z + k, ZN)
+
+
+def rcopy(src, dst, ssem, rsem, device):
+    return pltpu.make_async_remote_copy(
+        src_ref=src, dst_ref=dst, send_sem=ssem, recv_sem=rsem, device_id=device, device_id_type=MESH
+    )
+
+
+def band(start, size):
+    return pl.ds(pl.multiple_of(start, 16), size)
+
+
+def greet(peers):
+    barrier = pltpu.get_barrier_semaphore()
+    for peer in peers:
+        pl.semaphore_signal(barrier, inc=1, device_id=peer, device_id_type=MESH)
+    pl.semaphore_wait(barrier, len(peers))
+
+
+def comm_peers():
+    r, z, rx, ry, rd, rc = places_of()
+    return [(r, turn(z, 1)), (r, turn(z, 2)), (r, turn(z, 3)), (rx, z), (ry, z), (rc, z)]
+
+
+def col_step(width):
+    return 256 if width % 256 == 0 else 128
+
+
+def add_rows(dst, src, rows):
+    def step(i, carry):
+        here = band(i * 16, 16)
+        dst[here, :] = (dst[here, :].astype(F32) + src[here, :].astype(F32)).astype(BF16)
+        return carry
+    lax.fori_loop(0, rows // 16, step, 0)
+
+
+SEND = 0
+PLANE = 100
+PASS = 200
+LAST = 300
+WHOLE = 400
+NORM = 600
+SHARE = 700
+PROJECT = 800
+ATTEND = 900
+OUTPUT = 1000
+UP = 1100
+DOWN = 1200
+TOKENS = 500
+COTANGENT = 510
+WIDEN = 520
+RESULT = 530
+SECOND = 0
+NEAR = 100
+OVER_Z = 200
+CLOSE = 300
+THEIRS = 400
+OURS = 500
+SLOPE = 600
+THROUGH = 700
+NORM_BACK = 800
+ASK = 900
+KEYS = 1000
+ASKED = 1100
+ATTEND_BACK = 1200
+PARTIAL = 1300
+FIRST_BACK = 1400
+BEGIN = 1500
+SWAP_BACK = 1510
+
+FORWARD_ORDER = [
+    0, 100, 1, 2, 200, 500, 3, 300, 101, 400, 102, 201, 301, 4, 401, 103, 202, 520, 600, 5, 800, 802, 104,
+    302, 203, 402, 105, 6, 303, 204, 700, 403, 7, 801, 803, 106, 8, 9, 900, 901, 304, 205, 107, 902, 903, 404,
+    206, 305, 207, 10, 1000, 108, 405, 1100, 306, 307, 109, 11, 1101, 406, 407, 1200, 1201, 110, 601, 810,
+    812, 208, 111, 701, 811, 209, 813, 910, 911, 912, 308, 913, 210, 408, 510, 309, 211, 1001, 1110, 409, 310,
+    1111, 311, 410, 1210, 411, 1211, 530,
+]
+BACKWARD_ORDER = [
+    1500, 410, 610, 710, 408, 611, 510, 10, 411, 711, 801, 1001, 901, 407, 508, 409, 511, 110, 11, 1101, 1213,
+    1212, 108, 1211, 1210, 111, 509, 210, 9, 507, 1312, 406, 8, 1313, 1311, 506, 6, 310, 211, 1401, 109, 404,
+    600, 208, 106, 311, 504, 209, 4, 700, 601, 405, 107, 701, 308, 104, 800, 900, 402, 505, 5, 309, 7, 1000,
+    204, 206, 403, 1100, 502, 207, 2, 1203, 105, 1202, 102, 306, 307, 205, 503, 3, 401, 1201, 202, 1200, 501,
+    1, 1302, 400, 1303, 305, 103, 1301, 304, 101, 500, 302, 0, 203, 201, 100, 200, 301, 1400, 1510, 412, 303,
+    512, 12, 112, 212, 300, 312,
+]
+
+
+GROUP = 640
+TOK = 256
+WIDE = 256
+PARTS = HEADS // 4
+CHUNK = 64
+FAR = -1e30
+KB = 256
+JOBS = 6
+
+
+def dot(a, b):
+    return jnp.dot(a, b, preferred_element_type=F32)
+
+
+def dot_nt(a, b):
+    return lax.dot_general(a, b, (((1,), (1,)), ((), ())), preferred_element_type=F32)
+
+
+def dot_tn(a, b):
+    return lax.dot_general(a, b, (((0,), (0,)), ((), ())), preferred_element_type=F32)
+
+
+def loop(count, body):
+    def step(i, carry):
+        body(i)
+        return carry
+    lax.fori_loop(0, count, step, 0)
+
+
+def cols(i, size):
+    return pl.ds(pl.multiple_of(i * size, 128), size)
+
+
+class Spot:
+    def __init__(self):
+        self.r, self.z, self.rx, self.ry, self.rd, self.rc = places_of()
+        self.c = lax.rem(self.r, 2)
+        self.parity = lax.rem(self.z, 2)
+        self.member = 2 * self.c + self.parity
+        self.swaps = (self.c + lax.div(self.z, 2)) == 1
+        self.partner = (self.rc, flip(self.z, 2))
+
+    def mate(self, k):
+        r = self.rc if k >= 2 else self.r
+        z = flip(self.z, 1) if k % 2 else self.z
+        return (r, z), 2 * lax.rem(r, 2) + lax.rem(z, 2)
+
+    def device(self, member):
+        return (self.r - self.c + lax.div(member, 2), self.z - self.parity + lax.rem(member, 2))
+
+    def peers(self):
+        return comm_peers() + [(self.rc, flip(self.z, 1)), self.partner]
+
+
+class Gather:
+    SEMS = 11
+
+    def __init__(self, own, whole, bufs, ssem, rsem, base, paired=False):
+        self.own, self.whole, self.bufs = own, whole, bufs
+        self.ssem, self.rsem, self.base = ssem, rsem, base
+        self.split, self.paired = len(bufs) > 0, paired
+        self.rows, self.width = whole.shape[0] // 8, whole.shape[1]
+        self.sent = []
+
+    def _copy(self, src, dst, at, device):
+        return rcopy(src, dst, self.ssem.at[self.base + at], self.rsem.at[self.base + at], device)
+
+    def _block(self, r, half=None):
+        if half is None:
+            return self.whole.at[band(r * self.rows, self.rows), :]
+        part = self.rows // 2
+        return self.whole.at[band(r * self.rows + half * part, part), :]
+
+    def _cored(self, r, column):
+        if not self.paired:
+            return self._block(r)
+        return self.whole.at[band(r * self.rows, self.rows), cols(column, self.width // 2)]
+
+    def _send(self, src, dst, at, device):
+        copy = self._copy(src, dst, at, device)
+        copy.start()
+        self.sent.append(copy)
+
+    def prepare(self):
+        r, z = places_of()[:2]
+        if self.split:
+            zbuf = self.bufs[0]
+            half = self.width // 2
+            values = [self.own(place) for place in (0, 1)] if self.paired else [self.own[...].astype(F32)]
+            for place, own in enumerate(values):
+                packed = jnp.concatenate(
+                    [own[:16], jnp.concatenate([own[16:, :half], own[16:, half:]], 0)], 1
+                ).astype(BF16)
+                if self.paired:
+                    self.bufs[1][place] = packed
+                else:
+                    zbuf[pl.ds(z, 1)] = packed[None]
+            if self.paired:
+                zbuf[pl.ds(z, 1)] = self.bufs[1][pl.ds(lax.rem(z, 2), 1)]
+        else:
+            part = self.rows // ZN
+            self.whole[band(r * self.rows + z * part, part), :] = self.own[...]
+
+    def _zref(self, z):
+        if self.split:
+            return self.bufs[0].at[z]
+        part = self.rows // ZN
+        return self.whole.at[band(places_of()[0] * self.rows + z * part, part), :]
+
+    def send_z(self):
+        r, z = places_of()[:2]
+        for k in (1, 2, 3):
+            there = turn(z, k)
+            src = self.bufs[1].at[lax.rem(there, 2)] if self.paired else self._zref(z)
+            self._send(src, self._zref(z), k - 1, (r, there))
+
+    def wait_z(self):
+        r, z = places_of()[:2]
+        for k in (1, 2, 3):
+            ref = self._zref(turn(z, ZN - k))
+            self._copy(ref, ref, k - 1, (r, turn(z, ZN - k))).wait_recv()
+        if self.split:
+            zbuf = self.bufs[0]
+            half = self.width // 2
+            step = col_step(half)
+            for side in (0, 1):
+                def assemble(i, side=side):
+                    at = pl.multiple_of(self.width + i * step, 128)
+                    here = pl.ds(pl.multiple_of(side * half + i * step, 128), step)
+                    parts = []
+                    for piece in range(ZN):
+                        parts.append(zbuf[piece, :, here].astype(F32))
+                        parts.append(zbuf[piece, :, pl.ds(at, step)].astype(F32)[8 * side : 8 * side + 8])
+                    self.whole[band(r * self.rows, self.rows), here] = jnp.concatenate(parts, 0).astype(BF16)
+                loop(half // step, assemble)
+
+    def send_plane(self):
+        r, z, rx, ry, rd, rc = places_of()
+        own = self._block(r)
+        self._send(own, own, 3, (rx, z))
+        self._send(own, own, 4, (ry, z))
+        self._core(r, 7)
+
+    def _core(self, block, at):
+        r, z, rx, ry, rd, rc = places_of()
+        ref = self._cored(block, lax.rem(rc, 2))
+        self._send(ref, ref, at, (rc, z))
+
+    def forward(self):
+        r, z, rx, ry, rd, rc = places_of()
+        first, second = self._block(rx), self._block(ry)
+        self._copy(first, first, 3, (rx, z)).wait_recv()
+        part = self._block(rx, 0)
+        self._send(part, part, 5, (ry, z))
+        self._copy(second, second, 4, (ry, z)).wait_recv()
+        part = self._block(ry, 1)
+        self._send(part, part, 6, (rx, z))
+        self._core(rx, 8)
+        self._core(ry, 9)
+
+    def forward_last(self):
+        r, z, rx, ry, rd, rc = places_of()
+        part = self._block(rd, 0)
+        self._copy(part, part, 5, (ry, z)).wait_recv()
+        part = self._block(rd, 1)
+        self._copy(part, part, 6, (rx, z)).wait_recv()
+        self._core(rd, 10)
+
+    def finish(self):
+        r, z, rx, ry, rd, rc = places_of()
+        for at, block in ((7, r), (8, rx), (9, ry), (10, rd)):
+            ref = self._cored(flip(block, 1), lax.rem(r, 2))
+            self._copy(ref, ref, at, (rc, z)).wait_recv()
+
+    def drain(self):
+        for copy in self.sent:
+            copy.wait_send()
+
+
+def swap(spot, src, dst, ssem, rsem):
+    @pl.when(spot.swaps)
+    def _():
+        rcopy(src, dst, ssem, rsem, spot.partner).start()
+
+    @pl.when(jnp.logical_not(spot.swaps))
+    def _():
+        pltpu.make_async_copy(src, dst, rsem).start()
+
+
+def swap_wait(spot, src, dst, ssem, rsem):
+    @pl.when(spot.swaps)
+    def _():
+        rcopy(src, dst, ssem, rsem, spot.partner).wait()
+
+    @pl.when(jnp.logical_not(spot.swaps))
+    def _():
+        pltpu.make_async_copy(src, dst, rsem).wait()
+
+
+def starts_of(lens, i):
+    places = lax.broadcasted_iota(jnp.int32, (1, TOK), 1) + i * TOK
+    end = jnp.zeros((1, 1), jnp.int32)
+    start = jnp.zeros((1, TOK), jnp.int32)
+    for n in range(4):
+        end = end + lens[0:1, n : n + 1]
+        start = jnp.maximum(start, jnp.where(end <= places, end, 0))
+    live = places < end
+    return places, jnp.where(live, start, 1 << 20), live
+
+
+def live_column(lens, spot, rows, first):
+    places = lax.broadcasted_iota(jnp.int32, (rows, 1), 0) + spot.member * TOK + first
+    end = lens[0:1, 0:1] + lens[0:1, 1:2] + lens[0:1, 2:3] + lens[0:1, 3:4]
+    return (places < end).astype(F32)
+
+
+def centred(value):
+    center = value - jnp.mean(value, -1, keepdims=True)
+    spread = jnp.mean(center * center, -1, keepdims=True)
+    return center * lax.rsqrt(spread + EPSILON)
+
+
+def fold_rows(value, op):
+    rows = value.shape[0]
+    parts = [value[8 * n : 8 * n + 8] for n in range(rows // 8)]
+    while len(parts) > 1:
+        parts = [op(parts[n], parts[n + 1]) if n + 1 < len(parts) else parts[n] for n in range(0, len(parts), 2)]
+    return parts[0]
+
+
+def head_lanes(shape, h, offset):
+    lanes = lax.broadcasted_iota(jnp.int32, shape, 1)
+    return lax.div(lanes, HEAD) == h + offset
+
+
+def masked_rows(first, rows, places, start, diagonal):
+    keys = lax.broadcasted_iota(jnp.int32, (rows, TOK), 0) + first
+    okay = keys >= start
+    return okay & (keys <= places) if diagonal else okay
+
+
+def over_blocks(i, body, carry):
+    per = TOK // KB if KB <= TOK else 1
+    if i:
+        carry = lax.fori_loop(0, i * per, lambda n, c: body(n * KB, c, False), carry)
+    for n in range(per):
+        carry = body(i * TOK + n * KB, carry, True)
+    return carry
+
+
+def key_rows(qkv, first, at):
+    quarter = lax.div(first, TOK)
+    here = pl.ds(pl.multiple_of(lax.rem(first, TOK), KB), KB)
+    return qkv[quarter, here, at : at + WIDE]
+
+
+def masked_heads(value_t, offset):
+    rows = lax.div(lax.broadcasted_iota(jnp.int32, value_t.shape, 0), HEAD)
+    return jnp.concatenate([jnp.where(rows == h + offset, value_t, 0.0) for h in range(PARTS)], 1).astype(BF16)
+
+
+def magnitude_of(s):
+    square = s * s + 1.0
+    back = lax.rsqrt(square)
+    return square * back, back
+
+
+def attend_quarter(i, lens, qkv, vt, acc, o_ref, stats, signed):
+    places, start, live = starts_of(lens, i)
+    mine = masked_heads(qkv[i, :, 0:WIDE].astype(F32).T * 0.125, 0)
+    acc[...] = jnp.zeros_like(acc)
+
+    def block(first, carry, diagonal):
+        keys = key_rows(qkv, first, 384)
+        okay = masked_rows(first, KB, places, start, diagonal)
+        here = pl.ds(pl.multiple_of(first, KB), KB)
+        out, lows, shrinks = [], [], []
+        scores = [dot(keys, mine[:, h * TOK : (h + 1) * TOK]) for h in range(PARTS)]
+        for h in range(PARTS):
+            old, total = carry[2 * h], carry[2 * h + 1]
+            s = scores[h]
+            value = jnp.where(okay, magnitude_of(s)[0] if signed else s, FAR)
+            new = jnp.maximum(old, jnp.max(fold_rows(value, jnp.maximum), 0, keepdims=True))
+            raised = jnp.exp(value - new)
+            shrink = jnp.exp(old - new)
+            lows.append((jnp.tanh(s) * raised if signed else raised).astype(BF16))
+            shrinks.append(shrink)
+            out += [new, total * shrink + jnp.sum(fold_rows(raised, jnp.add), 0, keepdims=True)]
+        terms = [dot(vt[HEAD * (h + 1) : HEAD * (h + 2), here], lows[h]) for h in range(PARTS)]
+        for h in range(PARTS):
+            rows = slice(HEAD * h, HEAD * (h + 1))
+            acc[rows, :] = acc[rows, :] * shrinks[h] + terms[h]
+        return tuple(out)
+    lowest = jnp.full((1, TOK), 0.0 if signed else -10000.0, F32)
+    carry = over_blocks(i, block, (lowest, jnp.zeros((1, TOK), F32)) * PARTS)
+    for h in range(PARTS):
+        inverse = 1.0 / (carry[2 * h + 1] + (1.0 - live.astype(F32)))
+        stats[i, h : h + 1, :] = carry[2 * h]
+        stats[i, PARTS + h : PARTS + h + 1, :] = inverse
+        acc[HEAD * h : HEAD * (h + 1), :] = acc[HEAD * h : HEAD * (h + 1), :] * inverse
+    o_ref[i] = acc[...].astype(BF16)
+
+
+class Keep:
+    def __init__(self, src, dst, sem):
+        self.copy = pltpu.make_async_copy(src, dst, sem)
+        self.copy.start()
+        self.open = True
+
+    def wait(self):
+        if self.open:
+            self.copy.wait()
+        self.open = False
+
+
+STASH = ("stream", "qkv", "middle", "nin_t", "att_t", "nmid_t", "pre", "act_t", "out", "stats")
+
+
+def stash_shapes(d, ff):
+    return [
+        ((TOK, d), F32),
+        ((4, TOK, GROUP), BF16),
+        ((TOK, d), F32),
+        ((d, 4 * TOK), BF16),
+        ((d, TOK), BF16),
+        ((d, TOK), BF16),
+        ((TOK, ff), F32),
+        ((ff, TOK), BF16),
+        ((4, 192, TOK), F32),
+        ((4, 8, TOK), F32),
+    ]
+
+
+def forward_kernel(*refs):
+    refs = list(refs)
+    take = lambda n: [refs.pop(0) for _ in range(n)]
+    tok, cot, lengths = take(3)
+    sources = take(4)
+    gains, biases = take(2)
+    result_o, cot_o, lens_o, norms_o = take(4)
+    whole_o = take(2 * JOBS)
+    stash_o = [take(10), take(10)]
+    wholes = take(2 * JOBS)
+    zbuf = [take((2, 1, 1, 1, 0, 0)[n % JOBS]) for n in range(2 * JOBS)]
+    tok_v, lens_in, lens_v, stream, nin0, nin1, qkv, vt, outs, stats, o_ref, att0, att1, pre, act, act_t, nin_t, nt_mid, normed, middle, res = take(21)
+    ssem, rsem, osem, stsem, ns, nr, os_, or_, ms, mr = take(10)
+    spot = Spot()
+    lens_in[...] = jnp.zeros_like(lens_in)
+    lens_in[0:1, 0:4] = lengths[...]
+    greet(spot.peers())
+    jobs = []
+
+    def grouped(layer):
+        def pair(place):
+            vectors = [ref[layer, which : which + 1, :].astype(F32) for which in (0, 1) for ref in (gains, biases)]
+            own = vectors[0].shape[1]
+            top = jnp.concatenate([jnp.concatenate(vectors, 0), jnp.zeros((4, 128 - own), F32)], 1)
+            edge = jnp.concatenate([top, jnp.zeros((124, 128), F32)], 0).T[:own, :HEAD]
+            parts = []
+            for g in (place, place + 2):
+                for at in (0, 2, 1):
+                    parts.append(sources[0][layer, :, 768 * at + 192 * g : 768 * at + 192 * g + 192].astype(F32))
+                parts.append(edge)
+            return jnp.concatenate(parts, 1)
+        return pair
+
+    for layer in range(LAYERS):
+        out_in, up_in, down_in = [source.at[layer] for source in sources[1:]]
+        ff, d = up_in.shape[1] // 2, down_in.shape[1] // 2
+        owns = [grouped(layer), out_in] + [up_in.at[:, h * ff : (h + 1) * ff] for h in (0, 1)] + [down_in.at[:, h * d : (h + 1) * d] for h in (0, 1)]
+        for n, own in enumerate(owns):
+            at = layer * JOBS + n
+            jobs.append(Gather(own, wholes[at], zbuf[at], ssem, rsem, at * Gather.SEMS, n == 0))
+    kept = {}
+
+    def keep(name, src, dst, sem):
+        kept[name] = Keep(src, dst, sem)
+
+    def settle(name):
+        if name in kept:
+            kept[name].wait()
+
+    def stash(layer, name, src):
+        at = STASH.index(name)
+        keep((layer, name), src, stash_o[layer][at], stsem.at[10 * layer + at])
+
+    steps = {}
+
+    def step(name):
+        def note(run):
+            steps[name] = run
+        return note
+
+    for n, job in enumerate(jobs):
+        def first(job=job):
+            job.prepare()
+            job.send_z()
+
+        def plane(job=job):
+            job.wait_z()
+            job.send_plane()
+
+        def done(job=job, n=n):
+            job.finish()
+            src = wholes[n]
+            if n % JOBS == 0:
+                src = src.at[:, cols(spot.c, GROUP)]
+            keep(("whole", n), src, whole_o[n], osem.at[n])
+        steps.update({SEND + n: first, PLANE + n: plane, PASS + n: job.forward, LAST + n: job.forward_last, WHOLE + n: done})
+
+    @step(TOKENS)
+    def _():
+        swap(spot, tok, tok_v, ms.at[0], mr.at[0])
+        swap(spot, lens_in, lens_v, ms.at[1], mr.at[1])
+
+    @step(COTANGENT)
+    def _():
+        swap(spot, cot, cot_o, ms.at[2], mr.at[2])
+
+    @step(WIDEN)
+    def _():
+        swap_wait(spot, tok, tok_v, ms.at[0], mr.at[0])
+        swap_wait(spot, lens_in, lens_v, ms.at[1], mr.at[1])
+        lens_o[...] = lens_v[...]
+
+        def widen(n):
+            here = band(n * CHUNK, CHUNK)
+            stream[here, :] = tok_v[here, :].astype(F32)
+        loop(TOK // CHUNK, widen)
+        stash(0, "stream", stream)
+
+    def layer_steps(layer):
+        base = layer * JOBS
+        w_qkv, w_out, w_up0, w_up1, w_down0, w_down1 = wholes[base : base + JOBS]
+        nin = (nin0, nin1)[layer]
+        att = (att0, att1)[layer]
+        signed = layer == 0
+
+        def gathered(k):
+            mate, member = spot.mate(k)
+            return rcopy(nin.at[member], nin.at[member], ns.at[4 * layer + k], nr.at[4 * layer + k], mate)
+
+        def give(k, member):
+            mate = spot.mate(1 if k == 1 else 2)[0]
+            return rcopy(nin.at[member], nin.at[member], ns.at[4 * layer + k], nr.at[4 * layer + k], mate)
+
+        @step(NORM + layer)
+        def _():
+            edge = w_qkv[:, pl.ds(pl.multiple_of(spot.c * GROUP + 512, 128), 128)].astype(F32).T
+            norms_o[layer] = edge[HEAD : HEAD + 8]
+
+            def first_norm(n):
+                here = band(n * CHUNK, CHUNK)
+                value = centred(stream[here, :]) * norms_o[layer, 0:1, :] + norms_o[layer, 1:2, :]
+                nin[spot.member, here, :] = value.astype(BF16)
+            loop(TOK // CHUNK, first_norm)
+            give(1, spot.member).start()
+            give(2, spot.member).start()
+
+        @step(SHARE + layer)
+        def _():
+            gathered(1).wait_recv()
+            give(3, spot.mate(1)[1]).start()
+
+        def project(k):
+            def run():
+                member = spot.member
+                if k:
+                    member = spot.mate(k)[1]
+                    if k != 1:
+                        gathered(k).wait_recv()
+                group = dot(nin[member], w_qkv[:, cols(spot.c, GROUP)]).astype(BF16)
+                if (layer, k) == (1, 0):
+                    settle((0, "qkv"))
+                    settle((0, "nin_t"))
+                qkv[pl.ds(member, 1)] = group[None]
+                at = pl.multiple_of(member * TOK, TOK)
+                vt[:, pl.ds(at, TOK)] = group[:, 128:384].astype(F32).T.astype(BF16)
+                nin_t[:, pl.ds(at, TOK)] = nin[member].astype(F32).T.astype(BF16)
+                if k == 3:
+                    stash(layer, "qkv", qkv)
+                    stash(layer, "nin_t", nin_t)
+            return run
+        for k in range(4):
+            steps[PROJECT + 10 * layer + k] = project(k)
+
+        def returned(i):
+            return rcopy(
+                o_ref.at[layer, i], att.at[band(spot.member * 192, 192), :], os_.at[4 * layer + i], or_.at[4 * layer + spot.member], spot.device(i)
+            )
+
+        def attend(i):
+            def run():
+                attend_quarter(i, lens_v, qkv, vt, outs.at[layer, i], o_ref.at[layer], stats.at[layer], signed)
+
+                @pl.when(spot.member != i)
+                def _():
+                    returned(i).start()
+
+                @pl.when(spot.member == i)
+                def _():
+                    att[i * 192 : (i + 1) * 192, :] = o_ref[layer, i]
+                if i == 3:
+                    stash(layer, "out", outs.at[layer])
+                    stash(layer, "stats", stats.at[layer])
+            return run
+        for i in range(4):
+            steps[ATTEND + 10 * layer + i] = attend(i)
+
+        @step(OUTPUT + layer)
+        def _():
+            for i in range(4):
+                @pl.when(spot.member != i)
+                def _():
+                    ref = att.at[i * 192 : (i + 1) * 192, :]
+                    rcopy(ref, ref, os_.at[4 * layer + i], or_.at[4 * layer + i], spot.device(i)).wait_recv()
+            stash(layer, "att_t", att)
+            settle((0, "middle"))
+            middle[...] = stream[...] + dot_tn(att[...], w_out[...])
+            stash(layer, "middle", middle)
+
+            def second_norm(n):
+                here = band(n * CHUNK, CHUNK)
+                value = centred(middle[here, :]) * norms_o[layer, 2:3, :] + norms_o[layer, 3:4, :]
+                normed[here, :] = value.astype(BF16)
+            loop(TOK // CHUNK, second_norm)
+            settle((0, "nmid_t"))
+            nt_mid[...] = normed[...].astype(F32).T.astype(BF16)
+            stash(layer, "nmid_t", nt_mid)
+            settle((0, "pre"))
+            settle((0, "act_t"))
+
+        def up(h):
+            w_up = (w_up0, w_up1)[h]
+            tile = 512
+            count = w_up.shape[1] // tile
+
+            def run():
+                def part(n):
+                    value = dot(normed[...], w_up[:, cols(n, tile)])
+                    here = cols(h * count + n, tile)
+                    pre[:, here] = value
+                    active = jax.nn.gelu(value)
+                    act[:, here] = active.astype(BF16)
+                    act_t[pl.ds(pl.multiple_of((h * count + n) * tile, tile), tile), :] = active.T.astype(BF16)
+                loop(count, part)
+                if h:
+                    stash(layer, "pre", pre)
+                    stash(layer, "act_t", act_t)
+            return run
+
+        def down(h):
+            w_down = (w_down0, w_down1)[h]
+            width = w_down.shape[1]
+
+            def run():
+                settle((layer, "stream"))
+
+                def part(n):
+                    here = cols(n + h * (width // 128), 128)
+                    stream[:, here] = middle[:, here] + dot(act[...], w_down[:, cols(n, 128)])
+                if width % 384 == 0:
+                    here = slice(h * width, (h + 1) * width)
+                    stream[:, here] = middle[:, here] + dot(act[...], w_down[...])
+                else:
+                    loop(width // 128, part)
+                if h and layer == 0:
+                    stash(1, "stream", stream)
+            return run
+        for h in (0, 1):
+            steps[UP + 10 * layer + h] = up(h)
+            steps[DOWN + 10 * layer + h] = down(h)
+
+        def close():
+            for k in (1, 2):
+                give(k, spot.member).wait_send()
+            give(3, spot.mate(1)[1]).wait_send()
+            for i in range(4):
+                @pl.when(spot.member != i)
+                def _():
+                    returned(i).wait_send()
+        return close
+
+    closes = [layer_steps(layer) for layer in range(LAYERS)]
+
+    @step(RESULT)
+    def _():
+        def last(n):
+            here = band(n * CHUNK, CHUNK)
+            res[here, :] = (stream[here, :] * live_column(lens_v, spot, CHUNK, n * CHUNK)).astype(BF16)
+        loop(TOK // CHUNK, last)
+        swap(spot, res, result_o, ms.at[3], mr.at[3])
+
+    for name in FORWARD_ORDER:
+        steps.pop(name)()
+    assert not steps
+    for job in jobs:
+        job.drain()
+    for close in closes:
+        close()
+    for copy in kept.values():
+        copy.wait()
+    swap_wait(spot, cot, cot_o, ms.at[2], mr.at[2])
+    swap_wait(spot, res, result_o, ms.at[3], mr.at[3])
+
+
+def forward_call(tok, cot, lengths, w_qkv, w_out, w_up, w_down, gains, biases):
+    d, ff = tok.shape[1], w_up.shape[2]
+    shapes = [(d, 2 * GROUP), (d, d), (d, ff // 2), (d, ff // 2), (ff, d // 2), (ff, d // 2)] * LAYERS
+    zshapes = []
+    for n, (rows, width) in enumerate(shapes):
+        if n % JOBS < 4:
+            zshapes.append(pltpu.VMEM((ZN, 16, width * 3 // 2), BF16))
+        if n % JOBS == 0:
+            zshapes.append(pltpu.VMEM((2, 16, width * 3 // 2), BF16))
+    any_space = pl.BlockSpec(memory_space=pl.ANY)
+    vmem = pl.BlockSpec(memory_space=pltpu.VMEM)
+    stash = [jax.ShapeDtypeStruct(shape, kind) for shape, kind in stash_shapes(d, ff)]
+    dma = lambda n: pltpu.SemaphoreType.DMA((n,))
+    kept_shapes = [(rows, GROUP if n % JOBS == 0 else width) for n, (rows, width) in enumerate(shapes)]
+    outs = pl.pallas_call(
+        forward_kernel,
+        out_shape=[
+            jax.ShapeDtypeStruct((TOK, d), BF16),
+            jax.ShapeDtypeStruct((TOK, d), BF16),
+            jax.ShapeDtypeStruct((8, 128), jnp.int32),
+            jax.ShapeDtypeStruct((LAYERS, 8, d), F32),
+        ]
+        + [jax.ShapeDtypeStruct(shape, BF16) for shape in kept_shapes]
+        + stash
+        + stash,
+        in_specs=[any_space, any_space] + [vmem] * 7,
+        out_specs=[any_space, any_space, vmem, vmem] + [any_space] * (2 * JOBS + 20),
+        scratch_shapes=[pltpu.VMEM(shape, BF16) for shape in shapes]
+        + zshapes
+        + [
+            pltpu.VMEM((TOK, d), BF16),
+            pltpu.VMEM((8, 128), jnp.int32),
+            pltpu.VMEM((8, 128), jnp.int32),
+            pltpu.VMEM((TOK, d), F32),
+            pltpu.VMEM((4, TOK, d), BF16),
+            pltpu.VMEM((4, TOK, d), BF16),
+            pltpu.VMEM((4, TOK, GROUP), BF16),
+            pltpu.VMEM((WIDE, 4 * TOK), BF16),
+            pltpu.VMEM((LAYERS, 4, 192, TOK), F32),
+            pltpu.VMEM((LAYERS, 4, 8, TOK), F32),
+            pltpu.VMEM((LAYERS, 4, 192, TOK), BF16),
+            pltpu.VMEM((d, TOK), BF16),
+            pltpu.VMEM((d, TOK), BF16),
+            pltpu.VMEM((TOK, ff), F32),
+            pltpu.VMEM((TOK, ff), BF16),
+            pltpu.VMEM((ff, TOK), BF16),
+            pltpu.VMEM((d, 4 * TOK), BF16),
+            pltpu.VMEM((d, TOK), BF16),
+            pltpu.VMEM((TOK, d), BF16),
+            pltpu.VMEM((TOK, d), F32),
+            pltpu.VMEM((TOK, d), BF16),
+        ]
+        + [dma(2 * JOBS * Gather.SEMS), dma(2 * JOBS * Gather.SEMS), dma(2 * JOBS), dma(20), dma(8), dma(8), dma(8), dma(8), dma(4), dma(4)],
+        compiler_params=pltpu.CompilerParams(collective_id=0, has_side_effects=True, vmem_limit_bytes=62 * 2**20),
+    )(tok, cot, lengths, w_qkv, w_out, w_up, w_down, gains, biases)
+    at = 4 + 2 * JOBS
+    return outs[:4], outs[4:at], (outs[at : at + 10], outs[at + 10 : at + 20])
+
+
+class Reduce:
+    SEMS = 10
+
+    def __init__(self, send, bufs, out, ssem, rsem, base, paired=False):
+        self.send = send
+        self.got, self.half, self.near = bufs[:3]
+        self.zs, self.zr = bufs[3:5]
+        self.out = out
+        self.ssem, self.rsem, self.base = ssem, rsem, base
+        self.rows, self.width = self.got.shape[1], self.got.shape[2]
+        self.split, self.paired = self.zs.shape[1] == 16, paired
+        self.sent = []
+
+    def _copy(self, src, dst, at, device):
+        return rcopy(src, dst, self.ssem.at[self.base + at], self.rsem.at[self.base + at], device)
+
+    def _send(self, src, dst, at, device):
+        copy = self._copy(src, dst, at, device)
+        copy.start()
+        self.sent.append(copy)
+
+    def _got(self, core):
+        if self.paired:
+            return self.got.at[:, :, cols(core, self.width // 2)]
+        return self.got
+
+    def send_core(self):
+        r, z, rx, ry, rd, rc = places_of()
+        self._send(self.send, self._got(lax.rem(r, 2)), 0, (rc, z))
+
+    def wait_core(self):
+        r, z, rx, ry, rd, rc = places_of()
+        ref = self._got(lax.rem(rc, 2))
+        self._copy(ref, ref, 0, (rc, z)).wait_recv()
+
+    def _part(self, other, i):
+        part = self.rows // 2
+        return self.got.at[lax.div(other, 2), pl.ds(i * part, part)]
+
+    def send_first(self):
+        r, z, rx, ry, rd, rc = places_of()
+        part = self.rows // 2
+        self._send(self._part(rd, 0), self.half.at[0], 1, (ry, z))
+        self._send(self._part(rd, 1), self.half.at[1], 2, (rx, z))
+
+    def send_second(self):
+        r, z, rx, ry, rd, rc = places_of()
+        part = self.rows // 2
+        self._send(self._part(rx, 1), self.near.at[0, pl.ds(part, part)], 3, (rx, z))
+        self._send(self._part(ry, 0), self.near.at[1, pl.ds(0, part)], 4, (ry, z))
+
+    def send_near(self):
+        r, z, rx, ry, rd, rc = places_of()
+        part = self.rows // 2
+        for i, side, other in ((0, ry, rx), (1, rx, ry)):
+            self._copy(self.half.at[i], self.half.at[i], 1 + i, (side, z)).wait_recv()
+            block = self._part(other, i)
+            add_rows(block, self.half.at[i], part)
+            self._send(block, self.near.at[i, pl.ds(i * part, part)], 5 + i, (other, z))
+
+    def send_z(self):
+        r, z, rx, ry, rd, rc = places_of()
+        part = self.rows // 2
+        for at, i, h, side in ((3, 0, 1, rx), (4, 1, 0, ry), (5, 0, 0, rx), (6, 1, 1, ry)):
+            ref = self.near.at[i, pl.ds(h * part, part)]
+            self._copy(ref, ref, at, (side, z)).wait_recv()
+        own = self.got.at[lax.div(r, 2)]
+        near = self.near
+
+        def total(rows, here):
+            return own[rows, here].astype(F32) + near[0, rows, here].astype(F32) + near[1, rows, here].astype(F32)
+
+        if self.split:
+            half = self.width // 2
+            step = col_step(half)
+
+            def cut(i):
+                at = pl.ds(pl.multiple_of(self.width + i * step, 128), step)
+                sums = [
+                    total(slice(None), pl.ds(pl.multiple_of(side * half + i * step, 128), step)) for side in (0, 1)
+                ]
+                for piece in range(ZN):
+                    for side in (0, 1):
+                        here = pl.ds(pl.multiple_of(side * half + i * step, 128), step)
+                        self.zs[piece, :, here] = sums[side][24 * piece : 24 * piece + 16].astype(BF16)
+                    self.zs[piece, :, at] = jnp.concatenate(
+                        [sums[side][24 * piece + 16 : 24 * piece + 24] for side in (0, 1)], 0
+                    ).astype(BF16)
+            loop(half // step, cut)
+        else:
+            size = self.rows // ZN
+            for piece in range(ZN):
+                def cut_rows(i, piece=piece):
+                    self.zs[piece, band(i * 16, 16), :] = total(band(piece * size + i * 16, 16), slice(None)).astype(BF16)
+                loop(size // 16, cut_rows)
+        for k in (1, 2, 3):
+            self._send(self.zs.at[turn(z, k)], self.zr.at[k - 1], 6 + k, (r, turn(z, k)))
+
+    def finish(self):
+        r, z = places_of()[:2]
+        for k in (1, 2, 3):
+            ref = self.zr.at[k - 1]
+            self._copy(ref, ref, 6 + k, (r, turn(z, ZN - k))).wait_recv()
+        half, width = self.width // 2, self.width
+        if self.paired:
+            for place, value in (
+                (lax.rem(z, 2), self.zs[z].astype(F32) + self.zr[1].astype(F32)),
+                (lax.rem(z + 1, 2), self.zr[0].astype(F32) + self.zr[2].astype(F32)),
+            ):
+                for side in (0, 1):
+                    here = cols(place + 2 * side, GROUP)
+                    self.out[pl.ds(0, 16), here] = value[:, side * GROUP : (side + 1) * GROUP]
+                    self.out[pl.ds(16, 8), here] = value[8 * side : 8 * side + 8, width:]
+        elif self.split:
+            value = self.zs[z].astype(F32)
+            for k in range(3):
+                value = value + self.zr[k].astype(F32)
+            self.out[pl.ds(0, 16), :] = value[:, :width]
+            self.out[pl.ds(16, 8), pl.ds(0, half)] = value[:8, width:]
+            self.out[pl.ds(16, 8), pl.ds(half, half)] = value[8:, width:]
+        else:
+            def total(i):
+                here = band(i * 16, 16)
+                value = self.zs[z, here, :].astype(F32)
+                for k in range(3):
+                    value = value + self.zr[k, here, :].astype(F32)
+                self.out[here, :] = value
+            loop(self.out.shape[0] // 16, total)
+
+    def drain(self):
+        for copy in self.sent:
+            copy.wait_send()
+        self.sent = []
+
+
+def left_rows(left, c):
+    return jnp.concatenate([left[band((2 * b + c) * 96, 96), :] for b in range(4)], 0)
+
+
+def norm_back(source, upstream, gain, add, out, low, sums):
+    sums[...] = jnp.zeros_like(sums)
+
+    def step(n):
+        here = band(n * CHUNK, CHUNK)
+        value = source[here, :]
+        center = value - jnp.mean(value, -1, keepdims=True)
+        scale = lax.rsqrt(jnp.mean(center * center, -1, keepdims=True) + EPSILON)
+        normal = center * scale
+        up = upstream(here)
+        sums[0:8, :] += fold_rows(up * normal, jnp.add)
+        sums[8:16, :] += fold_rows(up, jnp.add)
+        up = up * gain
+        inner = up - jnp.mean(up, -1, keepdims=True) - normal * jnp.mean(up * normal, -1, keepdims=True)
+        total = add[here, :] + inner * scale
+        out[here, :] = total
+        low[here, :] = total.astype(BF16)
+    loop(TOK // CHUNK, step)
+    gain_grad = jnp.sum(sums[0:8, :], 0, keepdims=True)
+    bias_grad = jnp.sum(sums[8:16, :], 0, keepdims=True)
+    return gain_grad, bias_grad
+
+
+def gelu_slope(x):
+    root = 0.7978845608028654
+    square = x * x
+    bend = jnp.tanh(root * (x + 0.044715 * x * square))
+    return 0.5 * (1.0 + bend) + 0.5 * x * (1.0 - bend * bend) * root * (1.0 + 3 * 0.044715 * square)
+
+
+def attend_quarter_back(i, lens, qkv, kt, datt, out, stats, scratch, signed):
+    dk, dv, dq = scratch
+    places, start, live = starts_of(lens, i)
+    queries = qkv[i, :, 0:WIDE].astype(F32) * 0.125
+    mine = masked_heads(queries.T, 0)
+    mine_rows = jnp.concatenate(
+        [jnp.where(head_lanes((TOK, WIDE), h, 0), queries, 0.0).astype(BF16) for h in range(PARTS)], 0
+    )
+    upstream = datt[i].astype(F32)
+    grads_t = jnp.concatenate([jnp.zeros((HEAD, TOK), F32), upstream], 0)
+    out_t = masked_heads(grads_t, 1)
+    grads = grads_t.T
+    out_rows = jnp.concatenate(
+        [jnp.where(head_lanes((TOK, WIDE), h, 1), grads, 0.0).astype(BF16) for h in range(PARTS)], 0
+    )
+    product = upstream * out[i].astype(F32)
+    inner = [
+        jnp.sum(fold_rows(product[HEAD * h : HEAD * (h + 1)], jnp.add), 0, keepdims=True) for h in range(PARTS)
+    ]
+    top = [stats[i, h : h + 1, :] for h in range(PARTS)]
+    inverse = [stats[i, PARTS + h : PARTS + h + 1, :] for h in range(PARTS)]
+    dq[...] = jnp.zeros_like(dq)
+
+    def block(first, carry, diagonal):
+        keys = key_rows(qkv, first, 384)
+        values = key_rows(qkv, first, 128)
+        okay = masked_rows(first, KB, places, start, diagonal)
+        here = pl.ds(pl.multiple_of(first, KB), KB)
+        lows, slopes = [], []
+        scores = [dot(keys, mine[:, h * TOK : (h + 1) * TOK]) for h in range(PARTS)]
+        gains = [dot(values, out_t[:, h * TOK : (h + 1) * TOK]) for h in range(PARTS)]
+        for h in range(PARTS):
+            s, dp = scores[h], gains[h]
+            if signed:
+                size, back = magnitude_of(s)
+                unsigned = jnp.exp(jnp.where(okay, size - top[h], FAR)) * inverse[h]
+                bend = jnp.tanh(s)
+                lows.append((unsigned * bend).astype(BF16))
+                slope = unsigned * ((bend * dp - inner[h]) * (s * back) + dp * (1.0 - bend * bend))
+            else:
+                unsigned = jnp.exp(jnp.where(okay, s - top[h], FAR)) * inverse[h]
+                lows.append(unsigned.astype(BF16))
+                slope = unsigned * (dp - inner[h])
+            slopes.append(slope.astype(BF16))
+        value_terms = dot(jnp.concatenate(lows, 1), out_rows)
+        key_terms = dot(jnp.concatenate(slopes, 1), mine_rows)
+        query_terms = [dot(kt[HEAD * h : HEAD * (h + 1), here], slopes[h]) for h in range(PARTS)]
+        dv[here, :] += value_terms
+        dk[here, :] += key_terms
+        for h in range(PARTS):
+            dq[HEAD * h : HEAD * (h + 1), :] += query_terms[h]
+        return carry
+    over_blocks(i, block, 0)
+    query_grad = jnp.concatenate([dq[...] * 0.125, jnp.zeros((HEAD, TOK), F32)], 0).T
+    value_grad = dv[i * TOK : (i + 1) * TOK, :]
+    key_grad = dk[i * TOK : (i + 1) * TOK, :]
+    lanes = lax.broadcasted_iota(jnp.int32, (TOK, 128), 1)
+    return jnp.concatenate(
+        [
+            query_grad[:, :128],
+            jnp.where(lanes < HEAD, query_grad[:, 128:], value_grad[:, :128]),
+            value_grad[:, 128:],
+            key_grad,
+        ],
+        1,
+    ).astype(BF16)
+
+
+EDGE = 256
+
+
+def reduce_shapes(d, ff):
+    return [(96, 2 * GROUP), (96, d), (96, ff // 2), (96, ff // 2), (ff // 8, d // 2), (ff // 8, d // 2), (96, EDGE)]
+
+
+def backward_kernel(*refs):
+    refs = list(refs)
+    take = lambda n: [refs.pop(0) for _ in range(n)]
+    cot, lens, norms = take(3)
+    wholes = take(2 * JOBS)
+    stash = [take(10), take(10)]
+    (input_o,) = take(1)
+    grads_o = take(4)
+    (edge_o,) = take(1)
+    weights = take(JOBS)
+    homes = take(10)
+    stream, qkv, middle, nin_t, att_t, nmid_t, pre, act_t, att_out, stats = homes
+    w_qkv, w_out, w_up0, w_up1, w_down0, w_down1 = weights
+    cot_v, grad, low, branch, dpre, dmid, sums, edges, datt_s, datt_r, kt, dk, dv, dq, dqkv, pn_s, pn_r = take(17)
+    sends = take(JOBS + 1)
+    buffers = [take(5) for n in range(JOBS + 1)]
+    ssem, rsem, lsem, csem, as_, ar, ps, pr, ms, mr = take(10)
+    spot = Spot()
+    r, z, rx, ry, rd, rc = spot.r, spot.z, spot.rx, spot.ry, spot.rd, spot.rc
+    loads = {}
+
+    def load(layer, *names):
+        for name in names:
+            if name in STASH:
+                at = STASH.index(name)
+                src, dst = stash[layer][at], homes[at]
+            else:
+                src, dst = wholes[JOBS * layer + name], weights[name]
+                at = 10 + name
+            loads[(layer, name)] = Keep(src, dst, lsem.at[(10 + JOBS) * layer + at])
+
+    def ready(layer, *names):
+        for name in names:
+            loads[(layer, name)].wait()
+
+    def free(layer, *names):
+        if layer:
+            load(0, *names)
+
+    start = Keep(cot, cot_v, lsem.at[2 * (10 + JOBS)])
+    load(1, "act_t", 4, 5, "pre", "nmid_t", 2, 3, "middle", 1, "att_t", "qkv", "out", "stats", "nin_t", 0, "stream")
+    greet(spot.peers())
+    peers = comm_peers()
+    jobs = []
+    for layer in range(LAYERS):
+        qkv_g, out_g, up_g, down_g = [ref.at[layer] for ref in grads_o]
+        ff, d = up_g.shape[1] // 2, down_g.shape[1] // 2
+        outs = [qkv_g, out_g] + [up_g.at[:, h * ff : (h + 1) * ff] for h in (0, 1)] + [down_g.at[:, h * d : (h + 1) * d] for h in (0, 1)]
+        for n, out in enumerate(outs):
+            jobs.append(Reduce(sends[n], buffers[n], out, ssem, rsem, (JOBS * layer + n) * Reduce.SEMS, n == 0))
+    jobs.append(Reduce(sends[JOBS], buffers[JOBS], edge_o, ssem, rsem, 2 * JOBS * Reduce.SEMS))
+    steps = {}
+
+    def step(name):
+        def note(run):
+            steps[name] = run
+        return note
+
+    for at, job in enumerate(jobs):
+        def close(job=job, at=at):
+            job.finish()
+            if JOBS <= at < 2 * JOBS:
+                job.drain()
+                for peer in peers:
+                    pl.semaphore_signal(csem.at[at - JOBS], inc=1, device_id=peer, device_id_type=MESH)
+        steps.update({SECOND + at: job.send_second, NEAR + at: job.send_near, OVER_Z + at: job.send_z, CLOSE + at: close})
+
+    def credit(at):
+        if at < JOBS:
+            pl.semaphore_wait(csem.at[at], len(peers))
+
+    @step(BEGIN)
+    def _():
+        def begin(n):
+            here = band(n * CHUNK, CHUNK)
+            value = cot_v[here, :].astype(F32) * live_column(lens, spot, CHUNK, n * CHUNK)
+            grad[here, :] = value
+            low[here, :] = value.astype(BF16)
+        start.wait()
+        loop(TOK // CHUNK, begin)
+
+    def terms(job, left, tile, right, other):
+        c = lax.rem(rc, 2) if other else spot.c
+        rows = left_rows(left, c)
+        width = job.width // 2 if job.paired else job.width
+
+        def part(n):
+            here = cols(n, tile)
+            value = dot(rows, right(n))
+            for b in range(4):
+                piece = value[96 * b : 96 * b + 96]
+                if other:
+                    job.send[b, :, here] = piece.astype(BF16)
+                elif job.paired:
+                    job.got[b, :, cols(spot.c, GROUP)] = piece.astype(BF16)
+                else:
+                    job.got[b, :, here] = (job.got[b, :, here].astype(F32) + piece).astype(BF16)
+        if width == tile:
+            part(0)
+        else:
+            loop(width // tile, part)
+
+    def down_terms(job, right, other):
+        c = lax.rem(rc, 2) if other else spot.c
+
+        def part(b):
+            value = dot(act_t[band((2 * b + c) * 384, 384), :], right())
+            if other:
+                job.send[b] = value.astype(BF16)
+            else:
+                job.got[b] = (job.got[b].astype(F32) + value).astype(BF16)
+        loop(4, part)
+
+    late = {}
+
+    def layer_steps(layer):
+        base = JOBS * layer
+        signed = layer == 0
+        gains = norms.at[layer]
+
+        def both(at, needs, compute, after=()):
+            job = jobs[at]
+
+            def theirs():
+                ready(layer, *needs)
+                credit(at)
+                compute(job, True)
+                job.send_core()
+
+            def ours():
+                job.wait_core()
+                compute(job, False)
+                free(layer, *after)
+                job.send_first()
+            steps[THEIRS + at] = theirs
+            steps[OURS + at] = ours
+
+        for h in (0, 1):
+            half = w_down0.shape[1]
+            both(
+                base + 4 + h,
+                ["act_t"],
+                lambda job, other, h=h: down_terms(job, lambda: low[:, h * half : (h + 1) * half], other),
+                ["act_t"] if h else [],
+            )
+            ff = w_up0.shape[1]
+            both(
+                base + 2 + h,
+                ["nmid_t"],
+                lambda job, other, h=h: terms(job, nmid_t, 512, lambda n: dpre[:, cols(n + h * (ff // 512), 512)], other),
+                ["nmid_t"] if h else [],
+            )
+        both(base + 1, ["att_t"], lambda job, other: terms(job, att_t, 256, lambda n: branch[:, cols(n, 256)], other), ["att_t"])
+        both(
+            base,
+            ["nin_t"],
+            lambda job, other: terms(job, nin_t, GROUP, lambda n: dqkv[...].reshape(4 * TOK, GROUP), other),
+            ["nin_t"],
+        )
+
+        def slope(h):
+            def run():
+                ready(layer, 4, 5, "pre")
+                half = w_down0.shape[1]
+
+                def part(n):
+                    here = cols(n, 512)
+                    rows = pl.ds(pl.multiple_of(n * 512, 512), 512)
+                    value = dot_nt(low[:, :half], w_down0[rows, :]) + dot_nt(low[:, half:], w_down1[rows, :])
+                    dpre[:, here] = (gelu_slope(pre[:, here]) * value).astype(BF16)
+                lax.fori_loop(3 * h, 3 * h + 3, lambda n, carry: (part(n), carry)[1], 0)
+                if h:
+                    free(layer, 4, 5, "pre")
+            return run
+        steps[SLOPE + 10 * layer + 0] = slope(0)
+        steps[SLOPE + 10 * layer + 1] = slope(1)
+
+        def through(h):
+            w_up = (w_up0, w_up1)[h]
+
+            def run():
+                ready(layer, 2 + h)
+                if h == 0:
+                    dmid[...] = jnp.zeros_like(dmid)
+                count = w_up.shape[1] // 512
+
+                def part(n):
+                    dmid[...] += dot_nt(dpre[:, cols(n + h * count, 512)], w_up[:, cols(n, 512)])
+                loop(count, part)
+                free(layer, 2 + h)
+            return run
+        steps[THROUGH + 10 * layer + 0] = through(0)
+        steps[THROUGH + 10 * layer + 1] = through(1)
+
+        @step(NORM_BACK + layer)
+        def _():
+            ready(layer, "middle")
+            late[layer] = norm_back(middle, lambda here: dmid[here, :], gains[2:3, :], grad, grad, branch, sums)
+            free(layer, "middle")
+
+        def asked(g, which=layer):
+            return rcopy(
+                datt_s.at[g], datt_r.at[spot.member], as_.at[4 * which + g], ar.at[4 * which + spot.member], spot.device(g)
+            )
+
+        @step(ASK + layer)
+        def _():
+            ready(layer, 1)
+            for g in range(4):
+                value = dot_nt(w_out[192 * g : 192 * g + 192, :], branch[...]).astype(BF16)
+                if layer == 0:
+                    @pl.when(spot.member != g)
+                    def _():
+                        asked(g, 1).wait_send()
+                datt_s[g] = value
+
+                @pl.when(spot.member != g)
+                def _():
+                    asked(g).start()
+
+                @pl.when(spot.member == g)
+                def _():
+                    datt_r[g] = datt_s[g]
+            free(layer, 1)
+
+        @step(KEYS + layer)
+        def _():
+            ready(layer, "qkv", "out", "stats")
+
+            def turn_keys(j):
+                kt[:, cols(j, TOK)] = qkv[j, :, 384:640].astype(F32).T.astype(BF16)
+            loop(4, turn_keys)
+            dk[...] = jnp.zeros_like(dk)
+            dv[...] = jnp.zeros_like(dv)
+
+        @step(ASKED + layer)
+        def _():
+            for g in range(4):
+                @pl.when(spot.member != g)
+                def _():
+                    rcopy(datt_r.at[g], datt_r.at[g], as_.at[4 * layer + g], ar.at[4 * layer + g], spot.device(g)).wait_recv()
+
+        def back(i):
+            def run():
+                dqkv[i] = attend_quarter_back(i, lens, qkv, kt, datt_r, att_out, stats, (dk, dv, dq), signed)
+                if i == 0:
+                    free(layer, "qkv", "out", "stats")
+            return run
+        for i in range(4):
+            steps[ATTEND_BACK + 10 * layer + i] = back(i)
+
+        def given(which, k):
+            mate = spot.mate(1 if k == 1 else 2)[0]
+            src = pn_s.at[k - 1]
+            return rcopy(src, pn_r.at[k - 1], ps.at[4 * which + k], pr.at[4 * which + k], mate)
+
+        def partial(member):
+            return dot_nt(dqkv[member], w_qkv[...])
+
+        @step(PARTIAL + 10 * layer + 2)
+        def _():
+            ready(layer, 0)
+            if layer == 0:
+                given(1, 2).wait_send()
+            pn_s[1] = partial(spot.mate(3)[1]).astype(BF16)
+            given(layer, 2).start()
+
+        @step(PARTIAL + 10 * layer + 3)
+        def _():
+            if layer == 0:
+                given(1, 3).wait_send()
+            pn_s[2] = partial(spot.mate(2)[1]).astype(BF16)
+            given(layer, 3).start()
+
+        @step(PARTIAL + 10 * layer + 1)
+        def _():
+            value = partial(spot.mate(1)[1])
+            if layer == 0:
+                given(1, 1).wait_send()
+            given(layer, 2).wait_recv()
+            pn_s[0] = (value + pn_r[1].astype(F32)).astype(BF16)
+            given(layer, 1).start()
+            dmid[...] = partial(spot.member)
+            free(layer, 0)
+
+        @step(FIRST_BACK + layer)
+        def _():
+            ready(layer, "stream")
+            given(layer, 3).wait_recv()
+            given(layer, 1).wait_recv()
+
+            def upstream(here):
+                return dmid[here, :] + pn_r[2, here, :].astype(F32) + pn_r[0, here, :].astype(F32)
+            early = norm_back(stream, upstream, gains[0:1, :], grad, grad, low, sums)
+            free(layer, "stream")
+            for n, value in enumerate(early + late[layer]):
+                edges[4 * layer + n : 4 * layer + n + 1, :] = value
+
+    for layer in (1, 0):
+        layer_steps(layer)
+
+    @step(SWAP_BACK)
+    def _():
+        swap(spot, low, input_o, ms.at[0], mr.at[0])
+
+    last = 2 * JOBS
+
+    def edge_rows(c):
+        turned = jnp.concatenate([edges[...], jnp.zeros((128 - 8, edges.shape[1]), F32)], 0).T
+        return [
+            jnp.where(c == 0, turned[192 * b : 192 * b + 96], turned[192 * b + 96 : 192 * b + 192]) for b in range(4)
+        ]
+
+    @step(THEIRS + last)
+    def _():
+        job = jobs[last]
+        for b, rows in enumerate(edge_rows(lax.rem(rc, 2))):
+            job.send[b, :, 0:128] = rows.astype(BF16)
+            job.send[b, :, 128:256] = jnp.zeros((96, 128), BF16)
+        job.send_core()
+
+    @step(OURS + last)
+    def _():
+        job = jobs[last]
+        job.wait_core()
+        for b, rows in enumerate(edge_rows(spot.c)):
+            job.got[b, :, 0:128] = (job.got[b, :, 0:128].astype(F32) + rows).astype(BF16)
+        job.send_first()
+
+    for name in BACKWARD_ORDER:
+        steps.pop(name)()
+    assert not steps
+    for job in jobs:
+        job.drain()
+    for g in range(4):
+        @pl.when(spot.member != g)
+        def _():
+            rcopy(
+                datt_s.at[g], datt_r.at[spot.member], as_.at[g], ar.at[spot.member], spot.device(g)
+            ).wait_send()
+    for k in (1, 2, 3):
+        mate = spot.mate(1 if k == 1 else 2)[0]
+        rcopy(pn_s.at[k - 1], pn_r.at[k - 1], ps.at[k], pr.at[k], mate).wait_send()
+    swap_wait(spot, low, input_o, ms.at[0], mr.at[0])
+
+
+def backward_call(cot, lens, norms, wholes, stash):
+    d, ff = cot.shape[1], stash[0][6].shape[1]
+    any_space = pl.BlockSpec(memory_space=pl.ANY)
+    vmem = pl.BlockSpec(memory_space=pltpu.VMEM)
+    dma = lambda n: pltpu.SemaphoreType.DMA((n,))
+    shapes = reduce_shapes(d, ff)
+    sends, buffers = [], []
+    for n, (rows, width) in enumerate(shapes):
+        sends.append(pltpu.VMEM((4, rows, width // 2 if n == 0 else width), BF16))
+        cut = (rows // 4, width) if n in (4, 5) else (16, width * 3 // 2)
+        buffers += [
+            pltpu.VMEM((4, rows, width), BF16),
+            pltpu.VMEM((2, rows // 2, width), BF16),
+            pltpu.VMEM((2, rows, width), BF16),
+        ]
+        buffers += [pltpu.VMEM((4,) + cut, BF16), pltpu.VMEM((3,) + cut, BF16)]
+    count = 2 * JOBS + 1
+    outs = pl.pallas_call(
+        backward_kernel,
+        out_shape=[
+            jax.ShapeDtypeStruct((TOK, d), BF16),
+            jax.ShapeDtypeStruct((LAYERS, 24, 4 * GROUP), F32),
+            jax.ShapeDtypeStruct((LAYERS, 24, d), F32),
+            jax.ShapeDtypeStruct((LAYERS, 24, ff), F32),
+            jax.ShapeDtypeStruct((LAYERS, ff // 32, d), F32),
+            jax.ShapeDtypeStruct((24, EDGE), F32),
+        ],
+        in_specs=[any_space, vmem, vmem] + [any_space] * (2 * JOBS + 20),
+        out_specs=[any_space] + [vmem] * 5,
+        scratch_shapes=[pltpu.VMEM(whole.shape, BF16) for whole in wholes[:JOBS]]
+        + [pltpu.VMEM(shape, kind) for shape, kind in stash_shapes(d, ff)]
+        + [
+            pltpu.VMEM((TOK, d), BF16),
+            pltpu.VMEM((TOK, d), F32),
+            pltpu.VMEM((TOK, d), BF16),
+            pltpu.VMEM((TOK, d), BF16),
+            pltpu.VMEM((TOK, ff), BF16),
+            pltpu.VMEM((TOK, d), F32),
+            pltpu.VMEM((16, d), F32),
+            pltpu.VMEM((8, d), F32),
+            pltpu.VMEM((4, 192, TOK), BF16),
+            pltpu.VMEM((4, 192, TOK), BF16),
+            pltpu.VMEM((WIDE, 4 * TOK), BF16),
+            pltpu.VMEM((4 * TOK, WIDE), F32),
+            pltpu.VMEM((4 * TOK, WIDE), F32),
+            pltpu.VMEM((192, TOK), F32),
+            pltpu.VMEM((4, TOK, GROUP), BF16),
+            pltpu.VMEM((3, TOK, d), BF16),
+            pltpu.VMEM((3, TOK, d), BF16),
+        ]
+        + sends
+        + buffers
+        + [
+            dma(count * Reduce.SEMS),
+            dma(count * Reduce.SEMS),
+            dma(2 * (10 + JOBS) + 1),
+            pltpu.SemaphoreType.REGULAR((JOBS,)),
+            dma(8),
+            dma(8),
+            dma(8),
+            dma(8),
+            dma(1),
+            dma(1),
+        ],
+        compiler_params=pltpu.CompilerParams(collective_id=1, has_side_effects=True, vmem_limit_bytes=62 * 2**20),
+    )(cot, lens, norms, *wholes, *stash[0], *stash[1])
+    return outs
+
+
+def finish_kernel(result, grad_in, qkv, out, up, down, edge, result_o, input_o, qkv_o, out_o, up_o, down_o, gains_o, biases_o, mids_o):
+    result_o[0] = result[...]
+    input_o[0] = grad_in[...].astype(F32)
+    out_o[...] = out[...]
+    up_o[...] = up[...]
+    down_o[...] = down[...]
+    own = edge.shape[0]
+    turned = jnp.concatenate([edge[:, 0:128], jnp.zeros((128 - own, 128), F32)], 0).T
+    for layer in range(LAYERS):
+        parts = [
+            qkv[layer, :, GROUP * g + at : GROUP * g + at + 192] for at in (0, 384, 192) for g in range(4)
+        ]
+        qkv_o[layer] = jnp.concatenate(parts, 1)
+        for n, ref in enumerate((gains_o.at[layer, 0:1], biases_o.at[layer : layer + 1], gains_o.at[layer, 1:2], mids_o.at[layer : layer + 1])):
+            ref[...] = turned[4 * layer + n : 4 * layer + n + 1, 0:own]
+
+
+def backward_part(result, cot, lens, norms, wholes, stash):
+    grads = backward_call(cot, lens, norms, wholes, stash)
+    d, own = cot.shape[1], grads[1].shape[1]
+    shape = lambda *sizes: jax.ShapeDtypeStruct(sizes, F32)
+    return pl.pallas_call(
+        finish_kernel,
+        out_shape=[
+            jax.ShapeDtypeStruct((1, TOK, d), BF16),
+            shape(1, TOK, d),
+            shape(LAYERS, own, 3 * d),
+            shape(*grads[2].shape),
+            shape(*grads[3].shape),
+            shape(*grads[4].shape),
+            shape(LAYERS, 2, own),
+            shape(LAYERS, own),
+            shape(LAYERS, own),
+        ],
+        in_specs=[pl.BlockSpec(memory_space=pltpu.VMEM)] * 7,
+        out_specs=[pl.BlockSpec(memory_space=pltpu.VMEM)] * 9,
+        compiler_params=pltpu.CompilerParams(vmem_limit_bytes=62 * 2**20),
+    )(result, *grads)
+
+
+def local_fast(tokens, lengths, w_qkv, w_out, w_up, w_down, gains, biases, cotangent):
+    (result, cot, lens, norms), wholes, stash = forward_call(
+        tokens[0], cotangent[0], lengths, w_qkv, w_out, w_up, w_down, gains, biases
+    )
+    return tuple(backward_part(result, cot, lens, norms, wholes, stash))
+
+
 def solution(mesh):
     in_specs = (
         P("rows", "kv", None),
@@ -338,4 +1817,5 @@
         P(None, ("rows", "kv")),
         P(None, ("rows", "kv")),
     )
-    return jax.shard_map(local, mesh=mesh, in_specs=in_specs, out_specs=out_specs, check_vma=False)
+    fast = dict(mesh.shape) == {"rows": 8, "kv": 4}
+    return jax.shard_map(local_fast if fast else local_generic, mesh=mesh, in_specs=in_specs, out_specs=out_specs, check_vma=False)

time: 1890 us -> 290 us (0.15)
  waiting for transfers between devices: 1150 us -> 0 us
  blocking collectives: 327 us -> 0 us
  Pallas kernels: 0 us -> 284 us
  matrix products: 218 us -> 0 us
  local copies, waits for them, and re-layouts: 88.5 us -> 0 us
  other arithmetic: 44.2 us -> 0 us
  starting transfers between devices: 30 us -> 0 us
    all_gather x18 -> x0, waiting for transfers between devices: 595 us -> none  [the longest x2 164 us: reduce_grads(): lax.all_gather(rights[2], 'kv', axis=0, tiled=True)]
    reduce_scatter x10 -> x0, waiting for transfers between devices: 337 us -> none  [the longest x2 79 us: reduce_grads(): lax.psum_scatter(partial_sums[3].astype(jnp.bfloat16), 'rows', scatter_di...]
    pallas_call x0 -> x3, Pallas kernels: none -> 284 us  [the longest x1 149 us: backward_call(): pl.pallas_call(backward_kernel, out_shape=[jax.ShapeDtypeStruct((TOK, d),...]
    all_gather x4 -> x0, blocking collectives: 282 us -> none  [the longest x2 148 us: local(): lax.all_gather(gains[number], ('rows', 'kv'), axis=1, tiled=True)]
    all_to_all x8 -> x0, waiting for transfers between devices: 215 us -> none  [the longest x2 121 us: reduce_grads(): lax.all_to_all(lefts[3], 'kv', split_axis=2, concat_axis=0, tiled=True)]
    dot_general x34 -> x0, matrix products: 156 us -> none  [the longest x8 32.8 us: reduce_grads(): jnp.einsum('ti,to->io', left_block, whole[number], preferred_element_type...]
    sub x3 -> x0, matrix products: 62.3 us -> none  [the longest x1 27.4 us: score_grads(): tanh_s * weight_grad - inner_sum]
    unnamed x1 -> x0, blocking collectives: 44.5 us -> none
  transfers between devices with their start and end apart: 36 -> 0, of which waited for: 26 -> 0; matrix products, arithmetic and copies ran while one was open for 15% -> 0% of each run, Pallas kernels for 0% -> 0%
where the time goes in v3:
time: 290 us; the launch traced here: 284 us
  Pallas kernels  284 us (98%)
    pallas_call x1, Pallas kernels, backward_call(): pl.pallas_call(backward_kernel, out_shape=[jax.ShapeDtypeStruct((TOK, d),...  149 us
    pallas_call x1, Pallas kernels, forward_call(): pl.pallas_call(forward_kernel, out_shape=[jax.ShapeDtypeStruct((TOK, d),...  131 us

profile of v3, /device:TPU:0, one launch (start us, length us, event | category | flops | bytes accessed | tf_op | source)
XLA Modules:
  0.0 284.4 jit_solution(8134835568342627379)
XLA Ops:
  0.6 130.8 %shard_map.160 = (bf16[256,768]{1,0:T(8,128)(2,1)}, bf16[256,768]{1,0:T(8,128)(2,1)}, s32[8,128]{1,0:T(8,128)}, f32[2,8,768]{2,1,0:T(8,128)}, bf16[768,640]{1,0:...) custom-call(bf16[256,768]{1,0:T(8,128)(2,1)} %bitcast.2, ...), custom_call_target="tpu_custom_call" | custom-call | tf_op jit(solution)/shard_map/pallas_call | solution.py:1046
  131.5 149.3 %shard_map.161 = (bf16[256,768]{1,0:T(8,128)(2,1)}, f32[2,24,2560]{2,1,0:T(8,128)}, f32[2,24,768]{2,1,0:T(8,128)}, f32[2,24,3072]{2,1,0:T(8,128)}, f32[2,96,768]{2,1,0:T(8,128)}, /*index=5*/f32[24,256]{1,0:T(8,128)}) custom-call(bf16[256,768]{1,0:T(8,128)(2,1)} %get-tuple-element.52.refs_0_, s32[8,128]{1,0:T(8,128)} %get-tuple-element.53.refs_1_, ...), custom_call_target="tpu_custom_call" | custom-call | tf_op jit(solution)/shard_map/pallas_call | solution.py:1698
  280.8 3.4 %shard_map.162 = (bf16[1,256,768]{2,1,0:T(8,128)(2,1)}, f32[1,256,768]{2,1,0:T(8,128)}, f32[2,24,2304]{2,1,0:T(8,128)}, f32[2,24,768]{2,1,0:T(8,128)}, f32[2,24,...) custom-call(bf16[256,768]{1,0:T(8,128)(2,1)} %get-tuple-element.51.result, ...), custom_call_target="tpu_custom_call" | custom-call | tf_op jit(solution)/shard_map/pallas_call | solution.py:1771

commit v4 on v3

--- a/solution.py
+++ b/solution.py
@@ -403,23 +403,25 @@
 ATTEND_BACK = 1200
 PARTIAL = 1300
 FIRST_BACK = 1400
+RELAY = 1600
 BEGIN = 1500
 SWAP_BACK = 1510
+RESULT_BACK = 1520
 
 FORWARD_ORDER = [
-    0, 100, 1, 2, 200, 500, 3, 300, 101, 400, 102, 201, 301, 4, 401, 103, 202, 520, 600, 5, 800, 802, 104,
-    302, 203, 402, 105, 6, 303, 204, 700, 403, 7, 801, 803, 106, 8, 9, 900, 901, 304, 205, 107, 902, 903, 404,
-    206, 305, 207, 10, 1000, 108, 405, 1100, 306, 307, 109, 11, 1101, 406, 407, 1200, 1201, 110, 601, 810,
-    812, 208, 111, 701, 811, 209, 813, 910, 911, 912, 308, 913, 210, 408, 510, 309, 211, 1001, 1110, 409, 310,
+    2, 1, 101, 0, 102, 201, 500, 3, 100, 301, 401, 4, 202, 200, 103, 300, 400, 5, 520, 600, 800, 104, 802,
+    203, 6, 105, 303, 403, 8, 9, 106, 302, 700, 801, 7, 204, 803, 205, 900, 402, 901, 902, 206, 903, 304, 107,
+    11, 10, 306, 305, 108, 109, 404, 406, 1000, 405, 1100, 1101, 1200, 1201, 601, 207, 810, 110, 812, 208,
+    209, 307, 111, 407, 701, 811, 813, 910, 911, 912, 913, 510, 308, 309, 210, 211, 1001, 409, 408, 1110, 310,
     1111, 311, 410, 1210, 411, 1211, 530,
 ]
 BACKWARD_ORDER = [
-    1500, 410, 610, 710, 408, 611, 510, 10, 411, 711, 801, 1001, 901, 407, 508, 409, 511, 110, 11, 1101, 1213,
-    1212, 108, 1211, 1210, 111, 509, 210, 9, 507, 1312, 406, 8, 1313, 1311, 506, 6, 310, 211, 1401, 109, 404,
-    600, 208, 106, 311, 504, 209, 4, 700, 601, 405, 107, 701, 308, 104, 800, 900, 402, 505, 5, 309, 7, 1000,
-    204, 206, 403, 1100, 502, 207, 2, 1203, 105, 1202, 102, 306, 307, 205, 503, 3, 401, 1201, 202, 1200, 501,
-    1, 1302, 400, 1303, 305, 103, 1301, 304, 101, 500, 302, 0, 203, 201, 100, 200, 301, 1400, 1510, 412, 303,
-    512, 12, 112, 212, 300, 312,
+    1500, 410, 610, 408, 710, 611, 711, 801, 901, 510, 10, 409, 1001, 407, 508, 8, 411, 1520, 1101, 1213,
+    1313, 1212, 1312, 110, 509, 1613, 1211, 1612, 1311, 108, 1210, 1310, 1611, 1610, 406, 9, 511, 210, 109,
+    11, 208, 506, 1401, 600, 507, 601, 700, 701, 800, 900, 1000, 111, 310, 308, 404, 6, 209, 107, 106, 402,
+    1100, 1203, 211, 1303, 7, 502, 2, 1202, 1603, 1302, 206, 207, 504, 311, 1602, 1201, 102, 405, 1301, 1200,
+    104, 1300, 4, 307, 202, 1601, 306, 309, 1600, 403, 505, 5, 204, 503, 105, 1400, 1510, 401, 400, 103, 3,
+    412, 304, 205, 501, 500, 0, 512, 112, 203, 101, 1, 305, 302, 100, 201, 303, 200, 301, 12, 212, 300, 312,
 ]
 
 
@@ -726,6 +728,14 @@
     o_ref[i] = acc[...].astype(BF16)
 
 
+def gelu_both(x):
+    root = 0.7978845608028654
+    square = x * x
+    bend = jnp.tanh(root * (x + 0.044715 * x * square))
+    half = 0.5 * (1.0 + bend)
+    return x * half, half + 0.5 * x * (1.0 - bend * bend) * root * (1.0 + 3 * 0.044715 * square)
+
+
 class Keep:
     def __init__(self, src, dst, sem):
         self.copy = pltpu.make_async_copy(src, dst, sem)
@@ -964,8 +974,7 @@
                 def part(n):
                     value = dot(normed[...], w_up[:, cols(n, tile)])
                     here = cols(h * count + n, tile)
-                    pre[:, here] = value
-                    active = jax.nn.gelu(value)
+                    active, pre[:, here] = gelu_both(value)
                     act[:, here] = active.astype(BF16)
                     act_t[pl.ds(pl.multiple_of((h * count + n) * tile, tile), tile), :] = active.T.astype(BF16)
                 loop(count, part)
@@ -1014,7 +1023,7 @@
             here = band(n * CHUNK, CHUNK)
             res[here, :] = (stream[here, :] * live_column(lens_v, spot, CHUNK, n * CHUNK)).astype(BF16)
         loop(TOK // CHUNK, last)
-        swap(spot, res, result_o, ms.at[3], mr.at[3])
+        keep("result", res, result_o, ms.at[3])
 
     for name in FORWARD_ORDER:
         steps.pop(name)()
@@ -1026,7 +1035,6 @@
     for copy in kept.values():
         copy.wait()
     swap_wait(spot, cot, cot_o, ms.at[2], mr.at[2])
-    swap_wait(spot, res, result_o, ms.at[3], mr.at[3])
 
 
 def forward_call(tok, cot, lengths, w_qkv, w_out, w_up, w_down, gains, biases):
@@ -1250,13 +1258,6 @@
     return gain_grad, bias_grad
 
 
-def gelu_slope(x):
-    root = 0.7978845608028654
-    square = x * x
-    bend = jnp.tanh(root * (x + 0.044715 * x * square))
-    return 0.5 * (1.0 + bend) + 0.5 * x * (1.0 - bend * bend) * root * (1.0 + 3 * 0.044715 * square)
-
-
 def attend_quarter_back(i, lens, qkv, kt, datt, out, stats, scratch, signed):
     dk, dv, dq = scratch
     places, start, live = starts_of(lens, i)
@@ -1335,17 +1336,17 @@
 def backward_kernel(*refs):
     refs = list(refs)
     take = lambda n: [refs.pop(0) for _ in range(n)]
-    cot, lens, norms = take(3)
+    cot, result, lens, norms = take(4)
     wholes = take(2 * JOBS)
     stash = [take(10), take(10)]
-    (input_o,) = take(1)
+    result_o, input_o = take(2)
     grads_o = take(4)
     (edge_o,) = take(1)
     weights = take(JOBS)
     homes = take(10)
     stream, qkv, middle, nin_t, att_t, nmid_t, pre, act_t, att_out, stats = homes
     w_qkv, w_out, w_up0, w_up1, w_down0, w_down1 = weights
-    cot_v, grad, low, branch, dpre, dmid, sums, edges, datt_s, datt_r, kt, dk, dv, dq, dqkv, pn_s, pn_r = take(17)
+    cot_v, grad, low, branch, dpre, dmid, sums, edges, datt_s, datt_r, kt, dk, dv, dq, dqkv, pn_s, pn_r, held = take(18)
     sends = take(JOBS + 1)
     buffers = [take(5) for n in range(JOBS + 1)]
     ssem, rsem, lsem, csem, as_, ar, ps, pr, ms, mr = take(10)
@@ -1501,7 +1502,7 @@
                     here = cols(n, 512)
                     rows = pl.ds(pl.multiple_of(n * 512, 512), 512)
                     value = dot_nt(low[:, :half], w_down0[rows, :]) + dot_nt(low[:, half:], w_down1[rows, :])
-                    dpre[:, here] = (gelu_slope(pre[:, here]) * value).astype(BF16)
+                    dpre[:, here] = (pre[:, here] * value).astype(BF16)
                 lax.fori_loop(3 * h, 3 * h + 3, lambda n, carry: (part(n), carry)[1], 0)
                 if h:
                     free(layer, 4, 5, "pre")
@@ -1583,45 +1584,57 @@
         for i in range(4):
             steps[ATTEND_BACK + 10 * layer + i] = back(i)
 
-        def given(which, k):
+        def given(which, k, i):
             mate = spot.mate(1 if k == 1 else 2)[0]
-            src = pn_s.at[k - 1]
-            return rcopy(src, pn_r.at[k - 1], ps.at[4 * which + k], pr.at[4 * which + k], mate)
-
-        def partial(member):
-            return dot_nt(dqkv[member], w_qkv[...])
-
-        @step(PARTIAL + 10 * layer + 2)
-        def _():
-            ready(layer, 0)
-            if layer == 0:
-                given(1, 2).wait_send()
-            pn_s[1] = partial(spot.mate(3)[1]).astype(BF16)
-            given(layer, 2).start()
-
-        @step(PARTIAL + 10 * layer + 3)
-        def _():
-            if layer == 0:
-                given(1, 3).wait_send()
-            pn_s[2] = partial(spot.mate(2)[1]).astype(BF16)
-            given(layer, 3).start()
-
-        @step(PARTIAL + 10 * layer + 1)
-        def _():
-            value = partial(spot.mate(1)[1])
-            if layer == 0:
-                given(1, 1).wait_send()
-            given(layer, 2).wait_recv()
-            pn_s[0] = (value + pn_r[1].astype(F32)).astype(BF16)
-            given(layer, 1).start()
-            dmid[...] = partial(spot.member)
-            free(layer, 0)
+            return rcopy(pn_s.at[i], pn_r.at[k - 1], ps.at[4 * which + k], pr.at[4 * which + k], mate)
+
+        def role(i, k):
+            return spot.mate(k)[1] == i if k else spot.member == i
+
+        def partial(i):
+            def run():
+                if i == 3:
+                    ready(layer, 0)
+                value = dot_nt(dqkv[i], w_qkv[...])
+
+                @pl.when(role(i, 0))
+                def _():
+                    dmid[...] = value
+
+                @pl.when(role(i, 1))
+                def _():
+                    held[...] = value
+                for k in (2, 3):
+                    @pl.when(role(i, k))
+                    def _(k=k):
+                        at = 3 if k == 2 else 2
+                        if layer == 0:
+                            given(1, at, i).wait_send()
+                        pn_s[i] = value.astype(BF16)
+                        given(layer, at, i).start()
+                if i == 0:
+                    free(layer, 0)
+            return run
+
+        def relay(i):
+            def run():
+                @pl.when(role(i, 1))
+                def _():
+                    if layer == 0:
+                        given(1, 1, i).wait_send()
+                    given(layer, 2, i).wait_recv()
+                    pn_s[i] = (held[...] + pn_r[1].astype(F32)).astype(BF16)
+                    given(layer, 1, i).start()
+            return run
+        for i in range(4):
+            steps[PARTIAL + 10 * layer + i] = partial(i)
+            steps[RELAY + 10 * layer + i] = relay(i)
 
         @step(FIRST_BACK + layer)
         def _():
             ready(layer, "stream")
-            given(layer, 3).wait_recv()
-            given(layer, 1).wait_recv()
+            given(layer, 3, 0).wait_recv()
+            given(layer, 1, 0).wait_recv()
 
             def upstream(here):
                 return dmid[here, :] + pn_r[2, here, :].astype(F32) + pn_r[0, here, :].astype(F32)
@@ -1632,6 +1645,10 @@
 
     for layer in (1, 0):
         layer_steps(layer)
+
+    @step(RESULT_BACK)
+    def _():
+        swap(spot, result, result_o, ms.at[1], mr.at[1])
 
     @step(SWAP_BACK)
     def _():
@@ -1674,11 +1691,12 @@
             ).wait_send()
     for k in (1, 2, 3):
         mate = spot.mate(1 if k == 1 else 2)[0]
-        rcopy(pn_s.at[k - 1], pn_r.at[k - 1], ps.at[k], pr.at[k], mate).wait_send()
+        rcopy(pn_s.at[0], pn_r.at[k - 1], ps.at[k], pr.at[k], mate).wait_send()
     swap_wait(spot, low, input_o, ms.at[0], mr.at[0])
-
-
-def backward_call(cot, lens, norms, wholes, stash):
+    swap_wait(spot, result, result_o, ms.at[1], mr.at[1])
+
+
+def backward_call(cot, result, lens, norms, wholes, stash):
     d, ff = cot.shape[1], stash[0][6].shape[1]
     any_space = pl.BlockSpec(memory_space=pl.ANY)
     vmem = pl.BlockSpec(memory_space=pltpu.VMEM)
@@ -1699,14 +1717,15 @@
         backward_kernel,
         out_shape=[
             jax.ShapeDtypeStruct((TOK, d), BF16),
+            jax.ShapeDtypeStruct((TOK, d), BF16),
             jax.ShapeDtypeStruct((LAYERS, 24, 4 * GROUP), F32),
             jax.ShapeDtypeStruct((LAYERS, 24, d), F32),
             jax.ShapeDtypeStruct((LAYERS, 24, ff), F32),
             jax.ShapeDtypeStruct((LAYERS, ff // 32, d), F32),
             jax.ShapeDtypeStruct((24, EDGE), F32),
         ],
-        in_specs=[any_space, vmem, vmem] + [any_space] * (2 * JOBS + 20),
-        out_specs=[any_space] + [vmem] * 5,
+        in_specs=[any_space, any_space, vmem, vmem] + [any_space] * (2 * JOBS + 20),
+        out_specs=[any_space, any_space] + [vmem] * 5,
         scratch_shapes=[pltpu.VMEM(whole.shape, BF16) for whole in wholes[:JOBS]]
         + [pltpu.VMEM(shape, kind) for shape, kind in stash_shapes(d, ff)]
         + [
@@ -1725,8 +1744,9 @@
             pltpu.VMEM((4 * TOK, WIDE), F32),
             pltpu.VMEM((192, TOK), F32),
             pltpu.VMEM((4, TOK, GROUP), BF16),
+            pltpu.VMEM((4, TOK, d), BF16),
             pltpu.VMEM((3, TOK, d), BF16),
-            pltpu.VMEM((3, TOK, d), BF16),
+            pltpu.VMEM((TOK, d), F32),
         ]
         + sends
         + buffers
@@ -1739,11 +1759,11 @@
             dma(8),
             dma(8),
             dma(8),
-            dma(1),
-            dma(1),
+            dma(2),
+            dma(2),
         ],
         compiler_params=pltpu.CompilerParams(collective_id=1, has_side_effects=True, vmem_limit_bytes=62 * 2**20),
-    )(cot, lens, norms, *wholes, *stash[0], *stash[1])
+    )(cot, result, lens, norms, *wholes, *stash[0], *stash[1])
     return outs
 
 
@@ -1765,8 +1785,8 @@
 
 
 def backward_part(result, cot, lens, norms, wholes, stash):
-    grads = backward_call(cot, lens, norms, wholes, stash)
-    d, own = cot.shape[1], grads[1].shape[1]
+    grads = backward_call(cot, result, lens, norms, wholes, stash)
+    d, own = cot.shape[1], grads[2].shape[1]
     shape = lambda *sizes: jax.ShapeDtypeStruct(sizes, F32)
     return pl.pallas_call(
         finish_kernel,
@@ -1774,9 +1794,9 @@
             jax.ShapeDtypeStruct((1, TOK, d), BF16),
             shape(1, TOK, d),
             shape(LAYERS, own, 3 * d),
-            shape(*grads[2].shape),
             shape(*grads[3].shape),
             shape(*grads[4].shape),
+            shape(*grads[5].shape),
             shape(LAYERS, 2, own),
             shape(LAYERS, own),
             shape(LAYERS, own),
@@ -1784,7 +1804,7 @@
         in_specs=[pl.BlockSpec(memory_space=pltpu.VMEM)] * 7,
         out_specs=[pl.BlockSpec(memory_space=pltpu.VMEM)] * 9,
         compiler_params=pltpu.CompilerParams(vmem_limit_bytes=62 * 2**20),
-    )(result, *grads)
+    )(*grads)
 
 
 def local_fast(tokens, lengths, w_qkv, w_out, w_up, w_down, gains, biases, cotangent):

time: 290 us -> 281 us (0.969)
  the two profiles are of different devices: /device:TPU:0 before, /device:TPU:2 now
where the time goes in v4:
time: 281 us; the launch traced here: 275 us
  Pallas kernels  274 us (98%)
    pallas_call x1, Pallas kernels, backward_call(): pl.pallas_call(backward_kernel, out_shape=[jax.ShapeDtypeStruct((TOK, d),...  141 us
    pallas_call x1, Pallas kernels, forward_call(): pl.pallas_call(forward_kernel, out_shape=[jax.ShapeDtypeStruct((TOK, d),...  129 us

profile of v4, /device:TPU:2, one launch (start us, length us, event | category | flops | bytes accessed | tf_op | source)
XLA Modules:
  0.0 275.2 jit_solution(399331581851453617)
XLA Ops:
  0.6 129.2 %shard_map.160 = (bf16[256,768]{1,0:T(8,128)(2,1)}, bf16[256,768]{1,0:T(8,128)(2,1)}, s32[8,128]{1,0:T(8,128)}, f32[2,8,768]{2,1,0:T(8,128)}, bf16[768,640]{1,0:...) custom-call(bf16[256,768]{1,0:T(8,128)(2,1)} %bitcast.2, ...), custom_call_target="tpu_custom_call" | custom-call | tf_op jit(solution)/shard_map/pallas_call | solution.py:1054
  129.9 141.4 %shard_map.161 = (bf16[256,768]{1,0:T(8,128)(2,1)}, bf16[256,768]{1,0:T(8,128)(2,1)}, f32[2,24,2560]{2,1,0:T(8,128)}, f32[2,24,768]{2,1,0:T(8,128)}, f32[2,24,30...) custom-call(bf16[256,768]{1,0:T(8,128)(2,1)} %get-tuple-element.52.refs_0_, ...), custom_call_target="tpu_custom_call" | custom-call | tf_op jit(solution)/shard_map/pallas_call | solution.py:1716
  271.3 3.4 %shard_map.162 = (bf16[1,256,768]{2,1,0:T(8,128)(2,1)}, f32[1,256,768]{2,1,0:T(8,128)}, f32[2,24,2304]{2,1,0:T(8,128)}, f32[2,24,768]{2,1,0:T(8,128)}, f32[2,24,...) custom-call(bf16[256,768]{1,0:T(8,128)(2,1)} %get-tuple-element.88.result, ...), custom_call_target="tpu_custom_call" | custom-call | tf_op jit(solution)/shard_map/pallas_call | solution.py:1791
